TPU v7x, 32 devices: a whole 2x2x4 slice. The times are simulated.
32 devices in a mesh: ctx: 16 (over z, x, core), mp: 2 (over y).
Axes of the slice: x: 2, y: 2, z: 4, core: 2. Of those that a mesh axis runs over, the one named last changes fastest.
Arguments:
- hidden: bfloat16 [32768, 512], P('ctx', 'mp'), may hold values from -6 to 6
- w_x: bfloat16 [512, 1024], P(None, 'mp'), may hold values from -0.25 to 0.25
- w_z: bfloat16 [512, 1024], P(None, 'mp'), may hold values from -0.25 to 0.25
- w_bc: bfloat16 [512, 256], replicated, may hold values from -0.25 to 0.25
- w_dt: bfloat16 [512, 16], P(None, 'mp'), may hold values from -0.25 to 0.25
- conv_x: float32 [4, 1024], P(None, 'mp'), may hold values from -3 to 3
- conv_bc: float32 [4, 256], replicated, may hold values from -3 to 3
- dt_bias: float32 [16], P('mp'), may hold values from -5 to -3
- decay_rate: float32 [16], P('mp'), may hold values from 2e-06 to 2
- skip_gain: float32 [16], P('mp'), may hold values from 0.1 to 1.9
- norm_gain: float32 [1024], P('mp'), may hold values from 0.1 to 1.9
- w_out: bfloat16 [1024, 512], P('mp'), may hold values from -0.1875 to 0.1875
- piece_lengths: int32 [4], replicated, may hold values from 1 to 16384, 32768 in all
Outputs:
- layer_out: bfloat16 [32768, 512], P('ctx', 'mp')
Inputs may be any that keep to these rules, and one draw needn't show every extreme that they name: `piece_lengths`: the piece lengths add up to 32768, and the longest is exactly 16384.
All inputs are finite; a program needn't handle non-finite values.
Results may differ from a plain program's by a relative error of at most 0.015.
Values may be sent and summed in bfloat16 or wider, within the bound.
A program may use at most 128 MiB of HBM per device.

v0:
```python
import functools
import jax
import jax.numpy as jnp
from jax import lax
from jax.experimental import pallas as pl
from jax.experimental.pallas import tpu as pltpu
from jax.sharding import PartitionSpec as P

HEAD_DIM = 64
NSTATE = 128
SUB = 128
CHUNK = 256
EPSILON = 1e-05
LOG2E = 1.4426950408889634
F32 = jnp.float32
BF16 = jnp.bfloat16
BIG = 1 << 30
VMEM_LIMIT = 48 * 1024 * 1024

NT = (((1,), (1,)), ((), ()))
TN = (((0,), (0,)), ((), ()))


def piece_start(sm, pieces, pos):
    out = jnp.zeros_like(pos)
    for k in range(pieces):
        bound = sm[k]
        out = jnp.maximum(out, jnp.where(pos >= bound, bound, 0))
    return out


def piece_end(sm, pieces, pos):
    out = jnp.full_like(pos, BIG)
    for k in range(pieces):
        bound = sm[k]
        out = jnp.minimum(out, jnp.where(pos < bound, bound, BIG))
    return out


def silu(value):
    half = 0.5 * value
    return half * jnp.tanh(half) + half


def expand_rows(weights, expander2):
    high = weights.astype(BF16)
    low = (weights - high.astype(F32)).astype(BF16)
    both = jnp.concatenate([high, low], axis=0)
    return lax.dot_general(both, expander2, TN, preferred_element_type=F32)


def project_kernel(nc, mp, inner, pieces, *refs):
    sm = refs[0]
    hf, hr, halo = refs[1 : 1 + mp], refs[1 + mp : 1 + 2 * mp], refs[1 + 2 * mp : 1 + 3 * mp]
    (wf, wr, wdt, cw, head_par, e1, e2) = refs[1 + 3 * mp : 8 + 3 * mp]
    outs = refs[8 + 3 * mp : 22 + 3 * mp]
    buf_f, buf_r, st_f, st_r, dec_f, dec_r = refs[22 + 3 * mp :]
    step = pl.program_id(0)
    base = sm[pieces]
    mixing = inner + 2 * NSTATE
    width = wf.shape[0] // mp

    def dots(blocks, weight, columns):
        total = None
        for b in range(mp):
            part = jnp.dot(
                blocks[b], weight[b * width : (b + 1) * width, columns], preferred_element_type=F32
            )
            total = part if total is None else total + part
        return total

    @pl.when(step == 0)
    def _():
        low = dots([h[0:16, :] for h in halo], wf, slice(0, mixing))
        high = dots([h[16:32, :] for h in halo], wr, slice(0, mixing))
        buf_f[0:8, :] = low[8:16].astype(BF16).astype(F32)
        buf_r[CHUNK : CHUNK + 8, :] = high[0:8].astype(BF16).astype(F32)
        st_f[...] = jnp.zeros_like(st_f)
        st_r[...] = jnp.zeros_like(st_r)
        dec_f[...] = jnp.ones_like(dec_f)
        dec_r[...] = jnp.ones_like(dec_r)

    @pl.when(step > 0)
    def _():
        buf_f[0:8, :] = buf_f[CHUNK : CHUNK + 8, :]
        buf_r[CHUNK : CHUNK + 8, :] = buf_r[0:8, :]

    rows = lax.broadcasted_iota(jnp.int32, (SUB, SUB), 0)
    lanes = lax.broadcasted_iota(jnp.int32, (SUB, SUB), 1)
    for forward in (True, False):
        blocks = [h[...] for h in (hf if forward else hr)]
        weight = wf if forward else wr
        buf = buf_f if forward else buf_r
        state, decay = (st_f, dec_f) if forward else (st_r, dec_r)
        x_out, bc_out, z_out, aux_out, before_out = outs[:5] if forward else outs[5:10]
        chunk = step if forward else nc - 1 - step
        first = base + chunk * CHUNK
        own = 8 if forward else 0
        buf[own : own + CHUNK, :] = (
            dots(blocks, weight, slice(0, mixing)).astype(BF16).astype(F32)
        )
        z_out[...] = dots(blocks, weight, slice(mixing, mixing + inner)).astype(BF16)

        raw = None
        lo = 0 if forward else 8
        for b in range(mp):
            part = lax.dot_general(
                wdt[lo : lo + 8, b * width : (b + 1) * width],
                blocks[b],
                NT,
                preferred_element_type=F32,
            )
            raw = part if raw is None else raw + part
        raw = raw.astype(BF16).astype(F32)
        raw = jnp.concatenate([raw[:, :SUB], raw[:, SUB:]], axis=0)
        par = head_par[...]
        shifted = raw + par[0:16]
        step_dt = jnp.maximum(shifted, 0.0) + jnp.log1p(jnp.exp(-jnp.abs(shifted)))
        log_decay = step_dt * par[16:32]
        tri = jnp.where(rows <= lanes if forward else rows >= lanes, 1.0, 0.0).astype(F32)
        cum = jnp.dot(
            log_decay, tri, precision=lax.Precision.HIGHEST, preferred_element_type=F32
        )
        total = cum[:, SUB - 1 : SUB] if forward else cum[:, 0:1]
        block_first = first + SUB * (lax.broadcasted_iota(jnp.int32, (16, SUB), 0) // 8)
        position = block_first + lax.broadcasted_iota(jnp.int32, (16, SUB), 1)
        start = piece_start(sm, pieces, position)
        end = piece_end(sm, pieces, position)
        block_last = block_first + SUB - 1
        if forward:
            to_end_ok = end > block_last
            from_start_ok = start < block_first
            whole_ok = piece_start(sm, pieces, block_last) < block_first
        else:
            to_end_ok = start <= block_first
            from_start_ok = end > block_last + 1
            whole_ok = piece_end(sm, pieces, block_first) > block_last + 1
        to_end = jnp.where(to_end_ok, jnp.exp2(total - cum) * step_dt, 0.0)
        from_start = jnp.where(from_start_ok, jnp.exp2(cum), 0.0)
        whole = jnp.where(whole_ok, jnp.exp2(jnp.broadcast_to(total, cum.shape)), 0.0)
        aux_out[0, 0:16, :] = cum
        aux_out[0, 16:32, :] = cum - jnp.log2(step_dt)
        aux_out[0, 32:48, :] = from_start
        aux_out[0, 48:64, :] = whole

        for b in (0, 1) if forward else (1, 0):
            at = first + b * SUB + rows
            if forward:
                room = at - piece_start(sm, pieces, at)
            else:
                room = piece_end(sm, pieces, at) - 1 - at
            same = [None] + [room >= j for j in (1, 2, 3)]
            r0 = own + b * SUB
            out_rows = slice(b * SUB, (b + 1) * SUB)
            for g in range(mixing // 128):
                cols = slice(g * 128, (g + 1) * 128)
                acc = buf[r0 : r0 + SUB, cols] * cw[3:4, cols]
                for j in (1, 2, 3):
                    off = r0 - j if forward else r0 + j
                    tap = buf[off : off + SUB, cols] * cw[3 - j : 4 - j, cols]
                    acc = acc + jnp.where(same[j], tap, 0.0)
                value = silu(acc).astype(BF16)
                if g * 128 < inner:
                    x_out[out_rows, cols] = value
                else:
                    bc_out[out_rows, slice(g * 128 - inner, g * 128 - inner + 128)] = value
            hb = slice(b * 8, b * 8 + 8)
            weights = expand_rows(to_end[hb], e2[...])
            scaled = (x_out[out_rows, :].astype(F32) * weights).astype(BF16)
            added = lax.dot_general(
                bc_out[out_rows, 0:NSTATE], scaled, TN, preferred_element_type=F32
            )
            grow = jnp.sum(whole[hb, 0:1] * e1[...], axis=0, keepdims=True)
            held = state[...]
            before_out[b] = held.astype(BF16)
            state[...] = held * grow + added
            decay[...] = decay[...] * grow

    outs[10][...] = st_f[...]
    outs[11][...] = st_r[...]
    outs[12][...] = dec_f[...]
    outs[13][...] = dec_r[...]


def intra_kernel(forward, heads, inner, pieces, sm, x_ref, bc_ref, aux_ref, skip_ref, y_ref):
    first = sm[pieces] + pl.program_id(0) * CHUNK
    rows = lax.broadcasted_iota(jnp.int32, (SUB, SUB), 0)
    lanes = lax.broadcasted_iota(jnp.int32, (SUB, SUB), 1)
    left = lanes < HEAD_DIM
    for b in (0, 1):
        at = slice(b * SUB, (b + 1) * SUB)
        begin = first + b * SUB
        if forward:
            mask = (lanes <= rows) & (begin + lanes >= piece_start(sm, pieces, begin + rows))
        else:
            mask = (lanes >= rows) & (begin + lanes < piece_end(sm, pieces, begin + rows))
        scores = lax.dot_general(
            bc_ref[at, NSTATE:], bc_ref[at, 0:NSTATE], NT, preferred_element_type=F32
        )
        cum_t = aux_ref[0, b * 8 : b * 8 + 8, :].T
        cum_s = aux_ref[0, 16 + b * 8 : 16 + b * 8 + 8, :]
        for pair in range(heads // 2):
            cols = slice(pair * 128, (pair + 1) * 128)
            xp = x_ref[at, cols]
            parts = []
            for h in (2 * pair, 2 * pair + 1):
                gap = jnp.where(mask, cum_t[:, h : h + 1] - cum_s[h : h + 1, :], -1e30)
                parts.append((jnp.exp2(gap) * scores).astype(BF16))
            xf = xp.astype(F32)
            stacked = jnp.concatenate(
                [
                    jnp.where(left, xf, 0.0).astype(BF16),
                    jnp.where(left, 0.0, xf).astype(BF16),
                ],
                axis=0,
            )
            mixed = jnp.dot(
                jnp.concatenate(parts, axis=1), stacked, preferred_element_type=F32
            )
            y_ref[at, cols] = mixed + skip_ref[0:1, cols] * xf


def finish_kernel(nc, inner, *refs):
    ins, par = refs[0:12], refs[12:15]
    outs = refs[15:19]
    grown = refs[19:21]
    gain_ref, e1, e2 = par
    step = pl.program_id(0)

    @pl.when(step == 0)
    def _():
        grown[0][...] = jnp.ones_like(grown[0])
        grown[1][...] = jnp.ones_like(grown[1])

    ones = jnp.ones((8, inner), BF16)
    for stream in (0, 1):
        y_ref, z_ref, bc_ref, aux_ref, before_ref, into_ref = ins[stream * 6 : stream * 6 + 6]
        g_out, ss_out = outs[stream * 2 : stream * 2 + 2]
        into = into_ref[...]
        for b in (0, 1) if stream == 0 else (1, 0):
            at = slice(b * SUB, (b + 1) * SUB)
            grow = grown[stream][...]
            state = (before_ref[b].astype(F32) + grow * into).astype(BF16)
            factor = expand_rows(aux_ref[0, 32 + b * 8 : 40 + b * 8, :], e2[...])
            inter = jnp.dot(bc_ref[at, NSTATE:], state, preferred_element_type=F32)
            mixed = y_ref[at, :] + inter * factor
            gated = mixed * silu(z_ref[at, :].astype(F32))
            ss_out[:, at] = lax.dot_general(
                ones, (gated * gated).astype(BF16), NT, preferred_element_type=F32
            )
            g_out[at, :] = (gated * gain_ref[0:1, :]).astype(BF16)
            whole = aux_ref[0, 48 + b * 8 : 56 + b * 8, 0:1]
            grown[stream][...] = grow * jnp.sum(whole * e1[...], axis=0, keepdims=True)


def output_kernel(mp, total_width, ss_ref, gf_ref, gr_ref, wf_ref, wr_ref, *outs):
    factor = lax.rsqrt(ss_ref[...] * (1.0 / total_width) + EPSILON).T
    width = wf_ref.shape[1] // mp
    for k in range(mp):
        cols = slice(k * width, (k + 1) * width)
        part = factor[:, 0:1] * jnp.dot(gf_ref[...], wf_ref[:, cols], preferred_element_type=F32)
        part = part + factor[:, 4:5] * jnp.dot(
            gr_ref[...], wr_ref[:, cols], preferred_element_type=F32
        )
        outs[k][...] = part.astype(outs[k].dtype)


def shift(value, axis, by, wrap):
    count = lax.axis_size(axis)
    if wrap:
        pairs = [(i, (i + by) % count) for i in range(count)]
    else:
        pairs = [(i, i + by) for i in range(count) if 0 <= i + by < count]
    return lax.ppermute(value, axis, pairs)


def pack_state(state, decay):
    high = decay[0:1].astype(BF16)
    low = (decay[0:1] - high.astype(F32)).astype(BF16)
    tail = jnp.concatenate([high, low, jnp.zeros((14, decay.shape[1]), BF16)], axis=0)
    return jnp.concatenate([state.astype(BF16), tail], axis=0)


def unpack_state(packed):
    decay = packed[NSTATE : NSTATE + 1].astype(F32) + packed[NSTATE + 1 : NSTATE + 2].astype(F32)
    return packed[:NSTATE].astype(F32), decay


def prefix_states(states, decays, axis):
    count = lax.axis_size(axis)
    signs = (1, -1)
    cur = [(s, d[0:1]) for s, d in zip(states, decays)]
    window = 1
    while 4 * window < count - 1:
        packed = [pack_state(*c) for c in cur]
        got = [
            [shift(p, axis, sign * window * k, False) for k in (1, 2, 3)]
            for p, sign in zip(packed, signs)
        ]
        new = []
        for (s, d), parts in zip(cur, got):
            for part in parts:
                more, fade = unpack_state(part)
                s, d = s + d * more, d * fade
            new.append((s, d))
        cur = new
        window *= 4
    reach = -(-(count - 1) // window)
    packed = [pack_state(*c) for c in cur]
    got = [
        [shift(p, axis, sign * (1 + window * k), False) for k in range(reach)]
        for p, sign in zip(packed, signs)
    ]
    result = []
    for parts in got:
        s, d = unpack_state(parts[0])
        for part in parts[1:]:
            more, fade = unpack_state(part)
            s, d = s + d * more, d * fade
        result.append(s)
    return result


def cost(flops, size, trans=0):
    return pl.CostEstimate(flops=flops, bytes_accessed=size, transcendentals=trans)


def shards(
    hidden, w_x, w_z, w_bc, w_dt, conv_x, conv_bc, dt_bias, decay_rate, skip_gain, norm_gain,
    w_out, piece_lengths,
):
    mp = lax.axis_size("mp")
    me = lax.axis_index("mp")
    rows, width = hidden.shape
    model = width * mp
    heads = dt_bias.shape[0]
    inner = heads * HEAD_DIM
    mixing = inner + 2 * NSTATE
    pieces = piece_lengths.shape[0]
    nc = rows // CHUNK
    params = pltpu.CompilerParams(vmem_limit_bytes=VMEM_LIMIT)

    blocks = [hidden] + [shift(hidden, "mp", k, True) for k in range(1, mp)]
    halo_own = jnp.concatenate(
        [shift(hidden[rows - 16 :], "ctx", 1, False), shift(hidden[:16], "ctx", -1, False)], axis=0
    )
    halos = [halo_own] + [shift(halo_own, "mp", k, True) for k in range(1, mp)]

    place = jnp.arange(model, dtype=jnp.int32)
    came = lax.rem(me - place // width + mp, mp) * width + lax.rem(place, width)
    columns = jnp.arange(model, dtype=jnp.int32)[None, :]
    pick_f = (came[:, None] == columns).astype(BF16)
    pick_r = (model - 1 - came[:, None] == columns).astype(BF16)
    w_in = jnp.concatenate([w_x, w_bc, w_z], axis=1)
    w_f = jnp.dot(pick_f, w_in, preferred_element_type=F32).astype(BF16)
    w_r = jnp.dot(pick_r, w_in, preferred_element_type=F32).astype(BF16)
    pad = 8 - heads
    dt_pad = jnp.pad(w_dt, ((0, 0), (0, pad)))
    dt_t = lax.dot_general(
        dt_pad,
        jnp.concatenate([pick_f, pick_r], axis=0),
        (((0,), (1,)), ((), ())),
        preferred_element_type=F32,
    ).astype(BF16)
    w_dt2 = jnp.concatenate([dt_t[:, :model], dt_t[:, model:]], axis=0)
    goes = lax.rem(me + place // width, mp) * width + lax.rem(place, width)
    out_f = jnp.dot(
        w_out, (columns.T == goes[None, :]).astype(BF16), preferred_element_type=F32
    ).astype(BF16)
    out_r = jnp.dot(
        w_out, (columns.T == model - 1 - goes[None, :]).astype(BF16), preferred_element_type=F32
    ).astype(BF16)

    bounds = jnp.cumsum(piece_lengths).astype(jnp.int32)
    sm = jnp.concatenate([bounds, (lax.axis_index("ctx") * rows).astype(jnp.int32)[None]])
    conv_w = jnp.pad(jnp.concatenate([conv_x, conv_bc], axis=1), ((0, 4), (0, 0)))
    bias = jnp.pad(dt_bias, (0, pad))
    rate = jnp.pad(-LOG2E * decay_rate, (0, pad))
    head_par = jnp.broadcast_to(
        jnp.concatenate([bias, bias, rate, rate])[:, None], (32, SUB)
    ).astype(F32)
    owner = jnp.arange(inner, dtype=jnp.int32)[None, :] // HEAD_DIM
    e1 = (jnp.arange(8, dtype=jnp.int32)[:, None] == owner).astype(F32)
    e2 = jnp.concatenate([e1, e1], axis=0).astype(BF16)
    skip8 = jnp.broadcast_to(jnp.repeat(skip_gain, HEAD_DIM)[None, :], (8, inner))
    gain8 = jnp.broadcast_to(norm_gain[None, :], (8, inner))

    smem = pl.BlockSpec(memory_space=pltpu.SMEM)

    def whole(shape):
        return pl.BlockSpec(shape, lambda i: (0,) * len(shape))

    def up(cols):
        return pl.BlockSpec((CHUNK, cols), lambda i: (i, 0))

    def down(cols):
        return pl.BlockSpec((CHUNK, cols), lambda i: (nc - 1 - i, 0))

    aux_up = pl.BlockSpec((1, 64, SUB), lambda i: (i, 0, 0))
    aux_down = pl.BlockSpec((1, 64, SUB), lambda i: (nc - 1 - i, 0, 0))
    st_up = pl.BlockSpec((2, NSTATE, inner), lambda i: (i, 0, 0))
    st_down = pl.BlockSpec((2, NSTATE, inner), lambda i: (nc - 1 - i, 0, 0))

    def sds(shape, dtype):
        return jax.ShapeDtypeStruct(shape, dtype)

    stream_shapes = [
        sds((rows, inner), BF16),
        sds((rows, 2 * NSTATE), BF16),
        sds((rows, inner), BF16),
        sds((nc, 64, SUB), F32),
        sds((2 * nc, NSTATE, inner), BF16),
    ]
    made = pl.pallas_call(
        functools.partial(project_kernel, nc, mp, inner, pieces),
        grid=(nc,),
        in_specs=[smem]
        + [up(width)] * mp
        + [down(width)] * mp
        + [whole((32, width))] * mp
        + [
            whole((model, mixing + inner)),
            whole((model, mixing + inner)),
            whole((16, model)),
            whole((8, mixing)),
            whole((32, SUB)),
            whole((8, inner)),
            whole((16, inner)),
        ],
        out_specs=[up(inner), up(2 * NSTATE), up(inner), aux_up, st_up]
        + [down(inner), down(2 * NSTATE), down(inner), aux_down, st_down]
        + [whole((NSTATE, inner))] * 2
        + [whole((8, inner))] * 2,
        out_shape=stream_shapes
        + stream_shapes
        + [sds((NSTATE, inner), F32)] * 2
        + [sds((8, inner), F32)] * 2,
        scratch_shapes=[
            pltpu.VMEM((CHUNK + 8, mixing), F32),
            pltpu.VMEM((CHUNK + 8, mixing), F32),
            pltpu.VMEM((NSTATE, inner), F32),
            pltpu.VMEM((NSTATE, inner), F32),
            pltpu.VMEM((8, inner), F32),
            pltpu.VMEM((8, inner), F32),
        ],
        compiler_params=params,
        cost_estimate=cost(4 * rows * model * (mixing + inner), 20 << 20),
        name="project",
    )(sm, *blocks, *blocks, *halos, w_f, w_r, w_dt2, conv_w, head_par, e1, e2)
    fwd, rev = made[0:5], made[5:10]

    into = prefix_states(made[10:12], made[12:14], "ctx")

    mixed = []
    for forward, parts in ((True, fwd), (False, rev)):
        mixed.append(
            pl.pallas_call(
                functools.partial(intra_kernel, forward, heads, inner, pieces),
                grid=(nc,),
                in_specs=[smem, up(inner), up(2 * NSTATE), aux_up, whole((8, inner))],
                out_specs=up(inner),
                out_shape=sds((rows, inner), F32),
                compiler_params=params,
                cost_estimate=cost(20 * rows * SUB * inner, 8 << 20, rows * SUB * heads),
                name="intra",
            )(sm, parts[0], parts[1], parts[3], skip8)
        )

    finished = pl.pallas_call(
        functools.partial(finish_kernel, nc, inner),
        grid=(nc,),
        in_specs=[up(inner), up(inner), up(2 * NSTATE), aux_up, st_up, whole((NSTATE, inner))]
        + [down(inner), down(inner), down(2 * NSTATE), aux_down, st_down, whole((NSTATE, inner))]
        + [whole((8, inner)), whole((8, inner)), whole((16, inner))],
        out_specs=[
            up(inner),
            pl.BlockSpec((8, CHUNK), lambda i: (0, i)),
            down(inner),
            pl.BlockSpec((8, CHUNK), lambda i: (0, nc - 1 - i)),
        ],
        out_shape=[sds((rows, inner), BF16), sds((8, rows), F32)] * 2,
        scratch_shapes=[pltpu.VMEM((1, inner), F32)] * 2,
        compiler_params=params,
        cost_estimate=cost(4 * rows * NSTATE * inner, 24 << 20),
        name="finish",
    )(
        mixed[0], fwd[2], fwd[1], fwd[3], fwd[4], into[0],
        mixed[1], rev[2], rev[1], rev[3], rev[4], into[1],
        gain8, e1, e2,
    )
    upper = jnp.arange(8, dtype=jnp.int32)[:, None] < 4
    squares = jnp.where(upper, finished[1], finished[3])
    total = squares
    for k in range(1, mp):
        total = total + shift(squares, "mp", k, True)

    parts = pl.pallas_call(
        functools.partial(output_kernel, mp, inner * mp),
        grid=(nc,),
        in_specs=[
            pl.BlockSpec((8, CHUNK), lambda i: (0, i)),
            up(inner),
            up(inner),
            whole((inner, model)),
            whole((inner, model)),
        ],
        out_specs=[up(width)] * mp,
        out_shape=[sds((rows, width), F32)] + [sds((rows, width), BF16)] * (mp - 1),
        compiler_params=params,
        cost_estimate=cost(4 * rows * inner * model, 8 << 20),
        name="output",
    )(total, finished[0], finished[2], out_f, out_r)
    result = parts[0]
    for k in range(1, mp):
        result = result + shift(parts[k], "mp", k, True).astype(F32)
    return result.astype(BF16)


def solution(mesh):
    return jax.shard_map(
        shards,
        mesh=mesh,
        in_specs=(
            P("ctx", "mp"), P(None, "mp"), P(None, "mp"), P(), P(None, "mp"), P(None, "mp"), P(),
            P("mp"), P("mp"), P("mp"), P("mp"), P("mp", None), P(),
        ),
        out_specs=P("ctx", "mp"),
        check_vma=False,
    )
```

profile of v0, /device:TPU:0, one launch (start us, length us, event | category | flops | bytes accessed | tf_op | source)
XLA Modules:
  0.0 169.8 jit_solution(9710895284057927690)
XLA Ops:
  0.0 3.0 %collective-permute-start = (bf16[2048,256]{1,0:T(8,128)(2,1)}, bf16[2048,256]{1,0:T(8,128)(2,1)S(1)}, u32[]{:S(2)}, u32[]{:S(2)}) collective-permute-start(bf16[2048,256]{1,0:T(8,128)(2,1)} %refs_3_.1), channel_id=1, source_target_pairs={{0,1},{1,0},{2,3},{3,2},{4,5},{5,4},{6,7},{7,6},{8,9},{9,8},{10,11... | collective-permute-start | bytes 3145736 | tf_op jit(solution)/shard_map/ppermute | solution.py:274
  3.0 0.7 fusion.58
  3.7 1.4 collective-permute-start.1
  5.2 1.3 collective-permute-start.2
  6.5 0.2 iota_compare_fusion.2
  6.7 0.2 iota_compare_fusion.3
  7.0 0.0 copy-start.12
  7.0 0.0 copy-start.7
  7.0 0.0 copy-start.6
  7.0 1.1 fusion.4
  8.1 0.0 copy-start.8
  8.2 0.0 copy-start.9
  8.2 0.9 constant_dynamic-update-slice_fusion.4
  9.1 0.7 constant_dynamic-update-slice_fusion.3
  9.8 0.9 constant_dynamic-update-slice_fusion.2
  10.7 0.5 fusion.1.wf_ref
  11.3 0.2 reduce-window.9
  11.4 3.3 %convolution_convert_fusion.refs_8_ = bf16[512,1280]{1,0:T(8,128)(2,1)} fusion(bf16[512,1280]{1,0:T(8,128)(2,1)} %constant_dynamic-update-slice_fusion.2, s32[512]{0:T(512)S(1)} %get-tuple-element.76), kind=kOutput, calls=%fused_computation | convolution fusion | flops 672006144 | bytes 2623488 | tf_op jit(solution)/shard_map/dot_general | solution.py:356
  14.7 3.4 %convolution_convert_fusion.1.refs_7_ = bf16[512,1280]{1,0:T(8,128)(2,1)} fusion(bf16[512,1280]{1,0:T(8,128)(2,1)} %constant_dynamic-update-slice_fusion.2, s32[512]{0:T(512)S(1)} %get-tuple-element.75), kind=kOutput, calls=%fused_computation.1 | convolution fusion | flops 672006144 | bytes 2623488 | tf_op jit(solution)/shard_map/dot_general | solution.py:355
  18.2 0.1 pad_add_fusion.6.refs_0_.sm
  18.2 0.4 collective-permute-start.3
  18.7 0.1 pad_maximum_fusion.2
  18.8 0.1 broadcast_in_dim.20
  18.8 0.1 broadcast_in_dim.21
  18.9 0.1 pad.20.clone
  19.0 7.7 %collective-permute-done.3.refs_6_ = bf16[32,256]{1,0:T(8,128)(2,1)S(1)} collective-permute-done((bf16[32,256]{1,0:T(8,128)(2,1)S(1)}, bf16[32,256]{1,0:T(8,128)(2,1)S(1)}, u32[]{:S(2)}, u32[]{:S(2)}) %collective-permute-start.3) | collective-permute-done | bytes 16416 | tf_op jit(solution)/shard_map/ppermute | solution.py:274
  26.7 0.1 broadcast_in_dim.19.refs_11_
  26.8 28.9 %project.1 = (bf16[2048,512]{1,0:T(8,128)(2,1)}, bf16[2048,256]{1,0:T(8,128)(2,1)S(1)}, bf16[2048,512]{1,0:T(8,128)(2,1)}, f32[8,64,128]{2,1,0:T(8,128)S(1)}, bf...) custom-call(s32[5]{0:T(128)S(1)} %pad_add_fusion.6.refs_0_.sm, ...), custom_call_target="tpu_custom_call" | custom-call | flops 5368709120 | bytes 20971520 | tf_op jit(solution)/shard_map/project/pallas_call | solution.py:414
  55.7 0.1 maximum_maximum_fusion.2
  55.8 1.3 collective-permute-start.4
  57.1 4.2 %collective-permute-start.5 = (bf16[144,512]{1,0:T(8,128)(2,1)S(1)}, bf16[144,512]{1,0:T(8,128)(2,1)S(1)}, u32[]{:S(2)}, u32[]{:S(2)}) collective-permute-start(bf16[144,512]{1,0:T(8,128)(2,1)S(1)} %get-tuple-element.72), channel_id=1, source_target_pairs={{0,4},{2,6},{4,8},{6,10},{8,12},{10,14},{12,16},{14,18},{16,20},{1... | collective-permute-start | bytes 442376 | tf_op jit(solution)/shard_map/ppermute | solution.py:274
  61.4 4.4 %collective-permute-start.6 = (bf16[144,512]{1,0:T(8,128)(2,1)S(1)}, bf16[144,512]{1,0:T(8,128)(2,1)S(1)}, u32[]{:S(2)}, u32[]{:S(2)}) collective-permute-start(bf16[144,512]{1,0:T(8,128)(2,1)S(1)} %get-tuple-element.72), channel_id=1, source_target_pairs={{0,6},{2,8},{4,10},{6,12},{8,14},{10,16},{12,18},{14,20},{16,22},{... | collective-permute-start | bytes 442376 | tf_op jit(solution)/shard_map/ppermute | solution.py:274
  65.8 1.3 collective-permute-start.11
  67.1 1.3 collective-permute-start.12
  68.4 1.6 copy-done.4
  70.0 7.7 %intra.3.refs_6_ = f32[2048,512]{1,0:T(8,128)} custom-call(s32[5]{0:T(128)S(1)} %pad_add_fusion.6.refs_0_.sm, bf16[2048,512]{1,0:T(8,128)(2,1)S(1)} %copy-done.4, bf16[2048,256]{1,0:T(8,128)(2,1)S(1)} %get-tuple-element.33.bc_ref.refs_8_, f32[8,64,128]{2,1,0:T(8,128)S(1)} %get-tuple-element.34.aux_ref.refs_9_, f32[8,512]{1,0:T(8,128)S(1)} %broadcast_in_dim.22.skip_ref), custom_call_target="tpu_custom_call" | custom-call | flops 2684354560 | bytes 8388608 | tf_op jit(solution)/shard_map/intra/pallas_call | solution.py:457
  77.6 1.4 collective-permute-start.13
  79.1 6.4 %collective-permute-done.13 = bf16[144,512]{1,0:T(8,128)(2,1)S(1)} collective-permute-done((bf16[144,512]{1,0:T(8,128)(2,1)S(1)}, bf16[144,512]{1,0:T(8,128)(2,1)S(1)}, u32[]{:S(2)}, u32[]{:S(2)}) %collective-permute-start.13) | collective-permute-done | bytes 147488 | tf_op jit(solution)/shard_map/ppermute | solution.py:274
  85.6 0.1 add_convert_fusion.2
  85.7 0.1 add_convert_fusion.1
  85.8 0.1 maximum_maximum_fusion.3
  85.9 1.3 collective-permute-start.14
  87.2 1.3 collective-permute-start.15
  88.5 1.3 collective-permute-start.16
  89.8 7.7 %intra.2.refs_0_ = f32[2048,512]{1,0:T(8,128)} custom-call(s32[5]{0:T(128)S(1)} %pad_add_fusion.6.refs_0_.sm, bf16[2048,512]{1,0:T(8,128)(2,1)S(1)} %copy-done.3, bf16[2048,256]{1,0:T(8,128)(2,1)S(1)} %get-tuple-element.26.bc_ref.refs_2_, f32[8,64,128]{2,1,0:T(8,128)S(1)} %get-tuple-element.27.aux_ref.refs_3_, f32[8,512]{1,0:T(8,128)S(1)} %broadcast_in_dim.22.skip_ref), custom_call_target="tpu_custom_call" | custom-call | flops 2684354560 | bytes 8388608 | tf_op jit(solution)/shard_map/intra/pallas_call | solution.py:457
  97.6 1.4 collective-permute-start.17
  99.0 4.9 %collective-permute-start.7 = (bf16[144,512]{1,0:T(8,128)(2,1)S(1)}, bf16[144,512]{1,0:T(8,128)(2,1)S(1)}, u32[]{:S(2)}, u32[]{:S(2)}) collective-permute-start(bf16[144,512]{1,0:T(8,128)(2,1)S(1)} %get-tuple-element.70), channel_id=1, source_target_pairs={{0,2},{2,4},{4,6},{6,8},{8,10},{10,12},{12,14},{14,16},{16,18},{18... | collective-permute-start | bytes 442376 | tf_op jit(solution)/shard_map/ppermute | solution.py:274
  103.9 5.4 %collective-permute-start.8 = (bf16[144,512]{1,0:T(8,128)(2,1)S(1)}, bf16[144,512]{1,0:T(8,128)(2,1)S(1)}, u32[]{:S(2)}, u32[]{:S(2)}) collective-permute-start(bf16[144,512]{1,0:T(8,128)(2,1)S(1)} %get-tuple-element.70), channel_id=1, source_target_pairs={{0,10},{2,12},{4,14},{6,16},{8,18},{10,20},{12,22},{14,24},{16,26}... | collective-permute-start | bytes 442376 | tf_op jit(solution)/shard_map/ppermute | solution.py:274
  109.4 5.6 %collective-permute-start.9 = (bf16[144,512]{1,0:T(8,128)(2,1)S(1)}, bf16[144,512]{1,0:T(8,128)(2,1)S(1)}, u32[]{:S(2)}, u32[]{:S(2)}) collective-permute-start(bf16[144,512]{1,0:T(8,128)(2,1)S(1)} %get-tuple-element.70), channel_id=1, source_target_pairs={{0,18},{2,20},{4,22},{6,24},{8,26},{10,28},{12,30},{1,19},{3,21},{... | collective-permute-start | bytes 442376 | tf_op jit(solution)/shard_map/ppermute | solution.py:274
  115.0 1.5 collective-permute-start.10
  116.6 0.1 multiply_add_fusion.refs_11_
  116.7 2.6 %collective-permute-done.9 = bf16[144,512]{1,0:T(8,128)(2,1)S(1)} collective-permute-done((bf16[144,512]{1,0:T(8,128)(2,1)S(1)}, bf16[144,512]{1,0:T(8,128)(2,1)S(1)}, u32[]{:S(2)}, u32[]{:S(2)}) %collective-permute-start.9) | collective-permute-done | bytes 147488 | tf_op jit(solution)/shard_map/ppermute | solution.py:274
  119.3 1.9 %collective-permute-done.10 = bf16[144,512]{1,0:T(8,128)(2,1)S(1)} collective-permute-done((bf16[144,512]{1,0:T(8,128)(2,1)S(1)}, bf16[144,512]{1,0:T(8,128)(2,1)S(1)}, u32[]{:S(2)}, u32[]{:S(2)}) %collective-permute-start.10) | collective-permute-done | bytes 147488 | tf_op jit(solution)/shard_map/ppermute | solution.py:274
  121.1 0.1 multiply_add_fusion.1.refs_5_
  121.3 12.1 %finish.1 = (bf16[2048,512]{1,0:T(8,128)(2,1)S(1)}, f32[8,2048]{1,0:T(8,128)S(1)}, bf16[2048,512]{1,0:T(8,128)(2,1)}, f32[8,2048]{1,0:T(8,128)S(1)}) custom-call(f32[2048,512]{1,0:T(8,128)} %intra.2.refs_0_, bf16[2048,512]{1,0:T(8,128)(2,1)} %get-tuple-element.28.refs_1_, bf16[2048,256]{1,0:T(8,128)(2,1)S(1)} %get-tuple-element.26.bc_ref.refs_2_, ...), custom_call_target="tpu_custom_call" | custom-call | flops 536870912 | bytes 25165824 | tf_op jit(solution)/shard_map/finish/pallas_call | solution.py:469
  133.4 1.3 copy-done.2
  134.7 0.1 broadcast_select_fusion
  134.8 1.5 collective-permute-start.18
  136.3 0.5 fusion.2.wr_ref
  136.8 2.3 %collective-permute-done.18 = f32[8,2048]{1,0:T(8,128)S(1)} collective-permute-done((f32[8,2048]{1,0:T(8,128)S(1)}, f32[8,2048]{1,0:T(8,128)S(1)}, u32[]{:S(2)}, u32[]{:S(2)}) %collective-permute-start.18) | collective-permute-done | bytes 65568 | tf_op jit(solution)/shard_map/ppermute | solution.py:274
  139.1 6.7 %output.1 = (f32[2048,256]{1,0:T(8,128)S(1)}, bf16[2048,256]{1,0:T(8,128)(2,1)S(1)}) custom-call(f32[8,2048]{1,0:T(8,128)S(1)} %add.168.ss_ref, bf16[2048,512]{1,0:T(8,128)(2,1)} %copy-done.2, bf16[2048,512]{1,0:T(8,128)(2,1)} %get-tuple-element.42.gr_ref, bf16[512,512]{1,0:T(8,128)(2,1)S(1)} %fusion.1.wf_ref, bf16[512,512]{1,0:T(8,128)(2,1)S(1)} %fusion.2.wr_ref), custom_call_target="tpu_custom_call" | custom-call | flops 2147483648 | bytes 8388608 | tf_op jit(solution)/shard_map/output/pallas_call | solution.py:497
  145.8 1.6 collective-permute-start.19
  147.4 21.2 %collective-permute-done.19 = bf16[2048,256]{1,0:T(8,128)(2,1)S(1)} collective-permute-done((bf16[2048,256]{1,0:T(8,128)(2,1)S(1)}, bf16[2048,256]{1,0:T(8,128)(2,1)S(1)}, u32[]{:S(2)}, u32[]{:S(2)}) %collective-permute-start.19) | collective-permute-done | bytes 1048608 | tf_op jit(solution)/shard_map/ppermute | solution.py:274
  168.6 1.2 add_convert_fusion
  (65 shorter events, 0.3 us)
Async XLA Ops:
  0.0 10.7 %copy-start = (bf16[512,512]{1,0:T(8,128)(2,1)S(1)}, bf16[512,512]{1,0:T(8,128)(2,1)}, u32[]{:S(2)}) copy-start(bf16[512,512]{1,0:T(8,128)(2,1)} %param.24) | copy-start | bytes 1572868
  0.0 8.1 %copy-start.5 = (bf16[512,512]{1,0:T(8,128)(2,1)S(1)}, bf16[512,512]{1,0:T(8,128)(2,1)}, u32[]{:S(2)}) copy-start(bf16[512,512]{1,0:T(8,128)(2,1)} %param.14) | copy-start | bytes 1572868
  0.0 26.7 %collective-permute-start = (bf16[2048,256]{1,0:T(8,128)(2,1)}, bf16[2048,256]{1,0:T(8,128)(2,1)S(1)}, u32[]{:S(2)}, u32[]{:S(2)}) collective-permute-start(bf16[2048,256]{1,0:T(8,128)(2,1)} %refs_3_.1), channel_id=1, source_target_pairs={{0,1},{1,0},{2,3},{3,2},{4,5},{5,4},{6,7},{7,6},{8,9},{9,8},{10,11... | collective-permute-start | bytes 3145736 | tf_op jit(solution)/shard_map/ppermute | solution.py:274
  3.7 14.5 %collective-permute-start.1 = (bf16[16,256]{1,0:T(8,128)(2,1)S(1)}, bf16[16,256]{1,0:T(8,128)(2,1)S(1)}, u32[]{:S(2)}, u32[]{:S(2)}) collective-permute-start(bf16[16,256]{1,0:T(8,128)(2,1)S(1)} %get-tuple-element.60), channel_id=1, source_target_pairs={{0,2},{2,4},{4,6},{6,8},{8,10},{10,12},{12,14},{14,16},{16,18},{18... | collective-permute-start | bytes 24584 | tf_op jit(solution)/shard_map/ppermute | solution.py:274
  5.2 13.1 %collective-permute-start.2 = (bf16[16,256]{1,0:T(8,128)(2,1)S(1)}, bf16[16,256]{1,0:T(8,128)(2,1)S(1)}, u32[]{:S(2)}, u32[]{:S(2)}) collective-permute-start(bf16[16,256]{1,0:T(8,128)(2,1)S(1)} %get-tuple-element.59), channel_id=1, source_target_pairs={{2,0},{4,2},{6,4},{8,6},{10,8},{12,10},{14,12},{16,14},{18,16},{20... | collective-permute-start | bytes 24584 | tf_op jit(solution)/shard_map/ppermute | solution.py:274
  7.0 2.1 %copy-start.12 = (f32[8]{0:T(128)S(1)}, f32[8]{0:T(128)}, u32[]{:S(2)}) copy-start(f32[8]{0:T(128)} %param.21) | copy-start | bytes 100
  7.0 2.1 %copy-start.7 = (bf16[512,256]{1,0:T(8,128)(2,1)S(1)}, bf16[512,256]{1,0:T(8,128)(2,1)}, u32[]{:S(2)}) copy-start(bf16[512,256]{1,0:T(8,128)(2,1)} %param.16) | copy-start | bytes 786436
  7.0 2.8 %copy-start.6 = (bf16[512,512]{1,0:T(8,128)(2,1)S(1)}, bf16[512,512]{1,0:T(8,128)(2,1)}, u32[]{:S(2)}) copy-start(bf16[512,512]{1,0:T(8,128)(2,1)} %param.15) | copy-start | bytes 1572868
  8.1 2.6 %copy-start.8 = (f32[4,512]{1,0:T(4,128)S(1)}, f32[4,512]{1,0:T(4,128)}, u32[]{:S(2)}) copy-start(f32[4,512]{1,0:T(4,128)} %param.18) | copy-start | bytes 24580
  8.2 2.6 %copy-start.9 = (f32[4,256]{1,0:T(4,128)S(1)}, f32[4,256]{1,0:T(4,128)}, u32[]{:S(2)}) copy-start(f32[4,256]{1,0:T(4,128)} %param.19) | copy-start | bytes 12292
  9.8 1.4 copy-start.13
  14.7 4.0 %copy-start.14 = (f32[8]{0:T(128)S(1)}, f32[8]{0:T(128)}, u32[]{:S(2)}) copy-start(f32[8]{0:T(128)} %param.20) | copy-start | bytes 100
  14.7 4.0 %copy-start.11 = (f32[8]{0:T(128)S(1)}, f32[8]{0:T(128)}, u32[]{:S(2)}) copy-start(f32[8]{0:T(128)} %param.22) | copy-start | bytes 100
  14.7 12.0 %copy-start.1 = (bf16[2048,256]{1,0:T(8,128)(2,1)S(1)}, bf16[2048,256]{1,0:T(8,128)(2,1)}, u32[]{:S(2)}) copy-start(bf16[2048,256]{1,0:T(8,128)(2,1)} %refs_3_.1) | copy-start | bytes 3145732
  18.2 8.4 %collective-permute-start.3 = (bf16[32,256]{1,0:T(8,128)(2,1)S(1)}, bf16[32,256]{1,0:T(8,128)(2,1)S(1)}, u32[]{:S(2)}, u32[]{:S(2)}) collective-permute-start(bf16[32,256]{1,0:T(8,128)(2,1)S(1)} %constant_dynamic-update-slice_fusion.refs_5_), channel_id=1, source_target_pairs={{0,1},{1,0},{2,3},{3,2},{4,5},{5,4},{6,7},{7,6},{8,9},{9,8},{10,11... | collective-permute-start | bytes 49160 | tf_op jit(solution)/shard_map/ppermute | solution.py:274
  55.8 21.8 %collective-permute-start.4 = (bf16[144,512]{1,0:T(8,128)(2,1)S(1)}, bf16[144,512]{1,0:T(8,128)(2,1)S(1)}, u32[]{:S(2)}, u32[]{:S(2)}) collective-permute-start(bf16[144,512]{1,0:T(8,128)(2,1)S(1)} %get-tuple-element.72), channel_id=1, source_target_pairs={{0,2},{2,4},{4,6},{6,8},{8,10},{10,12},{12,14},{14,16},{16,18},{18... | collective-permute-start | bytes 442376 | tf_op jit(solution)/shard_map/ppermute | solution.py:274
  57.1 21.9 %collective-permute-start.5 = (bf16[144,512]{1,0:T(8,128)(2,1)S(1)}, bf16[144,512]{1,0:T(8,128)(2,1)S(1)}, u32[]{:S(2)}, u32[]{:S(2)}) collective-permute-start(bf16[144,512]{1,0:T(8,128)(2,1)S(1)} %get-tuple-element.72), channel_id=1, source_target_pairs={{0,4},{2,6},{4,8},{6,10},{8,12},{10,14},{12,16},{14,18},{16,20},{1... | collective-permute-start | bytes 442376 | tf_op jit(solution)/shard_map/ppermute | solution.py:274
  61.4 17.7 %collective-permute-start.6 = (bf16[144,512]{1,0:T(8,128)(2,1)S(1)}, bf16[144,512]{1,0:T(8,128)(2,1)S(1)}, u32[]{:S(2)}, u32[]{:S(2)}) collective-permute-start(bf16[144,512]{1,0:T(8,128)(2,1)S(1)} %get-tuple-element.72), channel_id=1, source_target_pairs={{0,6},{2,8},{4,10},{6,12},{8,14},{10,16},{12,18},{14,20},{16,22},{... | collective-permute-start | bytes 442376 | tf_op jit(solution)/shard_map/ppermute | solution.py:274
  65.8 13.3 %collective-permute-start.11 = (bf16[144,512]{1,0:T(8,128)(2,1)S(1)}, bf16[144,512]{1,0:T(8,128)(2,1)S(1)}, u32[]{:S(2)}, u32[]{:S(2)}) collective-permute-start(bf16[144,512]{1,0:T(8,128)(2,1)S(1)} %get-tuple-element.71), channel_id=1, source_target_pairs={{2,0},{4,2},{6,4},{8,6},{10,8},{12,10},{14,12},{16,14},{18,16},{20... | collective-permute-start | bytes 442376 | tf_op jit(solution)/shard_map/ppermute | solution.py:274
  67.1 12.1 %collective-permute-start.12 = (bf16[144,512]{1,0:T(8,128)(2,1)S(1)}, bf16[144,512]{1,0:T(8,128)(2,1)S(1)}, u32[]{:S(2)}, u32[]{:S(2)}) collective-permute-start(bf16[144,512]{1,0:T(8,128)(2,1)S(1)} %get-tuple-element.71), channel_id=1, source_target_pairs={{4,0},{6,2},{8,4},{10,6},{12,8},{14,10},{16,12},{18,14},{20,16},{2... | collective-permute-start | bytes 442376 | tf_op jit(solution)/shard_map/ppermute | solution.py:274
  68.4 1.6 copy-start.4
  77.6 12.2 %copy-start.3 = (bf16[2048,512]{1,0:T(8,128)(2,1)S(1)}, bf16[2048,512]{1,0:T(8,128)(2,1)}, u32[]{:S(2)}) copy-start(bf16[2048,512]{1,0:T(8,128)(2,1)} %get-tuple-element.25.x_ref) | copy-start | bytes 6291460
  77.6 7.9 %collective-permute-start.13 = (bf16[144,512]{1,0:T(8,128)(2,1)S(1)}, bf16[144,512]{1,0:T(8,128)(2,1)S(1)}, u32[]{:S(2)}, u32[]{:S(2)}) collective-permute-start(bf16[144,512]{1,0:T(8,128)(2,1)S(1)} %get-tuple-element.71), channel_id=1, source_target_pairs={{6,0},{8,2},{10,4},{12,6},{14,8},{16,10},{18,12},{20,14},{22,16},{... | collective-permute-start | bytes 442376 | tf_op jit(solution)/shard_map/ppermute | solution.py:274
  85.9 18.0 %collective-permute-start.14 = (bf16[144,512]{1,0:T(8,128)(2,1)S(1)}, bf16[144,512]{1,0:T(8,128)(2,1)S(1)}, u32[]{:S(2)}, u32[]{:S(2)}) collective-permute-start(bf16[144,512]{1,0:T(8,128)(2,1)S(1)} %get-tuple-element.69), channel_id=1, source_target_pairs={{2,0},{4,2},{6,4},{8,6},{10,8},{12,10},{14,12},{16,14},{18,16},{20... | collective-permute-start | bytes 442376 | tf_op jit(solution)/shard_map/ppermute | solution.py:274
  87.2 22.1 %collective-permute-start.15 = (bf16[144,512]{1,0:T(8,128)(2,1)S(1)}, bf16[144,512]{1,0:T(8,128)(2,1)S(1)}, u32[]{:S(2)}, u32[]{:S(2)}) collective-permute-start(bf16[144,512]{1,0:T(8,128)(2,1)S(1)} %get-tuple-element.69), channel_id=1, source_target_pairs={{10,0},{12,2},{14,4},{16,6},{18,8},{20,10},{22,12},{24,14},{26,16}... | collective-permute-start | bytes 442376 | tf_op jit(solution)/shard_map/ppermute | solution.py:274
  88.5 26.5 %collective-permute-start.16 = (bf16[144,512]{1,0:T(8,128)(2,1)S(1)}, bf16[144,512]{1,0:T(8,128)(2,1)S(1)}, u32[]{:S(2)}, u32[]{:S(2)}) collective-permute-start(bf16[144,512]{1,0:T(8,128)(2,1)S(1)} %get-tuple-element.69), channel_id=1, source_target_pairs={{18,0},{20,2},{22,4},{24,6},{26,8},{28,10},{30,12},{19,1},{21,3},{... | collective-permute-start | bytes 442376 | tf_op jit(solution)/shard_map/ppermute | solution.py:274
  97.6 23.7 %copy-start.10 = (f32[512]{0:T(512)S(1)}, f32[512]{0:T(512)}, u32[]{:S(2)}) copy-start(f32[512]{0:T(512)} %param.23) | copy-start | bytes 6148
  97.6 19.0 %collective-permute-start.17 = (bf16[144,512]{1,0:T(8,128)(2,1)S(1)}, bf16[144,512]{1,0:T(8,128)(2,1)S(1)}, u32[]{:S(2)}, u32[]{:S(2)}) collective-permute-start(bf16[144,512]{1,0:T(8,128)(2,1)S(1)} %get-tuple-element.69), channel_id=1, source_target_pairs={{26,0},{28,2},{30,4},{27,1},{29,3},{31,5}} | collective-permute-start | bytes 442376 | tf_op jit(solution)/shard_map/ppermute | solution.py:274
  99.0 17.7 %collective-permute-start.7 = (bf16[144,512]{1,0:T(8,128)(2,1)S(1)}, bf16[144,512]{1,0:T(8,128)(2,1)S(1)}, u32[]{:S(2)}, u32[]{:S(2)}) collective-permute-start(bf16[144,512]{1,0:T(8,128)(2,1)S(1)} %get-tuple-element.70), channel_id=1, source_target_pairs={{0,2},{2,4},{4,6},{6,8},{8,10},{10,12},{12,14},{14,16},{16,18},{18... | collective-permute-start | bytes 442376 | tf_op jit(solution)/shard_map/ppermute | solution.py:274
  103.9 12.7 %collective-permute-start.8 = (bf16[144,512]{1,0:T(8,128)(2,1)S(1)}, bf16[144,512]{1,0:T(8,128)(2,1)S(1)}, u32[]{:S(2)}, u32[]{:S(2)}) collective-permute-start(bf16[144,512]{1,0:T(8,128)(2,1)S(1)} %get-tuple-element.70), channel_id=1, source_target_pairs={{0,10},{2,12},{4,14},{6,16},{8,18},{10,20},{12,22},{14,24},{16,26}... | collective-permute-start | bytes 442376 | tf_op jit(solution)/shard_map/ppermute | solution.py:274
  109.4 9.9 %collective-permute-start.9 = (bf16[144,512]{1,0:T(8,128)(2,1)S(1)}, bf16[144,512]{1,0:T(8,128)(2,1)S(1)}, u32[]{:S(2)}, u32[]{:S(2)}) collective-permute-start(bf16[144,512]{1,0:T(8,128)(2,1)S(1)} %get-tuple-element.70), channel_id=1, source_target_pairs={{0,18},{2,20},{4,22},{6,24},{8,26},{10,28},{12,30},{1,19},{3,21},{... | collective-permute-start | bytes 442376 | tf_op jit(solution)/shard_map/ppermute | solution.py:274
  115.0 6.1 %collective-permute-start.10 = (bf16[144,512]{1,0:T(8,128)(2,1)S(1)}, bf16[144,512]{1,0:T(8,128)(2,1)S(1)}, u32[]{:S(2)}, u32[]{:S(2)}) collective-permute-start(bf16[144,512]{1,0:T(8,128)(2,1)S(1)} %get-tuple-element.70), channel_id=1, source_target_pairs={{0,26},{2,28},{4,30},{1,27},{3,29},{5,31}} | collective-permute-start | bytes 442376 | tf_op jit(solution)/shard_map/ppermute | solution.py:274
  133.4 1.3 copy-start.2
  134.8 4.3 %collective-permute-start.18 = (f32[8,2048]{1,0:T(8,128)S(1)}, f32[8,2048]{1,0:T(8,128)S(1)}, u32[]{:S(2)}, u32[]{:S(2)}) collective-permute-start(f32[8,2048]{1,0:T(8,128)S(1)} %broadcast_select_fusion), channel_id=1, source_target_pairs={{0,1},{1,0},{2,3},{3,2},{4,5},{5,4},{6,7},{7,6},{8,9},{9,8},{10,11... | collective-permute-start | bytes 196616 | tf_op jit(solution)/shard_map/ppermute | solution.py:274
  145.8 22.8 %collective-permute-start.19 = (bf16[2048,256]{1,0:T(8,128)(2,1)S(1)}, bf16[2048,256]{1,0:T(8,128)(2,1)S(1)}, u32[]{:S(2)}, u32[]{:S(2)}) collective-permute-start(bf16[2048,256]{1,0:T(8,128)(2,1)S(1)} %get-tuple-element.44), channel_id=1, source_target_pairs={{0,1},{1,0},{2,3},{3,2},{4,5},{5,4},{6,7},{7,6},{8,9},{9,8},{10,11... | collective-permute-start | bytes 3145736 | tf_op jit(solution)/shard_map/ppermute | solution.py:274
where the time goes:
time: 172 us; the launch traced here: 170 us
  Pallas kernels  63 us (37%)
  starting transfers between devices  45.9 us (27%)
  waiting for transfers between devices  42.1 us (24%)
  matrix products  8.83 us (5%)
  local copies, waits for them, and re-layouts  6.53 us (4%)
  other arithmetic  2.85 us (2%)
    ppermute x20, starting transfers between devices, shift(): return lax.ppermute(value, axis, pairs)  45.9 us
    ppermute x20, waiting for transfers between devices, shift(): return lax.ppermute(value, axis, pairs)  42.1 us
    pallas_call x1, Pallas kernels, shards(): pl.pallas_call(functools.partial(project_kernel, nc, mp, inner, pieces),...  28.9 us
    pallas_call x2, Pallas kernels, shards(): pl.pallas_call(functools.partial(intra_kernel, forward, heads, inner, pie...  15.4 us
    pallas_call x1, Pallas kernels, shards(): pl.pallas_call(functools.partial(finish_kernel, nc, inner), grid=(nc,), i...  12.1 us
    pallas_call x1, Pallas kernels, shards(): pl.pallas_call(functools.partial(output_kernel, mp, inner * mp), grid=(nc...  6.72 us
    unnamed x33, local copies, waits for them, and re-layouts  4.59 us
  transfers between devices with their start and end apart: 20, of which 6 were waited for; matrix products, arithmetic and copies ran while one was open for 8% of the time, Pallas kernels for 9%

commit v1 on v0

--- a/solution.py
+++ b/solution.py
@@ -182,14 +182,15 @@
     outs[13][...] = dec_r[...]
 
 
-def intra_kernel(forward, heads, inner, pieces, sm, x_ref, bc_ref, aux_ref, skip_ref, y_ref):
-    first = sm[pieces] + pl.program_id(0) * CHUNK
+def intra_rows(forward, heads, pieces, sm, x_ref, bc_ref, aux_ref, skip_ref, y_ref, chunk):
+    base = sm[pieces]
     rows = lax.broadcasted_iota(jnp.int32, (SUB, SUB), 0)
     lanes = lax.broadcasted_iota(jnp.int32, (SUB, SUB), 1)
     left = lanes < HEAD_DIM
+    aux = aux_ref[chunk]
     for b in (0, 1):
-        at = slice(b * SUB, (b + 1) * SUB)
-        begin = first + b * SUB
+        at = pl.ds(pl.multiple_of(chunk * CHUNK + b * SUB, SUB), SUB)
+        begin = base + chunk * CHUNK + b * SUB
         if forward:
             mask = (lanes <= rows) & (begin + lanes >= piece_start(sm, pieces, begin + rows))
         else:
@@ -197,16 +198,15 @@
         scores = lax.dot_general(
             bc_ref[at, NSTATE:], bc_ref[at, 0:NSTATE], NT, preferred_element_type=F32
         )
-        cum_t = aux_ref[0, b * 8 : b * 8 + 8, :].T
-        cum_s = aux_ref[0, 16 + b * 8 : 16 + b * 8 + 8, :]
+        cum_t = aux[b * 8 : b * 8 + 8, :].T
+        cum_s = aux[16 + b * 8 : 16 + b * 8 + 8, :]
         for pair in range(heads // 2):
             cols = slice(pair * 128, (pair + 1) * 128)
-            xp = x_ref[at, cols]
+            xf = x_ref[at, cols].astype(F32)
             parts = []
             for h in (2 * pair, 2 * pair + 1):
                 gap = jnp.where(mask, cum_t[:, h : h + 1] - cum_s[h : h + 1, :], -1e30)
                 parts.append((jnp.exp2(gap) * scores).astype(BF16))
-            xf = xp.astype(F32)
             stacked = jnp.concatenate(
                 [
                     jnp.where(left, xf, 0.0).astype(BF16),
@@ -217,7 +217,113 @@
             mixed = jnp.dot(
                 jnp.concatenate(parts, axis=1), stacked, preferred_element_type=F32
             )
-            y_ref[at, cols] = mixed + skip_ref[0:1, cols] * xf
+            y_ref[at, cols] = (mixed + skip_ref[0:1, cols] * xf).astype(BF16)
+
+
+def rounds_of(count):
+    rounds, window = [], 1
+    while 4 * window < count - 1:
+        rounds.append([window * k for k in (1, 2, 3)])
+        window *= 4
+    rounds.append([1 + window * k for k in range(-(-(count - 1) // window))])
+    return rounds
+
+
+def exchange_kernel(count, nc, heads, pieces, *refs):
+    sm, st_f, st_r, dec_f, dec_r, x_f, bc_f, aux_f, x_r, bc_r, aux_r, skip = refs[:12]
+    y_f, y_r, into_f, into_r = refs[12:16]
+    sent, landed, held, fade, send_sem, recv_sem = refs[16:]
+    index = lax.axis_index("ctx")
+    rounds = rounds_of(count)
+    signs = (1, -1)
+
+    def reaches(step):
+        return index + step < count if step > 0 else index + step >= 0
+
+    def peer(step):
+        return {"ctx": index + step}
+
+    barrier = pltpu.get_barrier_semaphore()
+    steps = sorted({sign * s for r in rounds for s in r for sign in signs})
+    for step in steps:
+
+        @pl.when(reaches(step))
+        def _(step=step):
+            pl.semaphore_signal(
+                barrier, inc=1, device_id=peer(step), device_id_type=pl.DeviceIdType.MESH
+            )
+
+    peers = sum(
+        1 - lax.div(index + step, count) if step > 0 else lax.div(index + step + count, count)
+        for step in steps
+    )
+    pl.semaphore_wait(barrier, peers)
+
+    held[0], held[1] = st_f[...], st_r[...]
+    fade[0], fade[1] = dec_f[...], dec_r[...]
+    jobs = (
+        (True, x_f, bc_f, aux_f, y_f),
+        (False, x_r, bc_r, aux_r, y_r),
+    )
+    slot = 0
+    for number, shifts in enumerate(rounds):
+        last = number == len(rounds) - 1
+        copies = []
+        for stream, sign in enumerate(signs):
+            at = number * 2 + stream
+            decay = fade[stream]
+            high = decay.astype(BF16)
+            low = (decay - high.astype(F32)).astype(BF16)
+            sent[at, 0:NSTATE, :] = held[stream].astype(BF16)
+            sent[at, NSTATE : NSTATE + 16, :] = jnp.concatenate([high, low], axis=0)
+            for s in shifts:
+                copy = pltpu.make_async_remote_copy(
+                    src_ref=sent.at[at],
+                    dst_ref=landed.at[slot],
+                    send_sem=send_sem.at[slot],
+                    recv_sem=recv_sem.at[slot],
+                    device_id=peer(sign * s),
+                    device_id_type=pl.DeviceIdType.MESH,
+                )
+                copies.append((stream, sign * s, slot, copy))
+                slot += 1
+
+                @pl.when(reaches(sign * s))
+                def _(copy=copy):
+                    copy.start()
+
+        if number < len(jobs):
+            forward, x_ref, bc_ref, aux_ref, y_ref = jobs[number]
+
+            def body(chunk, carry):
+                intra_rows(
+                    forward, heads, pieces, sm, x_ref, bc_ref, aux_ref, skip, y_ref, chunk
+                )
+                return carry
+
+            lax.fori_loop(0, nc, body, 0)
+
+        if last:
+            held[...] = jnp.zeros_like(held)
+            fade[...] = jnp.ones_like(fade)
+        for stream, step, at, copy in copies:
+
+            @pl.when(reaches(-step))
+            def _(stream=stream, at=at, copy=copy):
+                copy.wait_recv()
+                more = landed[at, 0:NSTATE, :].astype(F32)
+                tail = landed[at, NSTATE : NSTATE + 16, :].astype(F32)
+                held[stream] = held[stream] + fade[stream, 0:1, :] * more
+                fade[stream] = fade[stream] * (tail[0:8] + tail[8:16])
+
+        for stream, step, at, copy in copies:
+
+            @pl.when(reaches(step))
+            def _(copy=copy):
+                copy.wait_send()
+
+    into_f[...] = held[0]
+    into_r[...] = held[1]
 
 
 def finish_kernel(nc, inner, *refs):
@@ -243,7 +349,7 @@
             state = (before_ref[b].astype(F32) + grow * into).astype(BF16)
             factor = expand_rows(aux_ref[0, 32 + b * 8 : 40 + b * 8, :], e2[...])
             inter = jnp.dot(bc_ref[at, NSTATE:], state, preferred_element_type=F32)
-            mixed = y_ref[at, :] + inter * factor
+            mixed = y_ref[at, :].astype(F32) + inter * factor
             gated = mixed * silu(z_ref[at, :].astype(F32))
             ss_out[:, at] = lax.dot_general(
                 ones, (gated * gated).astype(BF16), NT, preferred_element_type=F32
@@ -272,53 +378,6 @@
     else:
         pairs = [(i, i + by) for i in range(count) if 0 <= i + by < count]
     return lax.ppermute(value, axis, pairs)
-
-
-def pack_state(state, decay):
-    high = decay[0:1].astype(BF16)
-    low = (decay[0:1] - high.astype(F32)).astype(BF16)
-    tail = jnp.concatenate([high, low, jnp.zeros((14, decay.shape[1]), BF16)], axis=0)
-    return jnp.concatenate([state.astype(BF16), tail], axis=0)
-
-
-def unpack_state(packed):
-    decay = packed[NSTATE : NSTATE + 1].astype(F32) + packed[NSTATE + 1 : NSTATE + 2].astype(F32)
-    return packed[:NSTATE].astype(F32), decay
-
-
-def prefix_states(states, decays, axis):
-    count = lax.axis_size(axis)
-    signs = (1, -1)
-    cur = [(s, d[0:1]) for s, d in zip(states, decays)]
-    window = 1
-    while 4 * window < count - 1:
-        packed = [pack_state(*c) for c in cur]
-        got = [
-            [shift(p, axis, sign * window * k, False) for k in (1, 2, 3)]
-            for p, sign in zip(packed, signs)
-        ]
-        new = []
-        for (s, d), parts in zip(cur, got):
-            for part in parts:
-                more, fade = unpack_state(part)
-                s, d = s + d * more, d * fade
-            new.append((s, d))
-        cur = new
-        window *= 4
-    reach = -(-(count - 1) // window)
-    packed = [pack_state(*c) for c in cur]
-    got = [
-        [shift(p, axis, sign * (1 + window * k), False) for k in range(reach)]
-        for p, sign in zip(packed, signs)
-    ]
-    result = []
-    for parts in got:
-        s, d = unpack_state(parts[0])
-        for part in parts[1:]:
-            more, fade = unpack_state(part)
-            s, d = s + d * more, d * fade
-        result.append(s)
-    return result
 
 
 def cost(flops, size, trans=0):
@@ -449,22 +508,33 @@
     )(sm, *blocks, *blocks, *halos, w_f, w_r, w_dt2, conv_w, head_par, e1, e2)
     fwd, rev = made[0:5], made[5:10]
 
-    into = prefix_states(made[10:12], made[12:14], "ctx")
-
-    mixed = []
-    for forward, parts in ((True, fwd), (False, rev)):
-        mixed.append(
-            pl.pallas_call(
-                functools.partial(intra_kernel, forward, heads, inner, pieces),
-                grid=(nc,),
-                in_specs=[smem, up(inner), up(2 * NSTATE), aux_up, whole((8, inner))],
-                out_specs=up(inner),
-                out_shape=sds((rows, inner), F32),
-                compiler_params=params,
-                cost_estimate=cost(20 * rows * SUB * inner, 8 << 20, rows * SUB * heads),
-                name="intra",
-            )(sm, parts[0], parts[1], parts[3], skip8)
-        )
+    count = lax.axis_size("ctx")
+    rounds = rounds_of(count)
+    slots = 2 * sum(len(r) for r in rounds)
+    packed = NSTATE + 16
+    vmem = pl.BlockSpec(memory_space=pltpu.VMEM)
+    *mixed, into_f, into_r = pl.pallas_call(
+        functools.partial(exchange_kernel, count, nc, heads, pieces),
+        in_specs=[smem] + [vmem] * 11,
+        out_specs=[vmem] * 4,
+        out_shape=[sds((rows, inner), BF16)] * 2 + [sds((NSTATE, inner), F32)] * 2,
+        scratch_shapes=[
+            pltpu.VMEM((2 * len(rounds), packed, inner), BF16),
+            pltpu.VMEM((slots, packed, inner), BF16),
+            pltpu.VMEM((2, NSTATE, inner), F32),
+            pltpu.VMEM((2, 8, inner), F32),
+            pltpu.SemaphoreType.DMA((slots,)),
+            pltpu.SemaphoreType.DMA((slots,)),
+        ],
+        compiler_params=pltpu.CompilerParams(
+            vmem_limit_bytes=VMEM_LIMIT, collective_id=0, has_side_effects=True
+        ),
+        cost_estimate=cost(40 * rows * SUB * inner, 16 << 20, 2 * rows * SUB * heads),
+        name="exchange",
+    )(
+        sm, *made[10:14], fwd[0], fwd[1], fwd[3], rev[0], rev[1], rev[3], skip8,
+    )
+    into = (into_f, into_r)
 
     finished = pl.pallas_call(
         functools.partial(finish_kernel, nc, inner),

time: 172 us -> 143 us (0.83)
  starting transfers between devices: 45.9 us -> 9.25 us
  Pallas kernels: 63 us -> 81.9 us
  waiting for transfers between devices: 42.1 us -> 36.5 us
  local copies, waits for them, and re-layouts: 6.53 us -> 4.6 us
    ppermute x20 -> x6, starting transfers between devices: 45.9 us -> 9.25 us  [shift(): return lax.ppermute(value, axis, pairs)]
    pallas_call x2 -> x1, Pallas kernels: 15.4 us -> 35 us  [shards(): pl.pallas_call(functools.partial(exchange_kernel, count, nc, heads, piece...]
    ppermute x20 -> x6, waiting for transfers between devices: 42.1 us -> 36.5 us  [shift(): return lax.ppermute(value, axis, pairs)]
  transfers between devices with their start and end apart: 20 -> 6, of which waited for: 6 -> 3; matrix products, arithmetic and copies ran while one was open for 8% -> 6% of each run, Pallas kernels for 9% -> 0%
where the time goes in v1:
time: 143 us; the launch traced here: 142 us
  Pallas kernels  81.9 us (57%)
  waiting for transfers between devices  36.5 us (26%)
  starting transfers between devices  9.25 us (6%)
  matrix products  7.45 us (5%)
  local copies, waits for them, and re-layouts  4.6 us (3%)
  other arithmetic  2.24 us (2%)
    ppermute x6, waiting for transfers between devices, shift(): return lax.ppermute(value, axis, pairs)  36.5 us
    pallas_call x1, Pallas kernels, shards(): pl.pallas_call(functools.partial(exchange_kernel, count, nc, heads, piece...  35 us
    pallas_call x1, Pallas kernels, shards(): pl.pallas_call(functools.partial(project_kernel, nc, mp, inner, pieces),...  28.6 us
    pallas_call x1, Pallas kernels, shards(): pl.pallas_call(functools.partial(finish_kernel, nc, inner), grid=(nc,), i...  11.5 us
    ppermute x6, starting transfers between devices, shift(): return lax.ppermute(value, axis, pairs)  9.25 us
    pallas_call x1, Pallas kernels, shards(): pl.pallas_call(functools.partial(output_kernel, mp, inner * mp), grid=(nc...  6.73 us
    unnamed x33, local copies, waits for them, and re-layouts  3.6 us
    dot_general x1, matrix products, shards(): w_f = jnp.dot(pick_f, w_in, preferred_element_type=F32).astype(BF16)  3.37 us
  transfers between devices with their start and end apart: 6, of which 3 were waited for; matrix products, arithmetic and copies ran while one was open for 6% of the time, Pallas kernels for 0%

profile of v1, /device:TPU:0, one launch (start us, length us, event | category | flops | bytes accessed | tf_op | source)
XLA Modules:
  0.0 142.3 jit_solution(3018592652895750972)
XLA Ops:
  0.0 0.0 copy-start
  0.0 0.0 copy-start.4
  0.0 3.0 %collective-permute-start = (bf16[2048,256]{1,0:T(8,128)(2,1)}, bf16[2048,256]{1,0:T(8,128)(2,1)S(1)}, u32[]{:S(2)}, u32[]{:S(2)}) collective-permute-start(bf16[2048,256]{1,0:T(8,128)(2,1)} %refs_3_.1), channel_id=1, source_target_pairs={{0,1},{1,0},{2,3},{3,2},{4,5},{5,4},{6,7},{7,6},{8,9},{9,8},{10,11... | collective-permute-start | bytes 3145736 | tf_op jit(solution)/shard_map/ppermute | solution.py:380
  3.0 0.7 fusion.24
  3.7 1.4 %collective-permute-start.1 = (bf16[16,256]{1,0:T(8,128)(2,1)S(1)}, bf16[16,256]{1,0:T(8,128)(2,1)S(1)}, u32[]{:S(2)}, u32[]{:S(2)}) collective-permute-start(bf16[16,256]{1,0:T(8,128)(2,1)S(1)} %get-tuple-element.54), channel_id=1, source_target_pairs={{0,2},{2,4},{4,6},{6,8},{8,10},{10,12},{12,14},{14,16},{16,18},{18... | collective-permute-start | bytes 24584 | tf_op jit(solution)/shard_map/ppermute | solution.py:380
  5.2 1.3 collective-permute-start.2
  6.5 0.2 iota_compare_fusion.2
  6.7 0.2 iota_compare_fusion.3
  7.0 0.0 copy-start.12
  7.0 0.0 copy-start.6
  7.0 0.0 copy-start.5
  7.0 1.1 fusion.4
  8.1 0.0 copy-done.4
  8.1 0.0 copy-start.8
  8.2 0.0 copy-start.9
  8.2 0.0 copy-done.12
  8.3 0.0 copy-done.6
  8.3 0.0 copy-done.5
  8.3 0.0 copy-start.13
  8.4 0.5 copy-done.8
  8.9 0.0 copy-done.9
  8.9 0.0 copy-start.7
  8.9 0.0 copy-done
  8.9 0.5 fusion.1.wf_ref
  9.4 0.0 copy-done.13
  9.4 0.2 reduce-window.9
  9.6 0.3 copy-done.7
  9.9 2.0 %convolution_convert_fusion.refs_8_ = bf16[512,1280]{1,0:T(8,128)(2,1)} fusion(bf16[512,1280]{1,0:T(8,128)(2,1)S(1)} %constant_dynamic-update-slice_fusion.2, s32[512]{0:T(512)S(1)} %get-tuple-element.62), kind=kOutput, calls=%fused_computation | convolution fusion | flops 672006144 | bytes 2623488 | tf_op jit(solution)/shard_map/dot_general | solution.py:415
  11.9 0.0 copy-start.14
  11.9 0.0 copy-start.11
  11.9 0.0 copy-start.2
  11.9 3.4 %convolution_convert_fusion.1.refs_7_ = bf16[512,1280]{1,0:T(8,128)(2,1)} fusion(bf16[512,1280]{1,0:T(8,128)(2,1)} %copy-done.7, s32[512]{0:T(512)S(1)} %get-tuple-element.61), kind=kOutput, calls=%fused_computation.1 | convolution fusion | flops 672006144 | bytes 2623488 | tf_op jit(solution)/shard_map/dot_general | solution.py:414
  15.3 0.1 pad_add_fusion.6.refs_0_
  15.3 0.0 collective-permute-done.1
  15.3 0.0 collective-permute-done.2
  15.4 0.4 collective-permute-start.3
  15.8 0.0 copy-done.14
  15.8 0.1 pad_maximum_fusion.2
  15.9 0.0 copy-done.11
  15.9 0.1 broadcast_in_dim.20
  15.9 0.1 broadcast_in_dim.21
  16.0 10.7 %collective-permute-done.3.refs_6_ = bf16[32,256]{1,0:T(8,128)(2,1)S(1)} collective-permute-done((bf16[32,256]{1,0:T(8,128)(2,1)S(1)}, bf16[32,256]{1,0:T(8,128)(2,1)S(1)}, u32[]{:S(2)}, u32[]{:S(2)}) %collective-permute-start.3) | collective-permute-done | bytes 16416 | tf_op jit(solution)/shard_map/ppermute | solution.py:380
  26.7 0.0 collective-permute-done.refs_2_.refs_4_
  26.7 0.1 broadcast_in_dim.19.refs_11_
  26.8 0.0 copy-done.2
  26.8 28.6 %project.1 = (bf16[2048,512]{1,0:T(8,128)(2,1)}, bf16[2048,256]{1,0:T(8,128)(2,1)S(1)}, bf16[2048,512]{1,0:T(8,128)(2,1)}, f32[8,64,128]{2,1,0:T(8,128)S(1)}, bf...) custom-call(s32[5]{0:T(128)S(1)} %pad_add_fusion.6.refs_0_, ...), custom_call_target="tpu_custom_call" | custom-call | flops 5368709120 | bytes 20971520 | tf_op jit(solution)/shard_map/project/pallas_call | solution.py:473
  55.4 0.0 copy-start.10
  55.4 35.0 %exchange.1 = (bf16[2048,512]{1,0:T(8,128)(2,1)S(1)}, bf16[2048,512]{1,0:T(8,128)(2,1)}, f32[128,512]{1,0:T(8,128)S(1)}, f32[128,512]{1,0:T(8,128)S(1)}) custom-call(s32[5]{0:T(128)S(1)} %pad_add_fusion.6.refs_0_, f32[128,512]{1,0:T(8,128)S(1)} %get-tuple-element.29.refs_1_, f32[128,512]{1,0:T(8,128)S(1)} %get-tuple-element.30.refs_2_, ...), custom_call_target="tpu_custom_call" | custom-call | flops 5368709120 | bytes 16777216 | tf_op jit(solution)/shard_map/exchange/pallas_call | solution.py:516
  90.5 0.0 copy-start.1
  90.5 1.3 copy-done.1
  91.8 0.0 copy-done.10
  91.8 11.5 %finish.1 = (bf16[2048,512]{1,0:T(8,128)(2,1)S(1)}, f32[8,2048]{1,0:T(8,128)S(1)}, bf16[2048,512]{1,0:T(8,128)(2,1)}, f32[8,2048]{1,0:T(8,128)S(1)}) custom-call(bf16[2048,512]{1,0:T(8,128)(2,1)} %copy-done.1, bf16[2048,512]{1,0:T(8,128)(2,1)} %get-tuple-element.40.refs_1_, bf16[2048,256]{1,0:T(8,128)(2,1)S(1)} %get-tuple-element.34.refs_6_.refs_2_, ...), custom_call_target="tpu_custom_call" | custom-call | flops 536870912 | bytes 25165824 | tf_op jit(solution)/shard_map/finish/pallas_call | solution.py:539
  103.3 0.0 copy-start.3
  103.3 1.3 copy-done.3
  104.6 0.1 broadcast_select_fusion
  104.7 1.5 %collective-permute-start.4 = (f32[8,2048]{1,0:T(8,128)S(1)}, f32[8,2048]{1,0:T(8,128)S(1)}, u32[]{:S(2)}, u32[]{:S(2)}) collective-permute-start(f32[8,2048]{1,0:T(8,128)S(1)} %broadcast_select_fusion), channel_id=1, source_target_pairs={{0,1},{1,0},{2,3},{3,2},{4,5},{5,4},{6,7},{7,6},{8,9},{9,8},{10,11... | collective-permute-start | bytes 196616 | tf_op jit(solution)/shard_map/ppermute | solution.py:380
  106.2 0.5 fusion.2.wr_ref
  106.7 2.5 %collective-permute-done.4 = f32[8,2048]{1,0:T(8,128)S(1)} collective-permute-done((f32[8,2048]{1,0:T(8,128)S(1)}, f32[8,2048]{1,0:T(8,128)S(1)}, u32[]{:S(2)}, u32[]{:S(2)}) %collective-permute-start.4) | collective-permute-done | bytes 65568 | tf_op jit(solution)/shard_map/ppermute | solution.py:380
  109.3 6.7 %output.1 = (f32[2048,256]{1,0:T(8,128)S(1)}, bf16[2048,256]{1,0:T(8,128)(2,1)S(1)}) custom-call(f32[8,2048]{1,0:T(8,128)S(1)} %add.72.ss_ref, bf16[2048,512]{1,0:T(8,128)(2,1)} %copy-done.3, bf16[2048,512]{1,0:T(8,128)(2,1)} %get-tuple-element.50.gr_ref, bf16[512,512]{1,0:T(8,128)(2,1)S(1)} %fusion.1.wf_ref, bf16[512,512]{1,0:T(8,128)(2,1)S(1)} %fusion.2.wr_ref), custom_call_target="tpu_custom_call" | custom-call | flops 2147483648 | bytes 8388608 | tf_op jit(solution)/shard_map/output/pallas_call | solution.py:567
  116.0 1.6 %collective-permute-start.5 = (bf16[2048,256]{1,0:T(8,128)(2,1)S(1)}, bf16[2048,256]{1,0:T(8,128)(2,1)S(1)}, u32[]{:S(2)}, u32[]{:S(2)}) collective-permute-start(bf16[2048,256]{1,0:T(8,128)(2,1)S(1)} %get-tuple-element.52), channel_id=1, source_target_pairs={{0,1},{1,0},{2,3},{3,2},{4,5},{5,4},{6,7},{7,6},{8,9},{9,8},{10,11... | collective-permute-start | bytes 3145736 | tf_op jit(solution)/shard_map/ppermute | solution.py:380
  117.6 23.3 %collective-permute-done.5 = bf16[2048,256]{1,0:T(8,128)(2,1)S(1)} collective-permute-done((bf16[2048,256]{1,0:T(8,128)(2,1)S(1)}, bf16[2048,256]{1,0:T(8,128)(2,1)S(1)}, u32[]{:S(2)}, u32[]{:S(2)}) %collective-permute-start.5) | collective-permute-done | bytes 1048608 | tf_op jit(solution)/shard_map/ppermute | solution.py:380
  140.9 1.3 add_convert_fusion
  (18 shorter events, 0.2 us)
Async XLA Ops:
  0.0 8.9 %copy-start = (bf16[512,512]{1,0:T(8,128)(2,1)S(1)}, bf16[512,512]{1,0:T(8,128)(2,1)}, u32[]{:S(2)}) copy-start(bf16[512,512]{1,0:T(8,128)(2,1)} %param.24) | copy-start | bytes 1572868
  0.0 8.1 %copy-start.4 = (bf16[512,512]{1,0:T(8,128)(2,1)S(1)}, bf16[512,512]{1,0:T(8,128)(2,1)}, u32[]{:S(2)}) copy-start(bf16[512,512]{1,0:T(8,128)(2,1)} %param.14) | copy-start | bytes 1572868
  0.0 26.7 %collective-permute-start = (bf16[2048,256]{1,0:T(8,128)(2,1)}, bf16[2048,256]{1,0:T(8,128)(2,1)S(1)}, u32[]{:S(2)}, u32[]{:S(2)}) collective-permute-start(bf16[2048,256]{1,0:T(8,128)(2,1)} %refs_3_.1), channel_id=1, source_target_pairs={{0,1},{1,0},{2,3},{3,2},{4,5},{5,4},{6,7},{7,6},{8,9},{9,8},{10,11... | collective-permute-start | bytes 3145736 | tf_op jit(solution)/shard_map/ppermute | solution.py:380
  3.7 11.6 %collective-permute-start.1 = (bf16[16,256]{1,0:T(8,128)(2,1)S(1)}, bf16[16,256]{1,0:T(8,128)(2,1)S(1)}, u32[]{:S(2)}, u32[]{:S(2)}) collective-permute-start(bf16[16,256]{1,0:T(8,128)(2,1)S(1)} %get-tuple-element.54), channel_id=1, source_target_pairs={{0,2},{2,4},{4,6},{6,8},{8,10},{10,12},{12,14},{14,16},{16,18},{18... | collective-permute-start | bytes 24584 | tf_op jit(solution)/shard_map/ppermute | solution.py:380
  5.2 10.2 %collective-permute-start.2 = (bf16[16,256]{1,0:T(8,128)(2,1)S(1)}, bf16[16,256]{1,0:T(8,128)(2,1)S(1)}, u32[]{:S(2)}, u32[]{:S(2)}) collective-permute-start(bf16[16,256]{1,0:T(8,128)(2,1)S(1)} %get-tuple-element.53), channel_id=1, source_target_pairs={{2,0},{4,2},{6,4},{8,6},{10,8},{12,10},{14,12},{16,14},{18,16},{20... | collective-permute-start | bytes 24584 | tf_op jit(solution)/shard_map/ppermute | solution.py:380
  7.0 1.3 copy-start.12
  7.0 1.3 copy-start.6
  7.0 1.3 copy-start.5
  8.1 0.7 copy-start.8
  8.2 0.7 copy-start.9
  8.3 1.1 copy-start.13
  8.9 1.1 copy-start.7
  11.9 3.9 %copy-start.14 = (f32[8]{0:T(128)S(1)}, f32[8]{0:T(128)}, u32[]{:S(2)}) copy-start(f32[8]{0:T(128)} %param.20) | copy-start | bytes 100
  11.9 4.0 %copy-start.11 = (f32[8]{0:T(128)S(1)}, f32[8]{0:T(128)}, u32[]{:S(2)}) copy-start(f32[8]{0:T(128)} %param.22) | copy-start | bytes 100
  11.9 14.9 %copy-start.2 = (bf16[2048,256]{1,0:T(8,128)(2,1)S(1)}, bf16[2048,256]{1,0:T(8,128)(2,1)}, u32[]{:S(2)}) copy-start(bf16[2048,256]{1,0:T(8,128)(2,1)} %refs_3_.1) | copy-start | bytes 3145732
  15.4 11.3 %collective-permute-start.3 = (bf16[32,256]{1,0:T(8,128)(2,1)S(1)}, bf16[32,256]{1,0:T(8,128)(2,1)S(1)}, u32[]{:S(2)}, u32[]{:S(2)}) collective-permute-start(bf16[32,256]{1,0:T(8,128)(2,1)S(1)} %constant_dynamic-update-slice_fusion.refs_5_), channel_id=1, source_target_pairs={{0,1},{1,0},{2,3},{3,2},{4,5},{5,4},{6,7},{7,6},{8,9},{9,8},{10,11... | collective-permute-start | bytes 49160 | tf_op jit(solution)/shard_map/ppermute | solution.py:380
  55.4 36.4 %copy-start.10 = (f32[512]{0:T(512)S(1)}, f32[512]{0:T(512)}, u32[]{:S(2)}) copy-start(f32[512]{0:T(512)} %param.23) | copy-start | bytes 6148
  90.5 1.3 copy-start.1
  103.3 1.3 copy-start.3
  104.7 4.6 %collective-permute-start.4 = (f32[8,2048]{1,0:T(8,128)S(1)}, f32[8,2048]{1,0:T(8,128)S(1)}, u32[]{:S(2)}, u32[]{:S(2)}) collective-permute-start(f32[8,2048]{1,0:T(8,128)S(1)} %broadcast_select_fusion), channel_id=1, source_target_pairs={{0,1},{1,0},{2,3},{3,2},{4,5},{5,4},{6,7},{7,6},{8,9},{9,8},{10,11... | collective-permute-start | bytes 196616 | tf_op jit(solution)/shard_map/ppermute | solution.py:380
  116.0 24.9 %collective-permute-start.5 = (bf16[2048,256]{1,0:T(8,128)(2,1)S(1)}, bf16[2048,256]{1,0:T(8,128)(2,1)S(1)}, u32[]{:S(2)}, u32[]{:S(2)}) collective-permute-start(bf16[2048,256]{1,0:T(8,128)(2,1)S(1)} %get-tuple-element.52), channel_id=1, source_target_pairs={{0,1},{1,0},{2,3},{3,2},{4,5},{5,4},{6,7},{7,6},{8,9},{9,8},{10,11... | collective-permute-start | bytes 3145736 | tf_op jit(solution)/shard_map/ppermute | solution.py:380

commit v2 on v1

--- a/solution.py
+++ b/solution.py
@@ -182,8 +182,8 @@
     outs[13][...] = dec_r[...]
 
 
-def intra_rows(forward, heads, pieces, sm, x_ref, bc_ref, aux_ref, skip_ref, y_ref, chunk):
-    base = sm[pieces]
+def intra_rows(forward, heads, pieces, sm, x_ref, bc_ref, aux_ref, skip_ref, y_ref, offset, chunk):
+    base = sm[pieces] + offset
     rows = lax.broadcasted_iota(jnp.int32, (SUB, SUB), 0)
     lanes = lax.broadcasted_iota(jnp.int32, (SUB, SUB), 1)
     left = lanes < HEAD_DIM
@@ -230,9 +230,12 @@
 
 
 def exchange_kernel(count, nc, heads, pieces, *refs):
-    sm, st_f, st_r, dec_f, dec_r, x_f, bc_f, aux_f, x_r, bc_r, aux_r, skip = refs[:12]
-    y_f, y_r, into_f, into_r = refs[12:16]
-    sent, landed, held, fade, send_sem, recv_sem = refs[16:]
+    sm, skip = refs[:2]
+    halves = (refs[2:12], refs[12:22])
+    mixed = (refs[22:24], refs[24:26])
+    into_f, into_r = refs[26:28]
+    sent, landed, held, fade, send_sem, recv_sem = refs[28:]
+    (st_f0, st_r0, dec_f0, dec_r0), (st_f1, st_r1, dec_f1, dec_r1) = (h[:4] for h in halves)
     index = lax.axis_index("ctx")
     rounds = rounds_of(count)
     signs = (1, -1)
@@ -259,12 +262,11 @@
     )
     pl.semaphore_wait(barrier, peers)
 
-    held[0], held[1] = st_f[...], st_r[...]
-    fade[0], fade[1] = dec_f[...], dec_r[...]
-    jobs = (
-        (True, x_f, bc_f, aux_f, y_f),
-        (False, x_r, bc_r, aux_r, y_r),
-    )
+    held[0] = st_f0[...] * dec_f1[0:1, :] + st_f1[...]
+    held[1] = st_r1[...] * dec_r0[0:1, :] + st_r0[...]
+    fade[0] = dec_f0[...] * dec_f1[...]
+    fade[1] = dec_r0[...] * dec_r1[...]
+    jobs = (True, False)
     slot = 0
     for number, shifts in enumerate(rounds):
         last = number == len(rounds) - 1
@@ -293,15 +295,19 @@
                     copy.start()
 
         if number < len(jobs):
-            forward, x_ref, bc_ref, aux_ref, y_ref = jobs[number]
-
-            def body(chunk, carry):
-                intra_rows(
-                    forward, heads, pieces, sm, x_ref, bc_ref, aux_ref, skip, y_ref, chunk
-                )
-                return carry
-
-            lax.fori_loop(0, nc, body, 0)
+            forward = jobs[number]
+            for half in (0, 1):
+                x_ref, bc_ref, aux_ref = halves[half][4:7] if forward else halves[half][7:10]
+                y_ref = mixed[half][number]
+
+                def body(chunk, carry):
+                    intra_rows(
+                        forward, heads, pieces, sm, x_ref, bc_ref, aux_ref, skip, y_ref,
+                        half * nc * CHUNK, chunk,
+                    )
+                    return carry
+
+                lax.fori_loop(0, nc, body, 0)
 
         if last:
             held[...] = jnp.zeros_like(held)
@@ -322,8 +328,10 @@
             def _(copy=copy):
                 copy.wait_send()
 
-    into_f[...] = held[0]
-    into_r[...] = held[1]
+    into_f[0] = held[0]
+    into_f[1] = st_f0[...] + dec_f0[0:1, :] * held[0]
+    into_r[0] = st_r1[...] + dec_r1[0:1, :] * held[1]
+    into_r[1] = held[1]
 
 
 def finish_kernel(nc, inner, *refs):
@@ -396,14 +404,27 @@
     inner = heads * HEAD_DIM
     mixing = inner + 2 * NSTATE
     pieces = piece_lengths.shape[0]
-    nc = rows // CHUNK
+    part_rows = rows // 2
+    nc = part_rows // CHUNK
     params = pltpu.CompilerParams(vmem_limit_bytes=VMEM_LIMIT)
 
-    blocks = [hidden] + [shift(hidden, "mp", k, True) for k in range(1, mp)]
+    from_below = shift(hidden[rows - 16 :], "ctx", 1, False)
+    from_above = shift(hidden[:16], "ctx", -1, False)
     halo_own = jnp.concatenate(
-        [shift(hidden[rows - 16 :], "ctx", 1, False), shift(hidden[:16], "ctx", -1, False)], axis=0
+        [
+            from_below,
+            hidden[part_rows : part_rows + 16],
+            hidden[part_rows - 16 : part_rows],
+            from_above,
+        ],
+        axis=0,
     )
     halos = [halo_own] + [shift(halo_own, "mp", k, True) for k in range(1, mp)]
+    lower, upper = hidden[:part_rows], hidden[part_rows:]
+    low_blocks = [shift(lower, "mp", k, True) for k in range(1, mp)]
+    upper, *low_blocks = lax.optimization_barrier((upper, *low_blocks))
+    high_blocks = [shift(upper, "mp", k, True) for k in range(1, mp)]
+    blocks = ([lower] + low_blocks, [upper] + high_blocks)
 
     place = jnp.arange(model, dtype=jnp.int32)
     came = lax.rem(me - place // width + mp, mp) * width + lax.rem(place, width)
@@ -431,7 +452,8 @@
     ).astype(BF16)
 
     bounds = jnp.cumsum(piece_lengths).astype(jnp.int32)
-    sm = jnp.concatenate([bounds, (lax.axis_index("ctx") * rows).astype(jnp.int32)[None]])
+    first_row = (lax.axis_index("ctx") * rows).astype(jnp.int32)[None]
+    sms = [jnp.concatenate([bounds, first_row + half * part_rows]) for half in (0, 1)]
     conv_w = jnp.pad(jnp.concatenate([conv_x, conv_bc], axis=1), ((0, 4), (0, 0)))
     bias = jnp.pad(dt_bias, (0, pad))
     rate = jnp.pad(-LOG2E * decay_rate, (0, pad))
@@ -464,13 +486,13 @@
         return jax.ShapeDtypeStruct(shape, dtype)
 
     stream_shapes = [
-        sds((rows, inner), BF16),
-        sds((rows, 2 * NSTATE), BF16),
-        sds((rows, inner), BF16),
+        sds((part_rows, inner), BF16),
+        sds((part_rows, 2 * NSTATE), BF16),
+        sds((part_rows, inner), BF16),
         sds((nc, 64, SUB), F32),
         sds((2 * nc, NSTATE, inner), BF16),
     ]
-    made = pl.pallas_call(
+    project = pl.pallas_call(
         functools.partial(project_kernel, nc, mp, inner, pieces),
         grid=(nc,),
         in_specs=[smem]
@@ -503,10 +525,17 @@
             pltpu.VMEM((8, inner), F32),
         ],
         compiler_params=params,
-        cost_estimate=cost(4 * rows * model * (mixing + inner), 20 << 20),
+        cost_estimate=cost(4 * part_rows * model * (mixing + inner), 10 << 20),
         name="project",
-    )(sm, *blocks, *blocks, *halos, w_f, w_r, w_dt2, conv_w, head_par, e1, e2)
-    fwd, rev = made[0:5], made[5:10]
+    )
+    made = [
+        project(
+            sms[half], *blocks[half], *blocks[half],
+            *[h[half * 32 : half * 32 + 32] for h in halos],
+            w_f, w_r, w_dt2, conv_w, head_par, e1, e2,
+        )
+        for half in (0, 1)
+    ]
 
     count = lax.axis_size("ctx")
     rounds = rounds_of(count)
@@ -515,9 +544,9 @@
     vmem = pl.BlockSpec(memory_space=pltpu.VMEM)
     *mixed, into_f, into_r = pl.pallas_call(
         functools.partial(exchange_kernel, count, nc, heads, pieces),
-        in_specs=[smem] + [vmem] * 11,
-        out_specs=[vmem] * 4,
-        out_shape=[sds((rows, inner), BF16)] * 2 + [sds((NSTATE, inner), F32)] * 2,
+        in_specs=[smem] + [vmem] * 21,
+        out_specs=[vmem] * 6,
+        out_shape=[sds((part_rows, inner), BF16)] * 4 + [sds((2, NSTATE, inner), F32)] * 2,
         scratch_shapes=[
             pltpu.VMEM((2 * len(rounds), packed, inner), BF16),
             pltpu.VMEM((slots, packed, inner), BF16),
@@ -532,11 +561,16 @@
         cost_estimate=cost(40 * rows * SUB * inner, 16 << 20, 2 * rows * SUB * heads),
         name="exchange",
     )(
-        sm, *made[10:14], fwd[0], fwd[1], fwd[3], rev[0], rev[1], rev[3], skip8,
+        sms[0],
+        skip8,
+        *[
+            value
+            for m in made
+            for value in (*m[10:14], m[0], m[1], m[3], m[5], m[6], m[8])
+        ],
     )
-    into = (into_f, into_r)
-
-    finished = pl.pallas_call(
+
+    finish = pl.pallas_call(
         functools.partial(finish_kernel, nc, inner),
         grid=(nc,),
         in_specs=[up(inner), up(inner), up(2 * NSTATE), aux_up, st_up, whole((NSTATE, inner))]
@@ -548,23 +582,13 @@
             down(inner),
             pl.BlockSpec((8, CHUNK), lambda i: (0, nc - 1 - i)),
         ],
-        out_shape=[sds((rows, inner), BF16), sds((8, rows), F32)] * 2,
+        out_shape=[sds((part_rows, inner), BF16), sds((8, part_rows), F32)] * 2,
         scratch_shapes=[pltpu.VMEM((1, inner), F32)] * 2,
         compiler_params=params,
-        cost_estimate=cost(4 * rows * NSTATE * inner, 24 << 20),
+        cost_estimate=cost(4 * part_rows * NSTATE * inner, 12 << 20),
         name="finish",
-    )(
-        mixed[0], fwd[2], fwd[1], fwd[3], fwd[4], into[0],
-        mixed[1], rev[2], rev[1], rev[3], rev[4], into[1],
-        gain8, e1, e2,
     )
-    upper = jnp.arange(8, dtype=jnp.int32)[:, None] < 4
-    squares = jnp.where(upper, finished[1], finished[3])
-    total = squares
-    for k in range(1, mp):
-        total = total + shift(squares, "mp", k, True)
-
-    parts = pl.pallas_call(
+    output = pl.pallas_call(
         functools.partial(output_kernel, mp, inner * mp),
         grid=(nc,),
         in_specs=[
@@ -575,15 +599,32 @@
             whole((inner, model)),
         ],
         out_specs=[up(width)] * mp,
-        out_shape=[sds((rows, width), F32)] + [sds((rows, width), BF16)] * (mp - 1),
+        out_shape=[sds((part_rows, width), F32)] + [sds((part_rows, width), BF16)] * (mp - 1),
         compiler_params=params,
-        cost_estimate=cost(4 * rows * inner * model, 8 << 20),
+        cost_estimate=cost(4 * part_rows * inner * model, 4 << 20),
         name="output",
-    )(total, finished[0], finished[2], out_f, out_r)
-    result = parts[0]
-    for k in range(1, mp):
-        result = result + shift(parts[k], "mp", k, True).astype(F32)
-    return result.astype(BF16)
+    )
+    forward_rows = jnp.arange(8, dtype=jnp.int32)[:, None] < 4
+    gated, squares = [], []
+    for half, m in enumerate(made):
+        gated_f, square_f, gated_r, square_r = finish(
+            mixed[2 * half], m[2], m[1], m[3], m[4], into_f[half],
+            mixed[2 * half + 1], m[7], m[6], m[8], m[9], into_r[half],
+            gain8, e1, e2,
+        )
+        gated.append((gated_f, gated_r))
+        squares.append(jnp.where(forward_rows, square_f, square_r))
+    other = [[shift(sq, "mp", k, True) for k in range(1, mp)] for sq in squares]
+    totals = [sum(got, sq) for got, sq in zip(other, squares)]
+    first = output(totals[0], *gated[0], out_f, out_r)
+    first, totals[1] = lax.optimization_barrier((first, totals[1]))
+    results = []
+    for parts in (first, output(totals[1], *gated[1], out_f, out_r)):
+        result = parts[0]
+        for k in range(1, mp):
+            result = result + shift(parts[k], "mp", k, True).astype(F32)
+        results.append(result.astype(BF16))
+    return jnp.concatenate(results, axis=0)
 
 
 def solution(mesh):

time: 143 us -> 138 us (0.965)
  waiting for transfers between devices: 36.5 us -> 25 us
  starting transfers between devices: 9.25 us -> 13 us
  local copies, waits for them, and re-layouts: 4.6 us -> 7.31 us
  matrix products: 7.45 us -> 5.33 us
    ppermute x6 -> x9, waiting for transfers between devices: 36.5 us -> 25 us  [shift(): return lax.ppermute(value, axis, pairs)]
    ppermute x6 -> x9, starting transfers between devices: 9.25 us -> 13 us  [shift(): return lax.ppermute(value, axis, pairs)]
    unnamed x33 -> x40, local copies, waits for them, and re-layouts: 3.6 us -> 4.89 us
    pallas_call x3 -> x6, Pallas kernels: 46.8 us -> 46 us  [the longest x2 30.8 us: shards(): project(sms[half], *blocks[half], *blocks[half], *[h[half * 32:half * 32...]
  transfers between devices with their start and end apart: 6 -> 9, of which waited for: 3 -> 4; matrix products, arithmetic and copies ran while one was open for 6% -> 7% of each run, Pallas kernels for 0% -> 14%
where the time goes in v2:
time: 138 us; the launch traced here: 137 us
  Pallas kernels  82.3 us (60%)
  waiting for transfers between devices  25 us (18%)
  starting transfers between devices  13 us (9%)
  local copies, waits for them, and re-layouts  7.31 us (5%)
  matrix products  5.33 us (4%)
  other arithmetic  3.62 us (3%)
    pallas_call x1, Pallas kernels, shards(): pl.pallas_call(functools.partial(exchange_kernel, count, nc, heads, piece...  36.3 us
    pallas_call x2, Pallas kernels, shards(): project(sms[half], *blocks[half], *blocks[half], *[h[half * 32:half * 32...  30.8 us
    ppermute x9, waiting for transfers between devices, shift(): return lax.ppermute(value, axis, pairs)  25 us
    ppermute x9, starting transfers between devices, shift(): return lax.ppermute(value, axis, pairs)  13 us
    pallas_call x2, Pallas kernels, shards(): finish(mixed[2 * half], m[2], m[1], m[3], m[4], into_f[half], mixed[2 * h...  11.3 us
    unnamed x40, local copies, waits for them, and re-layouts  4.89 us
  transfers between devices with their start and end apart: 9, of which 4 were waited for; matrix products, arithmetic and copies ran while one was open for 7% of the time, Pallas kernels for 14%

profile of v2, /device:TPU:0, one launch (start us, length us, event | category | flops | bytes accessed | tf_op | source)
XLA Modules:
  0.0 136.9 jit_solution(6689903395702586955)
XLA Ops:
  0.0 0.0 copy-start
  0.0 0.8 fusion.24
  0.8 2.3 %collective-permute-start.1 = (bf16[16,256]{1,0:T(8,128)(2,1)S(1)}, bf16[16,256]{1,0:T(8,128)(2,1)S(1)}, u32[]{:S(2)}, u32[]{:S(2)}) collective-permute-start(bf16[16,256]{1,0:T(8,128)(2,1)S(1)} %get-tuple-element.109), channel_id=1, source_target_pairs={{0,2},{2,4},{4,6},{6,8},{8,10},{10,12},{12,14},{14,16},{16,18},{18... | collective-permute-start | bytes 24584 | tf_op jit(solution)/shard_map/ppermute | solution.py:388
  3.2 0.0 copy-start.6
  3.2 1.4 %collective-permute-start.2 = (bf16[16,256]{1,0:T(8,128)(2,1)S(1)}, bf16[16,256]{1,0:T(8,128)(2,1)S(1)}, u32[]{:S(2)}, u32[]{:S(2)}) collective-permute-start(bf16[16,256]{1,0:T(8,128)(2,1)S(1)} %get-tuple-element.110), channel_id=1, source_target_pairs={{2,0},{4,2},{6,4},{8,6},{10,8},{12,10},{14,12},{16,14},{18,16},{20... | collective-permute-start | bytes 24584 | tf_op jit(solution)/shard_map/ppermute | solution.py:388
  4.6 1.3 fusion.25
  5.9 0.0 copy-start.8
  5.9 0.0 copy-start.7
  5.9 2.4 %collective-permute-start = (bf16[1024,256]{1,0:T(8,128)(2,1)S(1)}, bf16[1024,256]{1,0:T(8,128)(2,1)S(1)}, u32[]{:S(2)}, u32[]{:S(2)}) collective-permute-start(bf16[1024,256]{1,0:T(8,128)(2,1)S(1)} %get-tuple-element.112.refs_1_.refs_3_), channel_id=1, source_target_pairs={{0,1},{1,0},{2,3},{3,2},{4,5},{5,4},{6,7},{7,6},{8,9},{9,8},{10,11... | collective-permute-start | bytes 1572872 | tf_op jit(solution)/shard_map/ppermute | solution.py:388
  8.3 0.9 iota_compare_fusion.2
  9.3 0.9 iota_compare_fusion.3
  10.2 0.0 copy-done.6
  10.2 0.0 copy-done.8
  10.3 0.0 copy-done.7
  10.3 2.0 %convolution_convert_fusion.refs_8_ = bf16[512,1280]{1,0:T(8,128)(2,1)} fusion(bf16[512,1280]{1,0:T(8,128)(2,1)S(1)} %constant_dynamic-update-slice_fusion, s32[512]{0:T(512)S(1)} %get-tuple-element.130), kind=kOutput, calls=%fused_computation | convolution fusion | flops 672006144 | bytes 2623488 | tf_op jit(solution)/shard_map/dot_general | solution.py:436
  12.3 2.0 %convolution_convert_fusion.1.refs_7_ = bf16[512,1280]{1,0:T(8,128)(2,1)} fusion(bf16[512,1280]{1,0:T(8,128)(2,1)S(1)} %constant_dynamic-update-slice_fusion, s32[512]{0:T(512)S(1)} %get-tuple-element.129), kind=kOutput, calls=%fused_computation.1 | convolution fusion | flops 672006144 | bytes 2623488 | tf_op jit(solution)/shard_map/dot_general | solution.py:435
  14.3 0.0 copy-done.9
  14.4 0.0 copy-start.17
  14.4 0.0 copy-start.18
  14.4 0.0 copy-start.14
  14.4 0.4 fusion.4
  14.8 0.1 copy-done.16
  15.0 0.2 reduce-window.9
  15.1 0.1 pad_add_fusion.7
  15.2 0.0 copy-done.11
  15.2 0.5 fusion.1.wf_ref
  15.8 0.0 copy-done.18
  15.8 0.1 pad_maximum_fusion.6
  15.9 0.1 broadcast_in_dim.48
  15.9 0.1 broadcast_in_dim.49
  16.0 0.0 collective-permute-done.1
  16.0 0.0 collective-permute-done.2
  16.0 0.1 collective-permute-start.3
  16.1 3.0 %collective-permute-done.refs_2_.refs_4_ = bf16[1024,256]{1,0:T(8,128)(2,1)S(1)} collective-permute-done((bf16[1024,256]{1,0:T(8,128)(2,1)S(1)}, bf16[1024,256]{1,0:T(8,128)(2,1)S(1)}, u32[]{:S(2)}, u32[]{:S(2)}) %collective-permute-start) | collective-permute-done | bytes 524320 | tf_op jit(solution)/shard_map/ppermute | solution.py:388
  19.1 2.5 %collective-permute-start.4 = (bf16[1024,256]{1,0:T(8,128)(2,1)S(1)}, bf16[1024,256]{1,0:T(8,128)(2,1)S(1)}, u32[]{:S(2)}, u32[]{:S(2)}) collective-permute-start(bf16[1024,256]{1,0:T(8,128)(2,1)S(1)} %get-tuple-element.67.refs_1_.refs_3_), channel_id=1, source_target_pairs={{0,1},{1,0},{2,3},{3,2},{4,5},{5,4},{6,7},{7,6},{8,9},{9,8},{10,11... | collective-permute-start | bytes 1572872 | tf_op jit(solution)/shard_map/ppermute | solution.py:388
  21.6 0.0 collective-permute-done.3
  21.6 0.1 broadcast_in_dim.51.refs_11_
  21.7 15.4 %project.2 = (bf16[1024,512]{1,0:T(8,128)(2,1)S(1)}, bf16[1024,256]{1,0:T(8,128)(2,1)S(1)}, bf16[1024,512]{1,0:T(8,128)(2,1)S(1)}, f32[4,64,128]{2,1,0:T(8,128)S...) custom-call(s32[5]{0:T(128)S(1)} %get-tuple-element.126.refs_0_, ...), custom_call_target="tpu_custom_call" | custom-call | flops 2684354560 | bytes 10485760 | tf_op jit(solution)/shard_map/project/pallas_call | solution.py:532
  37.1 1.0 copy-done.1
  38.1 1.1 copy-done.4
  39.2 0.0 collective-permute-done.4.refs_2_.refs_4_
  39.2 15.4 %project.3 = (bf16[1024,512]{1,0:T(8,128)(2,1)S(1)}, bf16[1024,256]{1,0:T(8,128)(2,1)S(1)}, bf16[1024,512]{1,0:T(8,128)(2,1)S(1)}, f32[4,64,128]{2,1,0:T(8,128)S...) custom-call(s32[5]{0:T(128)S(1)} %get-tuple-element.125.refs_0_, ...), custom_call_target="tpu_custom_call" | custom-call | flops 2684354560 | bytes 10485760 | tf_op jit(solution)/shard_map/project/pallas_call | solution.py:532
  54.6 1.0 copy-done.2
  55.6 1.0 copy-done.5
  56.6 36.3 %exchange.1 = (bf16[1024,512]{1,0:T(8,128)(2,1)S(1)}, bf16[1024,512]{1,0:T(8,128)(2,1)}, bf16[1024,512]{1,0:T(8,128)(2,1)}, bf16[1024,512]{1,0:T(8,128)(2,1)}, f...) custom-call(s32[5]{0:T(128)S(1)} %get-tuple-element.126.refs_0_, f32[8,512]{1,0:T(8,128)S(1)} %broadcast_in_dim.50.refs_1_, ...), custom_call_target="tpu_custom_call" | custom-call | flops 5368709120 | bytes 16777216 | tf_op jit(solution)/shard_map/exchange/pallas_call | solution.py:545
  92.9 0.0 copy-start.13
  93.0 0.6 copy-done.13
  93.6 5.7 %finish.2 = (bf16[1024,512]{1,0:T(8,128)(2,1)S(1)}, f32[8,1024]{1,0:T(8,128)S(1)}, bf16[1024,512]{1,0:T(8,128)(2,1)S(1)}, f32[8,1024]{1,0:T(8,128)S(1)}) custom-call(bf16[1024,512]{1,0:T(8,128)(2,1)S(1)} %get-tuple-element.78.refs_0_, bf16[1024,512]{1,0:T(8,128)(2,1)S(1)} %get-tuple-element.79.refs_1_, ...), custom_call_target="tpu_custom_call" | custom-call | flops 268435456 | bytes 12582912 | tf_op jit(solution)/shard_map/finish/pallas_call | solution.py:610
  99.3 5.6 %finish.3 = (bf16[1024,512]{1,0:T(8,128)(2,1)S(1)}, f32[8,1024]{1,0:T(8,128)S(1)}, bf16[1024,512]{1,0:T(8,128)(2,1)S(1)}, f32[8,1024]{1,0:T(8,128)S(1)}) custom-call(bf16[1024,512]{1,0:T(8,128)(2,1)S(1)} %copy-done.3, bf16[1024,512]{1,0:T(8,128)(2,1)S(1)} %get-tuple-element.93.refs_1_, bf16[1024,256]{1,0:T(8,128)(2,1)S(1)} %get-tuple-element.73.refs_17_.refs_2_, ...), custom_call_target="tpu_custom_call" | custom-call | flops 268435456 | bytes 12582912 | tf_op jit(solution)/shard_map/finish/pallas_call | solution.py:610
  104.9 0.1 broadcast_select_fusion
  105.0 0.6 collective-permute-start.5
  105.6 0.5 fusion.2.wr_ref
  106.1 1.5 %collective-permute-start.6 = (f32[8,1024]{1,0:T(8,128)S(1)}, f32[8,1024]{1,0:T(8,128)S(1)}, u32[]{:S(2)}, u32[]{:S(2)}) collective-permute-start(f32[8,1024]{1,0:T(8,128)S(1)} %get-tuple-element.123), channel_id=1, source_target_pairs={{0,1},{1,0},{2,3},{3,2},{4,5},{5,4},{6,7},{7,6},{8,9},{9,8},{10,11... | collective-permute-start | bytes 98312 | tf_op jit(solution)/shard_map/ppermute | solution.py:388
  107.6 1.3 collective-permute-done.5
  108.9 1.9 %output.2 = (f32[1024,256]{1,0:T(8,128)S(1)}, bf16[1024,256]{1,0:T(8,128)(2,1)S(1)}) custom-call(f32[8,1024]{1,0:T(8,128)S(1)} %add.82.ss_ref, bf16[1024,512]{1,0:T(8,128)(2,1)S(1)} %get-tuple-element.88.gf_ref, bf16[1024,512]{1,0:T(8,128)(2,1)S(1)} %get-tuple-element.89.gr_ref, bf16[512,512]{1,0:T(8,128)(2,1)S(1)} %fusion.1.wf_ref, ...), custom_call_target="tpu_custom_call" | custom-call | flops 1073741824 | bytes 4194304 | tf_op jit(solution)/shard_map/output/pallas_call | solution.py:619
  110.9 0.0 collective-permute-done.6
  110.9 0.7 collective-permute-start.7
  111.6 1.9 %output.3 = (f32[1024,256]{1,0:T(8,128)S(1)}, bf16[1024,256]{1,0:T(8,128)(2,1)S(1)}) custom-call(f32[8,1024]{1,0:T(8,128)S(1)} %add.85.ss_ref, bf16[1024,512]{1,0:T(8,128)(2,1)S(1)} %get-tuple-element.103.gf_ref, bf16[1024,512]{1,0:T(8,128)(2,1)S(1)} %get-tuple-element.104.gr_ref, bf16[512,512]{1,0:T(8,128)(2,1)S(1)} %fusion.1.wf_ref, ...), custom_call_target="tpu_custom_call" | custom-call | flops 1073741824 | bytes 4194304 | tf_op jit(solution)/shard_map/output/pallas_call | solution.py:622
  113.6 1.4 %collective-permute-start.8 = (bf16[1024,256]{1,0:T(8,128)(2,1)S(1)}, bf16[1024,256]{1,0:T(8,128)(2,1)S(1)}, u32[]{:S(2)}, u32[]{:S(2)}) collective-permute-start(bf16[1024,256]{1,0:T(8,128)(2,1)S(1)} %get-tuple-element.106), channel_id=1, source_target_pairs={{0,1},{1,0},{2,3},{3,2},{4,5},{5,4},{6,7},{7,6},{8,9},{9,8},{10,11... | collective-permute-start | bytes 1572872 | tf_op jit(solution)/shard_map/ppermute | solution.py:388
  115.0 9.5 %collective-permute-done.7 = bf16[1024,256]{1,0:T(8,128)(2,1)S(1)} collective-permute-done((bf16[1024,256]{1,0:T(8,128)(2,1)S(1)}, bf16[1024,256]{1,0:T(8,128)(2,1)S(1)}, u32[]{:S(2)}, u32[]{:S(2)}) %collective-permute-start.7) | collective-permute-done | bytes 524320 | tf_op jit(solution)/shard_map/ppermute | solution.py:388
  124.5 0.1 add_convert_fusion.1
  124.6 11.1 %collective-permute-done.8 = bf16[1024,256]{1,0:T(8,128)(2,1)S(1)} collective-permute-done((bf16[1024,256]{1,0:T(8,128)(2,1)S(1)}, bf16[1024,256]{1,0:T(8,128)(2,1)S(1)}, u32[]{:S(2)}, u32[]{:S(2)}) %collective-permute-start.8) | collective-permute-done | bytes 524320 | tf_op jit(solution)/shard_map/ppermute | solution.py:388
  135.7 0.1 add_convert_fusion
  135.9 1.0 pad_maximum_fusion
  (41 shorter events, 0.3 us)
Async XLA Ops:
  0.0 15.2 %copy-start = (bf16[512,512]{1,0:T(8,128)(2,1)S(1)}, bf16[512,512]{1,0:T(8,128)(2,1)}, u32[]{:S(2)}) copy-start(bf16[512,512]{1,0:T(8,128)(2,1)} %param.24) | copy-start | bytes 1572868
  0.8 15.2 %collective-permute-start.1 = (bf16[16,256]{1,0:T(8,128)(2,1)S(1)}, bf16[16,256]{1,0:T(8,128)(2,1)S(1)}, u32[]{:S(2)}, u32[]{:S(2)}) collective-permute-start(bf16[16,256]{1,0:T(8,128)(2,1)S(1)} %get-tuple-element.109), channel_id=1, source_target_pairs={{0,2},{2,4},{4,6},{6,8},{8,10},{10,12},{12,14},{14,16},{16,18},{18... | collective-permute-start | bytes 24584 | tf_op jit(solution)/shard_map/ppermute | solution.py:388
  3.2 7.0 %copy-start.6 = (bf16[512,512]{1,0:T(8,128)(2,1)S(1)}, bf16[512,512]{1,0:T(8,128)(2,1)}, u32[]{:S(2)}) copy-start(bf16[512,512]{1,0:T(8,128)(2,1)} %param.14) | copy-start | bytes 1572868
  3.2 12.8 %collective-permute-start.2 = (bf16[16,256]{1,0:T(8,128)(2,1)S(1)}, bf16[16,256]{1,0:T(8,128)(2,1)S(1)}, u32[]{:S(2)}, u32[]{:S(2)}) collective-permute-start(bf16[16,256]{1,0:T(8,128)(2,1)S(1)} %get-tuple-element.110), channel_id=1, source_target_pairs={{2,0},{4,2},{6,4},{8,6},{10,8},{12,10},{14,12},{16,14},{18,16},{20... | collective-permute-start | bytes 24584 | tf_op jit(solution)/shard_map/ppermute | solution.py:388
  5.9 4.3 %copy-start.8 = (bf16[512,256]{1,0:T(8,128)(2,1)S(1)}, bf16[512,256]{1,0:T(8,128)(2,1)}, u32[]{:S(2)}) copy-start(bf16[512,256]{1,0:T(8,128)(2,1)} %param.16) | copy-start | bytes 786436
  5.9 4.4 %copy-start.7 = (bf16[512,512]{1,0:T(8,128)(2,1)S(1)}, bf16[512,512]{1,0:T(8,128)(2,1)}, u32[]{:S(2)}) copy-start(bf16[512,512]{1,0:T(8,128)(2,1)} %param.15) | copy-start | bytes 1572868
  5.9 13.2 %collective-permute-start = (bf16[1024,256]{1,0:T(8,128)(2,1)S(1)}, bf16[1024,256]{1,0:T(8,128)(2,1)S(1)}, u32[]{:S(2)}, u32[]{:S(2)}) collective-permute-start(bf16[1024,256]{1,0:T(8,128)(2,1)S(1)} %get-tuple-element.112.refs_1_.refs_3_), channel_id=1, source_target_pairs={{0,1},{1,0},{2,3},{3,2},{4,5},{5,4},{6,7},{7,6},{8,9},{9,8},{10,11... | collective-permute-start | bytes 1572872 | tf_op jit(solution)/shard_map/ppermute | solution.py:388
  12.3 2.1 %copy-start.9 = (pred[512,512]{1,0:T(32,128)(4,1)S(1)}, pred[512,512]{1,0:T(32,128)(4,1)}, u32[]{:S(2)}) copy-start(pred[512,512]{1,0:T(32,128)(4,1)} %iota_compare_fusion.2) | copy-start | bytes 786436
  12.3 2.1 %copy-start.10 = (pred[512,512]{1,0:T(32,128)(4,1)S(1)}, pred[512,512]{1,0:T(32,128)(4,1)}, u32[]{:S(2)}) copy-start(pred[512,512]{1,0:T(32,128)(4,1)} %iota_compare_fusion.3) | copy-start | bytes 786436
  12.3 2.1 %copy-start.15 = (bf16[512,8]{0,1:T(8,128)(2,1)S(1)}, bf16[512,8]{0,1:T(8,128)(2,1)}, u32[]{:S(2)}) copy-start(bf16[512,8]{0,1:T(8,128)(2,1)} %param.17) | copy-start | bytes 24580
  14.3 0.7 copy-start.16
  14.3 0.9 copy-start.11
  14.3 0.9 copy-start.12
  14.4 1.4 copy-start.17
  14.4 1.4 %copy-start.18 = (f32[8]{0:T(128)S(1)}, f32[8]{0:T(128)}, u32[]{:S(2)}) copy-start(f32[8]{0:T(128)} %param.20) | copy-start | bytes 100
  14.4 1.4 %copy-start.14 = (f32[8]{0:T(128)S(1)}, f32[8]{0:T(128)}, u32[]{:S(2)}) copy-start(f32[8]{0:T(128)} %param.22) | copy-start | bytes 100
  16.0 5.6 %collective-permute-start.3 = (bf16[64,256]{1,0:T(8,128)(2,1)S(1)}, bf16[64,256]{1,0:T(8,128)(2,1)S(1)}, u32[]{:S(2)}, u32[]{:S(2)}) collective-permute-start(bf16[64,256]{1,0:T(8,128)(2,1)S(1)} %pad_maximum_fusion.1), channel_id=1, source_target_pairs={{0,1},{1,0},{2,3},{3,2},{4,5},{5,4},{6,7},{7,6},{8,9},{9,8},{10,11... | collective-permute-start | bytes 98312 | tf_op jit(solution)/shard_map/ppermute | solution.py:388
  19.1 20.0 %collective-permute-start.4 = (bf16[1024,256]{1,0:T(8,128)(2,1)S(1)}, bf16[1024,256]{1,0:T(8,128)(2,1)S(1)}, u32[]{:S(2)}, u32[]{:S(2)}) collective-permute-start(bf16[1024,256]{1,0:T(8,128)(2,1)S(1)} %get-tuple-element.67.refs_1_.refs_3_), channel_id=1, source_target_pairs={{0,1},{1,0},{2,3},{3,2},{4,5},{5,4},{6,7},{7,6},{8,9},{9,8},{10,11... | collective-permute-start | bytes 1572872 | tf_op jit(solution)/shard_map/ppermute | solution.py:388
  37.1 1.0 copy-start.1
  38.1 1.1 copy-start.4
  54.6 1.0 copy-start.2
  55.6 1.0 copy-start.5
  92.9 0.7 copy-start.13
  93.6 5.7 %copy-start.3 = (bf16[1024,512]{1,0:T(8,128)(2,1)S(1)}, bf16[1024,512]{1,0:T(8,128)(2,1)}, u32[]{:S(2)}) copy-start(bf16[1024,512]{1,0:T(8,128)(2,1)} %get-tuple-element.92.refs_0_) | copy-start | bytes 3145732
  105.0 3.9 %collective-permute-start.5 = (f32[8,1024]{1,0:T(8,128)S(1)}, f32[8,1024]{1,0:T(8,128)S(1)}, u32[]{:S(2)}, u32[]{:S(2)}) collective-permute-start(f32[8,1024]{1,0:T(8,128)S(1)} %get-tuple-element.124), channel_id=1, source_target_pairs={{0,1},{1,0},{2,3},{3,2},{4,5},{5,4},{6,7},{7,6},{8,9},{9,8},{10,11... | collective-permute-start | bytes 98312 | tf_op jit(solution)/shard_map/ppermute | solution.py:388
  106.1 4.8 %collective-permute-start.6 = (f32[8,1024]{1,0:T(8,128)S(1)}, f32[8,1024]{1,0:T(8,128)S(1)}, u32[]{:S(2)}, u32[]{:S(2)}) collective-permute-start(f32[8,1024]{1,0:T(8,128)S(1)} %get-tuple-element.123), channel_id=1, source_target_pairs={{0,1},{1,0},{2,3},{3,2},{4,5},{5,4},{6,7},{7,6},{8,9},{9,8},{10,11... | collective-permute-start | bytes 98312 | tf_op jit(solution)/shard_map/ppermute | solution.py:388
  110.9 13.6 %collective-permute-start.7 = (bf16[1024,256]{1,0:T(8,128)(2,1)S(1)}, bf16[1024,256]{1,0:T(8,128)(2,1)S(1)}, u32[]{:S(2)}, u32[]{:S(2)}) collective-permute-start(bf16[1024,256]{1,0:T(8,128)(2,1)S(1)} %get-tuple-element.101), channel_id=1, source_target_pairs={{0,1},{1,0},{2,3},{3,2},{4,5},{5,4},{6,7},{7,6},{8,9},{9,8},{10,11... | collective-permute-start | bytes 1572872 | tf_op jit(solution)/shard_map/ppermute | solution.py:388
  113.6 22.2 %collective-permute-start.8 = (bf16[1024,256]{1,0:T(8,128)(2,1)S(1)}, bf16[1024,256]{1,0:T(8,128)(2,1)S(1)}, u32[]{:S(2)}, u32[]{:S(2)}) collective-permute-start(bf16[1024,256]{1,0:T(8,128)(2,1)S(1)} %get-tuple-element.106), channel_id=1, source_target_pairs={{0,1},{1,0},{2,3},{3,2},{4,5},{5,4},{6,7},{7,6},{8,9},{9,8},{10,11... | collective-permute-start | bytes 1572872 | tf_op jit(solution)/shard_map/ppermute | solution.py:388

commit v3 on v2

--- a/solution.py
+++ b/solution.py
@@ -234,81 +234,128 @@
     halves = (refs[2:12], refs[12:22])
     mixed = (refs[22:24], refs[24:26])
     into_f, into_r = refs[26:28]
-    sent, landed, held, fade, send_sem, recv_sem = refs[28:]
+    own, own_fade, held, fade, full = refs[28:33]
+    pair_sent, pair_landed, sent, landed, last_sent, last_landed = refs[33:39]
+    pair_sems, send_sem, recv_sem, last_sems = refs[39:]
     (st_f0, st_r0, dec_f0, dec_r0), (st_f1, st_r1, dec_f1, dec_r1) = (h[:4] for h in halves)
     index = lax.axis_index("ctx")
-    rounds = rounds_of(count)
+    core = lax.rem(index, 2)
+    sibling = {"ctx": index + 1 - 2 * core}
+    rounds = rounds_of(count // 2)
     signs = (1, -1)
+    part = NSTATE // 2
+    mine = pl.ds(pl.multiple_of(core * part, part), part)
+    theirs = pl.ds(pl.multiple_of((1 - core) * part, part), part)
 
     def reaches(step):
         return index + step < count if step > 0 else index + step >= 0
 
-    def peer(step):
-        return {"ctx": index + step}
+    def send(src, dst, send_at, recv_at, target):
+        return pltpu.make_async_remote_copy(
+            src_ref=src,
+            dst_ref=dst,
+            send_sem=send_at,
+            recv_sem=recv_at,
+            device_id=target,
+            device_id_type=pl.DeviceIdType.MESH,
+        )
+
+    def signal(target):
+        pl.semaphore_signal(barrier, inc=1, device_id=target, device_id_type=pl.DeviceIdType.MESH)
+
+    def pack_decay(decay):
+        high = decay.astype(BF16)
+        return jnp.concatenate([high, (decay - high.astype(F32)).astype(BF16)], axis=0)
+
+    def on_first(shape, yes, no):
+        return jnp.where(jnp.full(shape, core, jnp.int32) == 0, yes, no)
+
+    work = [(stream, half) for stream in (0, 1) for half in (0, 1)]
+
+    def compute(pieces_now):
+        for stream, half in pieces_now:
+            x_ref, bc_ref, aux_ref = halves[half][4 + 3 * stream : 7 + 3 * stream]
+            y_ref = mixed[half][stream]
+
+            def body(chunk, carry):
+                intra_rows(
+                    stream == 0, heads, pieces, sm, x_ref, bc_ref, aux_ref, skip, y_ref,
+                    half * nc * CHUNK, chunk,
+                )
+                return carry
+
+            lax.fori_loop(0, nc, body, 0)
 
     barrier = pltpu.get_barrier_semaphore()
-    steps = sorted({sign * s for r in rounds for s in r for sign in signs})
+    steps = sorted({2 * sign * s for r in rounds for s in r for sign in signs})
+    signal(sibling)
     for step in steps:
 
         @pl.when(reaches(step))
         def _(step=step):
-            pl.semaphore_signal(
-                barrier, inc=1, device_id=peer(step), device_id_type=pl.DeviceIdType.MESH
-            )
-
-    peers = sum(
+            signal({"ctx": index + step})
+
+    peers = 1 + sum(
         1 - lax.div(index + step, count) if step > 0 else lax.div(index + step + count, count)
         for step in steps
     )
     pl.semaphore_wait(barrier, peers)
 
-    held[0] = st_f0[...] * dec_f1[0:1, :] + st_f1[...]
-    held[1] = st_r1[...] * dec_r0[0:1, :] + st_r0[...]
-    fade[0] = dec_f0[...] * dec_f1[...]
-    fade[1] = dec_r0[...] * dec_r1[...]
-    jobs = (True, False)
+    own[0] = st_f0[...] * dec_f1[0:1, :] + st_f1[...]
+    own[1] = st_r1[...] * dec_r0[0:1, :] + st_r0[...]
+    own_fade[0] = dec_f0[...] * dec_f1[...]
+    own_fade[1] = dec_r0[...] * dec_r1[...]
+    swaps = []
+    for stream in (0, 1):
+        pair_sent[stream, 0:NSTATE, :] = own[stream].astype(BF16)
+        pair_sent[stream, NSTATE : NSTATE + 16, :] = pack_decay(own_fade[stream])
+        swap = send(
+            pair_sent.at[stream], pair_landed.at[stream],
+            pair_sems.at[stream], pair_sems.at[2 + stream], sibling,
+        )
+        swap.start()
+        swaps.append(swap)
+    compute(work[0:1])
+    for swap in swaps:
+        swap.wait()
+    shape = held.shape[1:]
+    for stream in (0, 1):
+        tail = pair_landed[stream, NSTATE : NSTATE + 16, :].astype(F32)
+        other_fade = tail[0:8] + tail[8:16]
+        other = pair_landed[stream, mine, :].astype(F32)
+        here = own[stream, mine, :]
+        before = other_fade[0:1] * here + other
+        after = own_fade[stream, 0:1, :] * other + here
+        held[stream] = on_first(shape, *((before, after) if stream == 0 else (after, before)))
+        fade[stream] = own_fade[stream] * other_fade
+
     slot = 0
     for number, shifts in enumerate(rounds):
         last = number == len(rounds) - 1
         copies = []
         for stream, sign in enumerate(signs):
             at = number * 2 + stream
-            decay = fade[stream]
-            high = decay.astype(BF16)
-            low = (decay - high.astype(F32)).astype(BF16)
-            sent[at, 0:NSTATE, :] = held[stream].astype(BF16)
-            sent[at, NSTATE : NSTATE + 16, :] = jnp.concatenate([high, low], axis=0)
+            sent[at, 0:part, :] = held[stream].astype(BF16)
+            sent[at, part : part + 16, :] = pack_decay(fade[stream])
             for s in shifts:
-                copy = pltpu.make_async_remote_copy(
-                    src_ref=sent.at[at],
-                    dst_ref=landed.at[slot],
-                    send_sem=send_sem.at[slot],
-                    recv_sem=recv_sem.at[slot],
-                    device_id=peer(sign * s),
-                    device_id_type=pl.DeviceIdType.MESH,
+                step = 2 * sign * s
+                copy = send(
+                    sent.at[at], landed.at[slot],
+                    send_sem.at[slot], recv_sem.at[slot], {"ctx": index + step},
                 )
-                copies.append((stream, sign * s, slot, copy))
+                copies.append((stream, step, slot, copy))
                 slot += 1
 
-                @pl.when(reaches(sign * s))
+                @pl.when(reaches(step))
                 def _(copy=copy):
                     copy.start()
 
-        if number < len(jobs):
-            forward = jobs[number]
-            for half in (0, 1):
-                x_ref, bc_ref, aux_ref = halves[half][4:7] if forward else halves[half][7:10]
-                y_ref = mixed[half][number]
-
-                def body(chunk, carry):
-                    intra_rows(
-                        forward, heads, pieces, sm, x_ref, bc_ref, aux_ref, skip, y_ref,
-                        half * nc * CHUNK, chunk,
-                    )
-                    return carry
-
-                lax.fori_loop(0, nc, body, 0)
-
+        if len(rounds) == 1:
+            compute(work[1:])
+        elif number == 0:
+            compute(work[1:3])
+        elif number == 1:
+            compute(work[3:])
         if last:
             held[...] = jnp.zeros_like(held)
             fade[...] = jnp.ones_like(fade)
@@ -317,8 +364,8 @@
             @pl.when(reaches(-step))
             def _(stream=stream, at=at, copy=copy):
                 copy.wait_recv()
-                more = landed[at, 0:NSTATE, :].astype(F32)
-                tail = landed[at, NSTATE : NSTATE + 16, :].astype(F32)
+                more = landed[at, 0:part, :].astype(F32)
+                tail = landed[at, part : part + 16, :].astype(F32)
                 held[stream] = held[stream] + fade[stream, 0:1, :] * more
                 fade[stream] = fade[stream] * (tail[0:8] + tail[8:16])
 
@@ -328,10 +375,31 @@
             def _(copy=copy):
                 copy.wait_send()
 
-    into_f[0] = held[0]
-    into_f[1] = st_f0[...] + dec_f0[0:1, :] * held[0]
-    into_r[0] = st_r1[...] + dec_r1[0:1, :] * held[1]
-    into_r[1] = held[1]
+    swaps = []
+    for stream in (0, 1):
+        last_sent[stream] = held[stream].astype(BF16)
+        swap = send(
+            last_sent.at[stream], last_landed.at[stream],
+            last_sems.at[stream], last_sems.at[2 + stream], sibling,
+        )
+        swap.start()
+        swaps.append(swap)
+    for stream in (0, 1):
+        swaps[stream].wait()
+        full[stream, mine, :] = held[stream]
+        full[stream, theirs, :] = last_landed[stream].astype(F32)
+        tail = pair_landed[stream, NSTATE : NSTATE + 16, :].astype(F32)
+        outer = full[stream]
+        passed = (tail[0:1] + tail[8:9]) * outer + pair_landed[stream, 0:NSTATE, :].astype(F32)
+        into = on_first(
+            outer.shape, *((outer, passed) if stream == 0 else (passed, outer))
+        )
+        if stream == 0:
+            into_f[0] = into
+            into_f[1] = st_f0[...] + dec_f0[0:1, :] * into
+        else:
+            into_r[0] = st_r1[...] + dec_r1[0:1, :] * into
+            into_r[1] = into
 
 
 def finish_kernel(nc, inner, *refs):
@@ -538,9 +606,9 @@
     ]
 
     count = lax.axis_size("ctx")
-    rounds = rounds_of(count)
+    rounds = rounds_of(count // 2)
     slots = 2 * sum(len(r) for r in rounds)
-    packed = NSTATE + 16
+    packed = NSTATE // 2 + 16
     vmem = pl.BlockSpec(memory_space=pltpu.VMEM)
     *mixed, into_f, into_r = pl.pallas_call(
         functools.partial(exchange_kernel, count, nc, heads, pieces),
@@ -548,12 +616,21 @@
         out_specs=[vmem] * 6,
         out_shape=[sds((part_rows, inner), BF16)] * 4 + [sds((2, NSTATE, inner), F32)] * 2,
         scratch_shapes=[
+            pltpu.VMEM((2, NSTATE, inner), F32),
+            pltpu.VMEM((2, 8, inner), F32),
+            pltpu.VMEM((2, NSTATE // 2, inner), F32),
+            pltpu.VMEM((2, 8, inner), F32),
+            pltpu.VMEM((2, NSTATE, inner), F32),
+            pltpu.VMEM((2, NSTATE + 16, inner), BF16),
+            pltpu.VMEM((2, NSTATE + 16, inner), BF16),
             pltpu.VMEM((2 * len(rounds), packed, inner), BF16),
             pltpu.VMEM((slots, packed, inner), BF16),
-            pltpu.VMEM((2, NSTATE, inner), F32),
-            pltpu.VMEM((2, 8, inner), F32),
+            pltpu.VMEM((2, NSTATE // 2, inner), BF16),
+            pltpu.VMEM((2, NSTATE // 2, inner), BF16),
+            pltpu.SemaphoreType.DMA((4,)),
             pltpu.SemaphoreType.DMA((slots,)),
             pltpu.SemaphoreType.DMA((slots,)),
+            pltpu.SemaphoreType.DMA((4,)),
         ],
         compiler_params=pltpu.CompilerParams(
             vmem_limit_bytes=VMEM_LIMIT, collective_id=0, has_side_effects=True

time: 138 us -> 129 us (0.935)
  Pallas kernels: 82.3 us -> 73.7 us
    pallas_call x1, Pallas kernels: 36.3 us -> 27.6 us  [shards(): pl.pallas_call(functools.partial(exchange_kernel, count, nc, heads, piece...]
  transfers between devices with their start and end apart: 9 -> 9, of which waited for: 4 -> 4; matrix products, arithmetic and copies ran while one was open for 7% -> 7% of each run, Pallas kernels for 14% -> 15%
where the time goes in v3:
time: 129 us; the launch traced here: 128 us
  Pallas kernels  73.7 us (57%)
  waiting for transfers between devices  24.5 us (19%)
  starting transfers between devices  13 us (10%)
  local copies, waits for them, and re-layouts  7.31 us (6%)
  matrix products  5.33 us (4%)
  other arithmetic  3.62 us (3%)
    pallas_call x2, Pallas kernels, shards(): project(sms[half], *blocks[half], *blocks[half], *[h[half * 32:half * 32...  30.8 us
    pallas_call x1, Pallas kernels, shards(): pl.pallas_call(functools.partial(exchange_kernel, count, nc, heads, piece...  27.6 us
    ppermute x9, waiting for transfers between devices, shift(): return lax.ppermute(value, axis, pairs)  24.5 us
    ppermute x9, starting transfers between devices, shift(): return lax.ppermute(value, axis, pairs)  13 us
    pallas_call x2, Pallas kernels, shards(): finish(mixed[2 * half], m[2], m[1], m[3], m[4], into_f[half], mixed[2 * h...  11.3 us
    unnamed x40, local copies, waits for them, and re-layouts  4.89 us
  transfers between devices with their start and end apart: 9, of which 4 were waited for; matrix products, arithmetic and copies ran while one was open for 7% of the time, Pallas kernels for 15%

profile of v3, /device:TPU:0, one launch (start us, length us, event | category | flops | bytes accessed | tf_op | source)
XLA Modules:
  0.0 127.7 jit_solution(9994245863531973492)
XLA Ops:
  0.0 0.0 copy-start
  0.0 0.8 fusion.24
  0.8 2.3 %collective-permute-start.1 = (bf16[16,256]{1,0:T(8,128)(2,1)S(1)}, bf16[16,256]{1,0:T(8,128)(2,1)S(1)}, u32[]{:S(2)}, u32[]{:S(2)}) collective-permute-start(bf16[16,256]{1,0:T(8,128)(2,1)S(1)} %get-tuple-element.109), channel_id=1, source_target_pairs={{0,2},{2,4},{4,6},{6,8},{8,10},{10,12},{12,14},{14,16},{16,18},{18... | collective-permute-start | bytes 24584 | tf_op jit(solution)/shard_map/ppermute | solution.py:456
  3.2 0.0 copy-start.6
  3.2 1.4 %collective-permute-start.2 = (bf16[16,256]{1,0:T(8,128)(2,1)S(1)}, bf16[16,256]{1,0:T(8,128)(2,1)S(1)}, u32[]{:S(2)}, u32[]{:S(2)}) collective-permute-start(bf16[16,256]{1,0:T(8,128)(2,1)S(1)} %get-tuple-element.110), channel_id=1, source_target_pairs={{2,0},{4,2},{6,4},{8,6},{10,8},{12,10},{14,12},{16,14},{18,16},{20... | collective-permute-start | bytes 24584 | tf_op jit(solution)/shard_map/ppermute | solution.py:456
  4.6 1.3 fusion.25
  5.9 0.0 copy-start.8
  5.9 0.0 copy-start.7
  5.9 2.4 %collective-permute-start = (bf16[1024,256]{1,0:T(8,128)(2,1)S(1)}, bf16[1024,256]{1,0:T(8,128)(2,1)S(1)}, u32[]{:S(2)}, u32[]{:S(2)}) collective-permute-start(bf16[1024,256]{1,0:T(8,128)(2,1)S(1)} %get-tuple-element.112.refs_1_.refs_3_), channel_id=1, source_target_pairs={{0,1},{1,0},{2,3},{3,2},{4,5},{5,4},{6,7},{7,6},{8,9},{9,8},{10,11... | collective-permute-start | bytes 1572872 | tf_op jit(solution)/shard_map/ppermute | solution.py:456
  8.3 0.9 iota_compare_fusion.2
  9.3 0.9 iota_compare_fusion.3
  10.2 0.0 copy-done.6
  10.3 2.0 %convolution_convert_fusion.refs_8_ = bf16[512,1280]{1,0:T(8,128)(2,1)} fusion(bf16[512,1280]{1,0:T(8,128)(2,1)S(1)} %constant_dynamic-update-slice_fusion, s32[512]{0:T(512)S(1)} %get-tuple-element.130), kind=kOutput, calls=%fused_computation | convolution fusion | flops 672006144 | bytes 2623488 | tf_op jit(solution)/shard_map/dot_general | solution.py:504
  12.3 2.0 %convolution_convert_fusion.1.refs_7_ = bf16[512,1280]{1,0:T(8,128)(2,1)} fusion(bf16[512,1280]{1,0:T(8,128)(2,1)S(1)} %constant_dynamic-update-slice_fusion, s32[512]{0:T(512)S(1)} %get-tuple-element.129), kind=kOutput, calls=%fused_computation.1 | convolution fusion | flops 672006144 | bytes 2623488 | tf_op jit(solution)/shard_map/dot_general | solution.py:503
  14.3 0.0 copy-done.9
  14.4 0.0 copy-done.10
  14.4 0.0 copy-done.15
  14.4 0.0 copy-start.17
  14.4 0.0 copy-start.18
  14.4 0.0 copy-start.14
  14.4 0.4 fusion.4
  14.8 0.1 copy-done.16
  15.0 0.2 reduce-window.9
  15.1 0.1 pad_add_fusion.7
  15.2 0.0 copy-done.12
  15.2 0.5 fusion.1.wf_ref
  15.8 0.1 pad_maximum_fusion.6
  15.8 0.0 copy-done.14
  15.9 0.1 broadcast_in_dim.48
  15.9 0.1 broadcast_in_dim.49
  16.0 0.0 collective-permute-done.1
  16.0 0.0 collective-permute-done.2
  16.0 0.1 collective-permute-start.3
  16.1 3.0 %collective-permute-done.refs_2_.refs_4_ = bf16[1024,256]{1,0:T(8,128)(2,1)S(1)} collective-permute-done((bf16[1024,256]{1,0:T(8,128)(2,1)S(1)}, bf16[1024,256]{1,0:T(8,128)(2,1)S(1)}, u32[]{:S(2)}, u32[]{:S(2)}) %collective-permute-start) | collective-permute-done | bytes 524320 | tf_op jit(solution)/shard_map/ppermute | solution.py:456
  19.1 2.5 %collective-permute-start.4 = (bf16[1024,256]{1,0:T(8,128)(2,1)S(1)}, bf16[1024,256]{1,0:T(8,128)(2,1)S(1)}, u32[]{:S(2)}, u32[]{:S(2)}) collective-permute-start(bf16[1024,256]{1,0:T(8,128)(2,1)S(1)} %get-tuple-element.67.refs_1_.refs_3_), channel_id=1, source_target_pairs={{0,1},{1,0},{2,3},{3,2},{4,5},{5,4},{6,7},{7,6},{8,9},{9,8},{10,11... | collective-permute-start | bytes 1572872 | tf_op jit(solution)/shard_map/ppermute | solution.py:456
  21.6 0.0 collective-permute-done.3
  21.6 0.1 broadcast_in_dim.51.refs_11_
  21.7 15.4 %project.2 = (bf16[1024,512]{1,0:T(8,128)(2,1)S(1)}, bf16[1024,256]{1,0:T(8,128)(2,1)S(1)}, bf16[1024,512]{1,0:T(8,128)(2,1)S(1)}, f32[4,64,128]{2,1,0:T(8,128)S...) custom-call(s32[5]{0:T(128)S(1)} %get-tuple-element.126.refs_0_, ...), custom_call_target="tpu_custom_call" | custom-call | flops 2684354560 | bytes 10485760 | tf_op jit(solution)/shard_map/project/pallas_call | solution.py:600
  37.1 1.0 copy-done.1
  38.1 1.1 copy-done.4
  39.2 0.0 collective-permute-done.4.refs_2_.refs_4_
  39.2 15.4 %project.3 = (bf16[1024,512]{1,0:T(8,128)(2,1)S(1)}, bf16[1024,256]{1,0:T(8,128)(2,1)S(1)}, bf16[1024,512]{1,0:T(8,128)(2,1)S(1)}, f32[4,64,128]{2,1,0:T(8,128)S...) custom-call(s32[5]{0:T(128)S(1)} %get-tuple-element.125.refs_0_, ...), custom_call_target="tpu_custom_call" | custom-call | flops 2684354560 | bytes 10485760 | tf_op jit(solution)/shard_map/project/pallas_call | solution.py:600
  54.6 1.0 copy-done.2
  55.6 1.0 copy-done.5
  56.6 27.6 %exchange.1 = (bf16[1024,512]{1,0:T(8,128)(2,1)S(1)}, bf16[1024,512]{1,0:T(8,128)(2,1)}, bf16[1024,512]{1,0:T(8,128)(2,1)}, bf16[1024,512]{1,0:T(8,128)(2,1)}, f...) custom-call(s32[5]{0:T(128)S(1)} %get-tuple-element.126.refs_0_, f32[8,512]{1,0:T(8,128)S(1)} %broadcast_in_dim.50.refs_1_, ...), custom_call_target="tpu_custom_call" | custom-call | flops 5368709120 | bytes 16777216 | tf_op jit(solution)/shard_map/exchange/pallas_call | solution.py:613
  84.3 0.0 copy-start.13
  84.4 0.6 copy-done.13
  85.0 5.7 %finish.2 = (bf16[1024,512]{1,0:T(8,128)(2,1)S(1)}, f32[8,1024]{1,0:T(8,128)S(1)}, bf16[1024,512]{1,0:T(8,128)(2,1)S(1)}, f32[8,1024]{1,0:T(8,128)S(1)}) custom-call(bf16[1024,512]{1,0:T(8,128)(2,1)S(1)} %get-tuple-element.78.refs_0_, bf16[1024,512]{1,0:T(8,128)(2,1)S(1)} %get-tuple-element.79.refs_1_, ...), custom_call_target="tpu_custom_call" | custom-call | flops 268435456 | bytes 12582912 | tf_op jit(solution)/shard_map/finish/pallas_call | solution.py:687
  90.6 5.6 %finish.3 = (bf16[1024,512]{1,0:T(8,128)(2,1)S(1)}, f32[8,1024]{1,0:T(8,128)S(1)}, bf16[1024,512]{1,0:T(8,128)(2,1)S(1)}, f32[8,1024]{1,0:T(8,128)S(1)}) custom-call(bf16[1024,512]{1,0:T(8,128)(2,1)S(1)} %copy-done.3, bf16[1024,512]{1,0:T(8,128)(2,1)S(1)} %get-tuple-element.93.refs_1_, bf16[1024,256]{1,0:T(8,128)(2,1)S(1)} %get-tuple-element.73.refs_17_.refs_2_, ...), custom_call_target="tpu_custom_call" | custom-call | flops 268435456 | bytes 12582912 | tf_op jit(solution)/shard_map/finish/pallas_call | solution.py:687
  96.3 0.1 broadcast_select_fusion
  96.3 0.5 collective-permute-start.5
  96.8 0.5 fusion.2.wr_ref
  97.3 1.6 %collective-permute-start.6 = (f32[8,1024]{1,0:T(8,128)S(1)}, f32[8,1024]{1,0:T(8,128)S(1)}, u32[]{:S(2)}, u32[]{:S(2)}) collective-permute-start(f32[8,1024]{1,0:T(8,128)S(1)} %get-tuple-element.123), channel_id=1, source_target_pairs={{0,1},{1,0},{2,3},{3,2},{4,5},{5,4},{6,7},{7,6},{8,9},{9,8},{10,11... | collective-permute-start | bytes 98312 | tf_op jit(solution)/shard_map/ppermute | solution.py:456
  98.9 1.5 %collective-permute-done.5 = f32[8,1024]{1,0:T(8,128)S(1)} collective-permute-done((f32[8,1024]{1,0:T(8,128)S(1)}, f32[8,1024]{1,0:T(8,128)S(1)}, u32[]{:S(2)}, u32[]{:S(2)}) %collective-permute-start.5) | collective-permute-done | bytes 32800 | tf_op jit(solution)/shard_map/ppermute | solution.py:456
  100.5 1.9 %output.2 = (f32[1024,256]{1,0:T(8,128)S(1)}, bf16[1024,256]{1,0:T(8,128)(2,1)S(1)}) custom-call(f32[8,1024]{1,0:T(8,128)S(1)} %add.82.ss_ref, bf16[1024,512]{1,0:T(8,128)(2,1)S(1)} %get-tuple-element.88.gf_ref, bf16[1024,512]{1,0:T(8,128)(2,1)S(1)} %get-tuple-element.89.gr_ref, bf16[512,512]{1,0:T(8,128)(2,1)S(1)} %fusion.1.wf_ref, ...), custom_call_target="tpu_custom_call" | custom-call | flops 1073741824 | bytes 4194304 | tf_op jit(solution)/shard_map/output/pallas_call | solution.py:696
  102.4 0.0 collective-permute-done.6
  102.5 0.4 collective-permute-start.7
  102.9 1.9 %output.3 = (f32[1024,256]{1,0:T(8,128)S(1)}, bf16[1024,256]{1,0:T(8,128)(2,1)S(1)}) custom-call(f32[8,1024]{1,0:T(8,128)S(1)} %add.85.ss_ref, bf16[1024,512]{1,0:T(8,128)(2,1)S(1)} %get-tuple-element.103.gf_ref, bf16[1024,512]{1,0:T(8,128)(2,1)S(1)} %get-tuple-element.104.gr_ref, bf16[512,512]{1,0:T(8,128)(2,1)S(1)} %fusion.1.wf_ref, ...), custom_call_target="tpu_custom_call" | custom-call | flops 1073741824 | bytes 4194304 | tf_op jit(solution)/shard_map/output/pallas_call | solution.py:699
  104.8 1.8 %collective-permute-start.8 = (bf16[1024,256]{1,0:T(8,128)(2,1)S(1)}, bf16[1024,256]{1,0:T(8,128)(2,1)S(1)}, u32[]{:S(2)}, u32[]{:S(2)}) collective-permute-start(bf16[1024,256]{1,0:T(8,128)(2,1)S(1)} %get-tuple-element.106), channel_id=1, source_target_pairs={{0,1},{1,0},{2,3},{3,2},{4,5},{5,4},{6,7},{7,6},{8,9},{9,8},{10,11... | collective-permute-start | bytes 1572872 | tf_op jit(solution)/shard_map/ppermute | solution.py:456
  106.6 10.8 %collective-permute-done.7 = bf16[1024,256]{1,0:T(8,128)(2,1)S(1)} collective-permute-done((bf16[1024,256]{1,0:T(8,128)(2,1)S(1)}, bf16[1024,256]{1,0:T(8,128)(2,1)S(1)}, u32[]{:S(2)}, u32[]{:S(2)}) %collective-permute-start.7) | collective-permute-done | bytes 524320 | tf_op jit(solution)/shard_map/ppermute | solution.py:456
  117.4 0.1 add_convert_fusion.1
  117.5 9.1 %collective-permute-done.8 = bf16[1024,256]{1,0:T(8,128)(2,1)S(1)} collective-permute-done((bf16[1024,256]{1,0:T(8,128)(2,1)S(1)}, bf16[1024,256]{1,0:T(8,128)(2,1)S(1)}, u32[]{:S(2)}, u32[]{:S(2)}) %collective-permute-start.8) | collective-permute-done | bytes 524320 | tf_op jit(solution)/shard_map/ppermute | solution.py:456
  126.6 0.1 add_convert_fusion
  126.7 1.0 pad_maximum_fusion
  (41 shorter events, 0.3 us)
Async XLA Ops:
  0.0 15.2 %copy-start = (bf16[512,512]{1,0:T(8,128)(2,1)S(1)}, bf16[512,512]{1,0:T(8,128)(2,1)}, u32[]{:S(2)}) copy-start(bf16[512,512]{1,0:T(8,128)(2,1)} %param.24) | copy-start | bytes 1572868
  0.8 15.2 %collective-permute-start.1 = (bf16[16,256]{1,0:T(8,128)(2,1)S(1)}, bf16[16,256]{1,0:T(8,128)(2,1)S(1)}, u32[]{:S(2)}, u32[]{:S(2)}) collective-permute-start(bf16[16,256]{1,0:T(8,128)(2,1)S(1)} %get-tuple-element.109), channel_id=1, source_target_pairs={{0,2},{2,4},{4,6},{6,8},{8,10},{10,12},{12,14},{14,16},{16,18},{18... | collective-permute-start | bytes 24584 | tf_op jit(solution)/shard_map/ppermute | solution.py:456
  3.2 7.0 %copy-start.6 = (bf16[512,512]{1,0:T(8,128)(2,1)S(1)}, bf16[512,512]{1,0:T(8,128)(2,1)}, u32[]{:S(2)}) copy-start(bf16[512,512]{1,0:T(8,128)(2,1)} %param.14) | copy-start | bytes 1572868
  3.2 12.8 %collective-permute-start.2 = (bf16[16,256]{1,0:T(8,128)(2,1)S(1)}, bf16[16,256]{1,0:T(8,128)(2,1)S(1)}, u32[]{:S(2)}, u32[]{:S(2)}) collective-permute-start(bf16[16,256]{1,0:T(8,128)(2,1)S(1)} %get-tuple-element.110), channel_id=1, source_target_pairs={{2,0},{4,2},{6,4},{8,6},{10,8},{12,10},{14,12},{16,14},{18,16},{20... | collective-permute-start | bytes 24584 | tf_op jit(solution)/shard_map/ppermute | solution.py:456
  5.9 4.3 %copy-start.8 = (bf16[512,256]{1,0:T(8,128)(2,1)S(1)}, bf16[512,256]{1,0:T(8,128)(2,1)}, u32[]{:S(2)}) copy-start(bf16[512,256]{1,0:T(8,128)(2,1)} %param.16) | copy-start | bytes 786436
  5.9 4.4 %copy-start.7 = (bf16[512,512]{1,0:T(8,128)(2,1)S(1)}, bf16[512,512]{1,0:T(8,128)(2,1)}, u32[]{:S(2)}) copy-start(bf16[512,512]{1,0:T(8,128)(2,1)} %param.15) | copy-start | bytes 1572868
  5.9 13.2 %collective-permute-start = (bf16[1024,256]{1,0:T(8,128)(2,1)S(1)}, bf16[1024,256]{1,0:T(8,128)(2,1)S(1)}, u32[]{:S(2)}, u32[]{:S(2)}) collective-permute-start(bf16[1024,256]{1,0:T(8,128)(2,1)S(1)} %get-tuple-element.112.refs_1_.refs_3_), channel_id=1, source_target_pairs={{0,1},{1,0},{2,3},{3,2},{4,5},{5,4},{6,7},{7,6},{8,9},{9,8},{10,11... | collective-permute-start | bytes 1572872 | tf_op jit(solution)/shard_map/ppermute | solution.py:456
  12.3 2.1 %copy-start.9 = (pred[512,512]{1,0:T(32,128)(4,1)S(1)}, pred[512,512]{1,0:T(32,128)(4,1)}, u32[]{:S(2)}) copy-start(pred[512,512]{1,0:T(32,128)(4,1)} %iota_compare_fusion.2) | copy-start | bytes 786436
  12.3 2.1 %copy-start.10 = (pred[512,512]{1,0:T(32,128)(4,1)S(1)}, pred[512,512]{1,0:T(32,128)(4,1)}, u32[]{:S(2)}) copy-start(pred[512,512]{1,0:T(32,128)(4,1)} %iota_compare_fusion.3) | copy-start | bytes 786436
  12.3 2.1 %copy-start.15 = (bf16[512,8]{0,1:T(8,128)(2,1)S(1)}, bf16[512,8]{0,1:T(8,128)(2,1)}, u32[]{:S(2)}) copy-start(bf16[512,8]{0,1:T(8,128)(2,1)} %param.17) | copy-start | bytes 24580
  14.3 0.7 copy-start.16
  14.3 0.9 copy-start.11
  14.3 0.9 copy-start.12
  14.4 1.4 %copy-start.17 = (f32[8]{0:T(128)S(1)}, f32[8]{0:T(128)}, u32[]{:S(2)}) copy-start(f32[8]{0:T(128)} %param.21) | copy-start | bytes 100
  14.4 1.4 %copy-start.18 = (f32[8]{0:T(128)S(1)}, f32[8]{0:T(128)}, u32[]{:S(2)}) copy-start(f32[8]{0:T(128)} %param.20) | copy-start | bytes 100
  14.4 1.4 %copy-start.14 = (f32[8]{0:T(128)S(1)}, f32[8]{0:T(128)}, u32[]{:S(2)}) copy-start(f32[8]{0:T(128)} %param.22) | copy-start | bytes 100
  16.0 5.6 %collective-permute-start.3 = (bf16[64,256]{1,0:T(8,128)(2,1)S(1)}, bf16[64,256]{1,0:T(8,128)(2,1)S(1)}, u32[]{:S(2)}, u32[]{:S(2)}) collective-permute-start(bf16[64,256]{1,0:T(8,128)(2,1)S(1)} %pad_maximum_fusion.1), channel_id=1, source_target_pairs={{0,1},{1,0},{2,3},{3,2},{4,5},{5,4},{6,7},{7,6},{8,9},{9,8},{10,11... | collective-permute-start | bytes 98312 | tf_op jit(solution)/shard_map/ppermute | solution.py:456
  19.1 20.0 %collective-permute-start.4 = (bf16[1024,256]{1,0:T(8,128)(2,1)S(1)}, bf16[1024,256]{1,0:T(8,128)(2,1)S(1)}, u32[]{:S(2)}, u32[]{:S(2)}) collective-permute-start(bf16[1024,256]{1,0:T(8,128)(2,1)S(1)} %get-tuple-element.67.refs_1_.refs_3_), channel_id=1, source_target_pairs={{0,1},{1,0},{2,3},{3,2},{4,5},{5,4},{6,7},{7,6},{8,9},{9,8},{10,11... | collective-permute-start | bytes 1572872 | tf_op jit(solution)/shard_map/ppermute | solution.py:456
  37.1 1.0 copy-start.1
  38.1 1.1 copy-start.4
  54.6 1.0 copy-start.2
  55.6 1.0 copy-start.5
  84.3 0.7 copy-start.13
  85.0 5.7 %copy-start.3 = (bf16[1024,512]{1,0:T(8,128)(2,1)S(1)}, bf16[1024,512]{1,0:T(8,128)(2,1)}, u32[]{:S(2)}) copy-start(bf16[1024,512]{1,0:T(8,128)(2,1)} %get-tuple-element.92.refs_0_) | copy-start | bytes 3145732
  96.3 4.2 %collective-permute-start.5 = (f32[8,1024]{1,0:T(8,128)S(1)}, f32[8,1024]{1,0:T(8,128)S(1)}, u32[]{:S(2)}, u32[]{:S(2)}) collective-permute-start(f32[8,1024]{1,0:T(8,128)S(1)} %get-tuple-element.124), channel_id=1, source_target_pairs={{0,1},{1,0},{2,3},{3,2},{4,5},{5,4},{6,7},{7,6},{8,9},{9,8},{10,11... | collective-permute-start | bytes 98312 | tf_op jit(solution)/shard_map/ppermute | solution.py:456
  97.3 5.1 %collective-permute-start.6 = (f32[8,1024]{1,0:T(8,128)S(1)}, f32[8,1024]{1,0:T(8,128)S(1)}, u32[]{:S(2)}, u32[]{:S(2)}) collective-permute-start(f32[8,1024]{1,0:T(8,128)S(1)} %get-tuple-element.123), channel_id=1, source_target_pairs={{0,1},{1,0},{2,3},{3,2},{4,5},{5,4},{6,7},{7,6},{8,9},{9,8},{10,11... | collective-permute-start | bytes 98312 | tf_op jit(solution)/shard_map/ppermute | solution.py:456
  102.5 14.9 %collective-permute-start.7 = (bf16[1024,256]{1,0:T(8,128)(2,1)S(1)}, bf16[1024,256]{1,0:T(8,128)(2,1)S(1)}, u32[]{:S(2)}, u32[]{:S(2)}) collective-permute-start(bf16[1024,256]{1,0:T(8,128)(2,1)S(1)} %get-tuple-element.101), channel_id=1, source_target_pairs={{0,1},{1,0},{2,3},{3,2},{4,5},{5,4},{6,7},{7,6},{8,9},{9,8},{10,11... | collective-permute-start | bytes 1572872 | tf_op jit(solution)/shard_map/ppermute | solution.py:456
  104.8 21.8 %collective-permute-start.8 = (bf16[1024,256]{1,0:T(8,128)(2,1)S(1)}, bf16[1024,256]{1,0:T(8,128)(2,1)S(1)}, u32[]{:S(2)}, u32[]{:S(2)}) collective-permute-start(bf16[1024,256]{1,0:T(8,128)(2,1)S(1)} %get-tuple-element.106), channel_id=1, source_target_pairs={{0,1},{1,0},{2,3},{3,2},{4,5},{5,4},{6,7},{7,6},{8,9},{9,8},{10,11... | collective-permute-start | bytes 1572872 | tf_op jit(solution)/shard_map/ppermute | solution.py:456

commit v4 on v3

--- a/solution.py
+++ b/solution.py
@@ -15,7 +15,7 @@
 F32 = jnp.float32
 BF16 = jnp.bfloat16
 BIG = 1 << 30
-VMEM_LIMIT = 48 * 1024 * 1024
+VMEM_LIMIT = 28 * 1024 * 1024
 
 NT = (((1,), (1,)), ((), ()))
 TN = (((0,), (0,)), ((), ()))
@@ -682,21 +682,21 @@
         name="output",
     )
     forward_rows = jnp.arange(8, dtype=jnp.int32)[:, None] < 4
-    gated, squares = [], []
+    results = []
+    mixed_now = mixed[0:2]
     for half, m in enumerate(made):
         gated_f, square_f, gated_r, square_r = finish(
-            mixed[2 * half], m[2], m[1], m[3], m[4], into_f[half],
-            mixed[2 * half + 1], m[7], m[6], m[8], m[9], into_r[half],
+            mixed_now[0], m[2], m[1], m[3], m[4], into_f[half],
+            mixed_now[1], m[7], m[6], m[8], m[9], into_r[half],
             gain8, e1, e2,
         )
-        gated.append((gated_f, gated_r))
-        squares.append(jnp.where(forward_rows, square_f, square_r))
-    other = [[shift(sq, "mp", k, True) for k in range(1, mp)] for sq in squares]
-    totals = [sum(got, sq) for got, sq in zip(other, squares)]
-    first = output(totals[0], *gated[0], out_f, out_r)
-    first, totals[1] = lax.optimization_barrier((first, totals[1]))
-    results = []
-    for parts in (first, output(totals[1], *gated[1], out_f, out_r)):
+        squares = jnp.where(forward_rows, square_f, square_r)
+        total = squares
+        for k in range(1, mp):
+            total = total + shift(squares, "mp", k, True)
+        parts = output(total, gated_f, gated_r, out_f, out_r)
+        if half == 0:
+            parts, mixed_now = lax.optimization_barrier((parts, mixed[2:4]))
         result = parts[0]
         for k in range(1, mp):
             result = result + shift(parts[k], "mp", k, True).astype(F32)

time: 129 us -> 117 us (0.907)
  Pallas kernels: 73.7 us -> 64.3 us
  local copies, waits for them, and re-layouts: 7.31 us -> 5.88 us
    pallas_call x2, Pallas kernels: 30.8 us -> 27.4 us  [shards(): project(sms[half], *blocks[half], *blocks[half], *[h[half * 32:half * 32...]
    pallas_call x1, Pallas kernels: 27.6 us -> 24.5 us  [shards(): pl.pallas_call(functools.partial(exchange_kernel, count, nc, heads, piece...]
    pallas_call x4, Pallas kernels: 15.2 us -> 12.5 us  [the longest x2 8.58 us: shards(): finish(mixed_now[0], m[2], m[1], m[3], m[4], into_f[half], mixed_now[1],...]
    unnamed x40 -> x34, local copies, waits for them, and re-layouts: 4.89 us -> 3.45 us
  transfers between devices with their start and end apart: 9 -> 9, of which waited for: 4 -> 4; matrix products, arithmetic and copies ran while one was open for 7% -> 8% of each run, Pallas kernels for 15% -> 17%
where the time goes in v4:
time: 117 us; the launch traced here: 116 us
  Pallas kernels  64.3 us (55%)
  waiting for transfers between devices  24.8 us (21%)
  starting transfers between devices  12 us (10%)
  local copies, waits for them, and re-layouts  5.88 us (5%)
  matrix products  5.33 us (5%)
  other arithmetic  3.67 us (3%)
    pallas_call x2, Pallas kernels, shards(): project(sms[half], *blocks[half], *blocks[half], *[h[half * 32:half * 32...  27.4 us
    ppermute x9, waiting for transfers between devices, shift(): return lax.ppermute(value, axis, pairs)  24.8 us
    pallas_call x1, Pallas kernels, shards(): pl.pallas_call(functools.partial(exchange_kernel, count, nc, heads, piece...  24.5 us
    ppermute x9, starting transfers between devices, shift(): return lax.ppermute(value, axis, pairs)  12 us
    pallas_call x2, Pallas kernels, shards(): finish(mixed_now[0], m[2], m[1], m[3], m[4], into_f[half], mixed_now[1],...  8.58 us
    pallas_call x2, Pallas kernels, shards(): parts = output(total, gated_f, gated_r, out_f, out_r)  3.89 us
    unnamed x34, local copies, waits for them, and re-layouts  3.45 us
  transfers between devices with their start and end apart: 9, of which 4 were waited for; matrix products, arithmetic and copies ran while one was open for 8% of the time, Pallas kernels for 17%

profile of v4, /device:TPU:0, one launch (start us, length us, event | category | flops | bytes accessed | tf_op | source)
XLA Modules:
  0.0 116.3 jit_solution(56410198402291952)
XLA Ops:
  0.0 0.0 copy-start
  0.0 0.8 fusion.24
  0.8 2.3 %collective-permute-start.1 = (bf16[16,256]{1,0:T(8,128)(2,1)S(1)}, bf16[16,256]{1,0:T(8,128)(2,1)S(1)}, u32[]{:S(2)}, u32[]{:S(2)}) collective-permute-start(bf16[16,256]{1,0:T(8,128)(2,1)S(1)} %get-tuple-element.111), channel_id=1, source_target_pairs={{0,2},{2,4},{4,6},{6,8},{8,10},{10,12},{12,14},{14,16},{16,18},{18... | collective-permute-start | bytes 24584 | tf_op jit(solution)/shard_map/ppermute | solution.py:456
  3.2 0.0 copy-start.3
  3.2 1.4 %collective-permute-start.2 = (bf16[16,256]{1,0:T(8,128)(2,1)S(1)}, bf16[16,256]{1,0:T(8,128)(2,1)S(1)}, u32[]{:S(2)}, u32[]{:S(2)}) collective-permute-start(bf16[16,256]{1,0:T(8,128)(2,1)S(1)} %get-tuple-element.112), channel_id=1, source_target_pairs={{2,0},{4,2},{6,4},{8,6},{10,8},{12,10},{14,12},{16,14},{18,16},{20... | collective-permute-start | bytes 24584 | tf_op jit(solution)/shard_map/ppermute | solution.py:456
  4.6 1.3 %fusion.25 = (bf16[1024,256]{1,0:T(8,128)(2,1)S(1)}, bf16[1024,256]{1,0:T(8,128)(2,1)S(1)}) fusion(bf16[2048,256]{1,0:T(8,128)(2,1)} %param.13), kind=kLoop, calls=%fused_computation.72 | loop fusion | bytes 2097152 | tf_op jit(solution)/shard_map/slice | solution.py:491
  5.9 0.0 copy-start.5
  5.9 0.0 copy-start.4
  5.9 2.4 %collective-permute-start = (bf16[1024,256]{1,0:T(8,128)(2,1)S(1)}, bf16[1024,256]{1,0:T(8,128)(2,1)S(1)}, u32[]{:S(2)}, u32[]{:S(2)}) collective-permute-start(bf16[1024,256]{1,0:T(8,128)(2,1)S(1)} %get-tuple-element.114.refs_1_.refs_3_), channel_id=1, source_target_pairs={{0,1},{1,0},{2,3},{3,2},{4,5},{5,4},{6,7},{7,6},{8,9},{9,8},{10,11... | collective-permute-start | bytes 1572872 | tf_op jit(solution)/shard_map/ppermute | solution.py:456
  8.3 0.9 iota_compare_fusion.2
  9.3 0.9 iota_compare_fusion.3
  10.2 0.0 copy-done.3
  10.2 0.0 copy-done.5
  10.3 2.0 %convolution_convert_fusion.refs_8_ = bf16[512,1280]{1,0:T(8,128)(2,1)} fusion(bf16[512,1280]{1,0:T(8,128)(2,1)S(1)} %constant_dynamic-update-slice_fusion, s32[512]{0:T(512)S(1)} %get-tuple-element.130), kind=kOutput, calls=%fused_computation | convolution fusion | flops 672006144 | bytes 2623488 | tf_op jit(solution)/shard_map/dot_general | solution.py:504
  12.3 2.0 %convolution_convert_fusion.1.refs_7_ = bf16[512,1280]{1,0:T(8,128)(2,1)} fusion(bf16[512,1280]{1,0:T(8,128)(2,1)S(1)} %constant_dynamic-update-slice_fusion, s32[512]{0:T(512)S(1)} %get-tuple-element.129), kind=kOutput, calls=%fused_computation.1 | convolution fusion | flops 672006144 | bytes 2623488 | tf_op jit(solution)/shard_map/dot_general | solution.py:503
  14.3 0.0 copy-done.6
  14.3 0.0 copy-done.7
  14.4 0.0 copy-done.12
  14.4 0.0 copy-start.14
  14.4 0.0 copy-start.15
  14.4 0.0 copy-start.11
  14.4 0.4 fusion.4
  14.8 0.1 copy-done.13
  15.0 0.2 reduce-window.9
  15.1 0.1 pad_add_fusion.7
  15.2 0.0 copy-done.9
  15.2 0.5 fusion.1.wf_ref
  15.8 0.1 pad_maximum_fusion.6
  15.8 0.0 copy-done.11
  15.8 0.1 broadcast_in_dim.48
  15.9 0.1 broadcast_in_dim.49
  16.0 0.0 collective-permute-done.1
  16.0 0.0 collective-permute-done.2
  16.0 0.1 collective-permute-start.3
  16.1 3.0 %collective-permute-done.refs_2_.refs_4_ = bf16[1024,256]{1,0:T(8,128)(2,1)S(1)} collective-permute-done((bf16[1024,256]{1,0:T(8,128)(2,1)S(1)}, bf16[1024,256]{1,0:T(8,128)(2,1)S(1)}, u32[]{:S(2)}, u32[]{:S(2)}) %collective-permute-start) | collective-permute-done | bytes 524320 | tf_op jit(solution)/shard_map/ppermute | solution.py:456
  19.1 2.5 %collective-permute-start.4 = (bf16[1024,256]{1,0:T(8,128)(2,1)S(1)}, bf16[1024,256]{1,0:T(8,128)(2,1)S(1)}, u32[]{:S(2)}, u32[]{:S(2)}) collective-permute-start(bf16[1024,256]{1,0:T(8,128)(2,1)S(1)} %get-tuple-element.68.refs_1_.refs_3_), channel_id=1, source_target_pairs={{0,1},{1,0},{2,3},{3,2},{4,5},{5,4},{6,7},{7,6},{8,9},{9,8},{10,11... | collective-permute-start | bytes 1572872 | tf_op jit(solution)/shard_map/ppermute | solution.py:456
  21.6 0.0 collective-permute-done.3
  21.6 0.1 broadcast_in_dim.51.refs_11_
  21.7 1.3 %copy-done.1 = bf16[512,1280]{1,0:T(8,128)(2,1)S(1)} copy-done((bf16[512,1280]{1,0:T(8,128)(2,1)S(1)}, bf16[512,1280]{1,0:T(8,128)(2,1)}, u32[]{:S(2)}) %copy-start.1) | copy-done | bytes 1310744
  23.0 1.3 %copy-done.2 = bf16[512,1280]{1,0:T(8,128)(2,1)S(1)} copy-done((bf16[512,1280]{1,0:T(8,128)(2,1)S(1)}, bf16[512,1280]{1,0:T(8,128)(2,1)}, u32[]{:S(2)}) %copy-start.2) | copy-done | bytes 1310744
  24.3 13.7 %project.2 = (bf16[1024,512]{1,0:T(8,128)(2,1)S(1)}, bf16[1024,256]{1,0:T(8,128)(2,1)S(1)}, bf16[1024,512]{1,0:T(8,128)(2,1)S(1)}, f32[4,64,128]{2,1,0:T(8,128)S...) custom-call(s32[5]{0:T(128)S(1)} %get-tuple-element.126.refs_0_, ...), custom_call_target="tpu_custom_call" | custom-call | flops 2684354560 | bytes 10485760 | tf_op jit(solution)/shard_map/project/pallas_call | solution.py:600
  38.0 0.0 collective-permute-done.4.refs_2_.refs_4_
  38.0 13.7 %project.3 = (bf16[1024,512]{1,0:T(8,128)(2,1)S(1)}, bf16[1024,256]{1,0:T(8,128)(2,1)S(1)}, bf16[1024,512]{1,0:T(8,128)(2,1)S(1)}, f32[4,64,128]{2,1,0:T(8,128)S...) custom-call(s32[5]{0:T(128)S(1)} %get-tuple-element.125.refs_0_, ...), custom_call_target="tpu_custom_call" | custom-call | flops 2684354560 | bytes 10485760 | tf_op jit(solution)/shard_map/project/pallas_call | solution.py:600
  51.8 24.5 %exchange.1 = (bf16[1024,512]{1,0:T(8,128)(2,1)S(1)}, bf16[1024,512]{1,0:T(8,128)(2,1)S(1)}, bf16[1024,512]{1,0:T(8,128)(2,1)S(1)}, bf16[1024,512]{1,0:T(8,128)(...) custom-call(s32[5]{0:T(128)S(1)} %get-tuple-element.126.refs_0_, ...), custom_call_target="tpu_custom_call" | custom-call | flops 5368709120 | bytes 16777216 | tf_op jit(solution)/shard_map/exchange/pallas_call | solution.py:613
  76.3 0.0 copy-start.10
  76.4 0.6 copy-done.10
  77.0 4.3 %finish.2 = (bf16[1024,512]{1,0:T(8,128)(2,1)S(1)}, f32[8,1024]{1,0:T(8,128)S(1)}, bf16[1024,512]{1,0:T(8,128)(2,1)S(1)}, f32[8,1024]{1,0:T(8,128)S(1)}) custom-call(bf16[1024,512]{1,0:T(8,128)(2,1)S(1)} %get-tuple-element.79.refs_0_, bf16[1024,512]{1,0:T(8,128)(2,1)S(1)} %get-tuple-element.80.refs_1_, ...), custom_call_target="tpu_custom_call" | custom-call | flops 268435456 | bytes 12582912 | tf_op jit(solution)/shard_map/finish/pallas_call | solution.py:688
  81.2 0.1 broadcast_select_fusion.1
  81.3 0.5 collective-permute-start.5
  81.8 0.5 fusion.2.wr_ref
  82.3 2.9 %collective-permute-done.5 = f32[8,1024]{1,0:T(8,128)S(1)} collective-permute-done((f32[8,1024]{1,0:T(8,128)S(1)}, f32[8,1024]{1,0:T(8,128)S(1)}, u32[]{:S(2)}, u32[]{:S(2)}) %collective-permute-start.5) | collective-permute-done | bytes 32800 | tf_op jit(solution)/shard_map/ppermute | solution.py:456
  85.2 1.9 %output.2 = (f32[1024,256]{1,0:T(8,128)S(1)}, bf16[1024,256]{1,0:T(8,128)(2,1)S(1)}) custom-call(f32[8,1024]{1,0:T(8,128)S(1)} %add.82.ss_ref, bf16[1024,512]{1,0:T(8,128)(2,1)S(1)} %get-tuple-element.89.gf_ref, bf16[1024,512]{1,0:T(8,128)(2,1)S(1)} %get-tuple-element.90.gr_ref, bf16[512,512]{1,0:T(8,128)(2,1)S(1)} %fusion.1.wf_ref, ...), custom_call_target="tpu_custom_call" | custom-call | flops 1073741824 | bytes 4194304 | tf_op jit(solution)/shard_map/output/pallas_call | solution.py:697
  87.2 0.6 collective-permute-start.6
  87.8 4.3 %finish.3 = (bf16[1024,512]{1,0:T(8,128)(2,1)S(1)}, f32[8,1024]{1,0:T(8,128)S(1)}, bf16[1024,512]{1,0:T(8,128)(2,1)S(1)}, f32[8,1024]{1,0:T(8,128)S(1)}) custom-call(bf16[1024,512]{1,0:T(8,128)(2,1)S(1)} %get-tuple-element.97.refs_0_, bf16[1024,512]{1,0:T(8,128)(2,1)S(1)} %get-tuple-element.98.refs_1_, ...), custom_call_target="tpu_custom_call" | custom-call | flops 268435456 | bytes 12582912 | tf_op jit(solution)/shard_map/finish/pallas_call | solution.py:688
  92.1 0.1 broadcast_select_fusion
  92.1 1.5 %collective-permute-start.7 = (f32[8,1024]{1,0:T(8,128)S(1)}, f32[8,1024]{1,0:T(8,128)S(1)}, u32[]{:S(2)}, u32[]{:S(2)}) collective-permute-start(f32[8,1024]{1,0:T(8,128)S(1)} %broadcast_select_fusion), channel_id=1, source_target_pairs={{0,1},{1,0},{2,3},{3,2},{4,5},{5,4},{6,7},{7,6},{8,9},{9,8},{10,11... | collective-permute-start | bytes 98312 | tf_op jit(solution)/shard_map/ppermute | solution.py:456
  93.7 7.3 %collective-permute-done.7 = f32[8,1024]{1,0:T(8,128)S(1)} collective-permute-done((f32[8,1024]{1,0:T(8,128)S(1)}, f32[8,1024]{1,0:T(8,128)S(1)}, u32[]{:S(2)}, u32[]{:S(2)}) %collective-permute-start.7) | collective-permute-done | bytes 32800 | tf_op jit(solution)/shard_map/ppermute | solution.py:456
  101.0 1.9 %output.3 = (f32[1024,256]{1,0:T(8,128)S(1)}, bf16[1024,256]{1,0:T(8,128)(2,1)S(1)}) custom-call(f32[8,1024]{1,0:T(8,128)S(1)} %add.86.ss_ref, bf16[1024,512]{1,0:T(8,128)(2,1)S(1)} %get-tuple-element.105.gf_ref, bf16[1024,512]{1,0:T(8,128)(2,1)S(1)} %get-tuple-element.106.gr_ref, bf16[512,512]{1,0:T(8,128)(2,1)S(1)} %fusion.1.wf_ref, ...), custom_call_target="tpu_custom_call" | custom-call | flops 1073741824 | bytes 4194304 | tf_op jit(solution)/shard_map/output/pallas_call | solution.py:697
  103.0 0.6 collective-permute-start.8
  103.5 0.0 collective-permute-done.6
  103.5 0.1 add_convert_fusion.1
  103.7 11.5 %collective-permute-done.8 = bf16[1024,256]{1,0:T(8,128)(2,1)S(1)} collective-permute-done((bf16[1024,256]{1,0:T(8,128)(2,1)S(1)}, bf16[1024,256]{1,0:T(8,128)(2,1)S(1)}, u32[]{:S(2)}, u32[]{:S(2)}) %collective-permute-start.8) | collective-permute-done | bytes 524320 | tf_op jit(solution)/shard_map/ppermute | solution.py:456
  115.1 0.1 add_convert_fusion
  115.3 1.0 pad_maximum_fusion
  (36 shorter events, 0.3 us)
Async XLA Ops:
  0.0 15.2 %copy-start = (bf16[512,512]{1,0:T(8,128)(2,1)S(1)}, bf16[512,512]{1,0:T(8,128)(2,1)}, u32[]{:S(2)}) copy-start(bf16[512,512]{1,0:T(8,128)(2,1)} %param.24) | copy-start | bytes 1572868
  0.8 15.2 %collective-permute-start.1 = (bf16[16,256]{1,0:T(8,128)(2,1)S(1)}, bf16[16,256]{1,0:T(8,128)(2,1)S(1)}, u32[]{:S(2)}, u32[]{:S(2)}) collective-permute-start(bf16[16,256]{1,0:T(8,128)(2,1)S(1)} %get-tuple-element.111), channel_id=1, source_target_pairs={{0,2},{2,4},{4,6},{6,8},{8,10},{10,12},{12,14},{14,16},{16,18},{18... | collective-permute-start | bytes 24584 | tf_op jit(solution)/shard_map/ppermute | solution.py:456
  3.2 7.0 %copy-start.3 = (bf16[512,512]{1,0:T(8,128)(2,1)S(1)}, bf16[512,512]{1,0:T(8,128)(2,1)}, u32[]{:S(2)}) copy-start(bf16[512,512]{1,0:T(8,128)(2,1)} %param.14) | copy-start | bytes 1572868
  3.2 12.8 %collective-permute-start.2 = (bf16[16,256]{1,0:T(8,128)(2,1)S(1)}, bf16[16,256]{1,0:T(8,128)(2,1)S(1)}, u32[]{:S(2)}, u32[]{:S(2)}) collective-permute-start(bf16[16,256]{1,0:T(8,128)(2,1)S(1)} %get-tuple-element.112), channel_id=1, source_target_pairs={{2,0},{4,2},{6,4},{8,6},{10,8},{12,10},{14,12},{16,14},{18,16},{20... | collective-permute-start | bytes 24584 | tf_op jit(solution)/shard_map/ppermute | solution.py:456
  5.9 4.3 %copy-start.5 = (bf16[512,256]{1,0:T(8,128)(2,1)S(1)}, bf16[512,256]{1,0:T(8,128)(2,1)}, u32[]{:S(2)}) copy-start(bf16[512,256]{1,0:T(8,128)(2,1)} %param.16) | copy-start | bytes 786436
  5.9 4.4 %copy-start.4 = (bf16[512,512]{1,0:T(8,128)(2,1)S(1)}, bf16[512,512]{1,0:T(8,128)(2,1)}, u32[]{:S(2)}) copy-start(bf16[512,512]{1,0:T(8,128)(2,1)} %param.15) | copy-start | bytes 1572868
  5.9 13.2 %collective-permute-start = (bf16[1024,256]{1,0:T(8,128)(2,1)S(1)}, bf16[1024,256]{1,0:T(8,128)(2,1)S(1)}, u32[]{:S(2)}, u32[]{:S(2)}) collective-permute-start(bf16[1024,256]{1,0:T(8,128)(2,1)S(1)} %get-tuple-element.114.refs_1_.refs_3_), channel_id=1, source_target_pairs={{0,1},{1,0},{2,3},{3,2},{4,5},{5,4},{6,7},{7,6},{8,9},{9,8},{10,11... | collective-permute-start | bytes 1572872 | tf_op jit(solution)/shard_map/ppermute | solution.py:456
  12.3 2.0 %copy-start.6 = (pred[512,512]{1,0:T(32,128)(4,1)S(1)}, pred[512,512]{1,0:T(32,128)(4,1)}, u32[]{:S(2)}) copy-start(pred[512,512]{1,0:T(32,128)(4,1)} %iota_compare_fusion.2) | copy-start | bytes 786436
  12.3 2.1 %copy-start.7 = (pred[512,512]{1,0:T(32,128)(4,1)S(1)}, pred[512,512]{1,0:T(32,128)(4,1)}, u32[]{:S(2)}) copy-start(pred[512,512]{1,0:T(32,128)(4,1)} %iota_compare_fusion.3) | copy-start | bytes 786436
  12.3 2.1 %copy-start.12 = (bf16[512,8]{0,1:T(8,128)(2,1)S(1)}, bf16[512,8]{0,1:T(8,128)(2,1)}, u32[]{:S(2)}) copy-start(bf16[512,8]{0,1:T(8,128)(2,1)} %param.17) | copy-start | bytes 24580
  14.3 0.7 copy-start.13
  14.3 0.9 copy-start.8
  14.3 0.9 copy-start.9
  14.4 1.4 %copy-start.14 = (f32[8]{0:T(128)S(1)}, f32[8]{0:T(128)}, u32[]{:S(2)}) copy-start(f32[8]{0:T(128)} %param.21) | copy-start | bytes 100
  14.4 1.4 %copy-start.15 = (f32[8]{0:T(128)S(1)}, f32[8]{0:T(128)}, u32[]{:S(2)}) copy-start(f32[8]{0:T(128)} %param.20) | copy-start | bytes 100
  14.4 1.4 %copy-start.11 = (f32[8]{0:T(128)S(1)}, f32[8]{0:T(128)}, u32[]{:S(2)}) copy-start(f32[8]{0:T(128)} %param.22) | copy-start | bytes 100
  16.0 5.6 %collective-permute-start.3 = (bf16[64,256]{1,0:T(8,128)(2,1)S(1)}, bf16[64,256]{1,0:T(8,128)(2,1)S(1)}, u32[]{:S(2)}, u32[]{:S(2)}) collective-permute-start(bf16[64,256]{1,0:T(8,128)(2,1)S(1)} %pad_maximum_fusion.1), channel_id=1, source_target_pairs={{0,1},{1,0},{2,3},{3,2},{4,5},{5,4},{6,7},{7,6},{8,9},{9,8},{10,11... | collective-permute-start | bytes 98312 | tf_op jit(solution)/shard_map/ppermute | solution.py:456
  19.1 18.9 %collective-permute-start.4 = (bf16[1024,256]{1,0:T(8,128)(2,1)S(1)}, bf16[1024,256]{1,0:T(8,128)(2,1)S(1)}, u32[]{:S(2)}, u32[]{:S(2)}) collective-permute-start(bf16[1024,256]{1,0:T(8,128)(2,1)S(1)} %get-tuple-element.68.refs_1_.refs_3_), channel_id=1, source_target_pairs={{0,1},{1,0},{2,3},{3,2},{4,5},{5,4},{6,7},{7,6},{8,9},{9,8},{10,11... | collective-permute-start | bytes 1572872 | tf_op jit(solution)/shard_map/ppermute | solution.py:456
  21.7 1.3 %copy-start.1 = (bf16[512,1280]{1,0:T(8,128)(2,1)S(1)}, bf16[512,1280]{1,0:T(8,128)(2,1)}, u32[]{:S(2)}) copy-start(bf16[512,1280]{1,0:T(8,128)(2,1)} %convolution_convert_fusion.refs_8_) | copy-start | bytes 3932164
  23.0 1.3 %copy-start.2 = (bf16[512,1280]{1,0:T(8,128)(2,1)S(1)}, bf16[512,1280]{1,0:T(8,128)(2,1)}, u32[]{:S(2)}) copy-start(bf16[512,1280]{1,0:T(8,128)(2,1)} %convolution_convert_fusion.1.refs_7_) | copy-start | bytes 3932164
  76.3 0.7 copy-start.10
  81.3 3.9 %collective-permute-start.5 = (f32[8,1024]{1,0:T(8,128)S(1)}, f32[8,1024]{1,0:T(8,128)S(1)}, u32[]{:S(2)}, u32[]{:S(2)}) collective-permute-start(f32[8,1024]{1,0:T(8,128)S(1)} %broadcast_select_fusion.1), channel_id=1, source_target_pairs={{0,1},{1,0},{2,3},{3,2},{4,5},{5,4},{6,7},{7,6},{8,9},{9,8},{10,11... | collective-permute-start | bytes 98312 | tf_op jit(solution)/shard_map/ppermute | solution.py:456
  87.2 16.3 %collective-permute-start.6 = (bf16[1024,256]{1,0:T(8,128)(2,1)S(1)}, bf16[1024,256]{1,0:T(8,128)(2,1)S(1)}, u32[]{:S(2)}, u32[]{:S(2)}) collective-permute-start(bf16[1024,256]{1,0:T(8,128)(2,1)S(1)} %get-tuple-element.96), channel_id=1, source_target_pairs={{0,1},{1,0},{2,3},{3,2},{4,5},{5,4},{6,7},{7,6},{8,9},{9,8},{10,11... | collective-permute-start | bytes 1572872 | tf_op jit(solution)/shard_map/ppermute | solution.py:456
  92.1 8.9 %collective-permute-start.7 = (f32[8,1024]{1,0:T(8,128)S(1)}, f32[8,1024]{1,0:T(8,128)S(1)}, u32[]{:S(2)}, u32[]{:S(2)}) collective-permute-start(f32[8,1024]{1,0:T(8,128)S(1)} %broadcast_select_fusion), channel_id=1, source_target_pairs={{0,1},{1,0},{2,3},{3,2},{4,5},{5,4},{6,7},{7,6},{8,9},{9,8},{10,11... | collective-permute-start | bytes 98312 | tf_op jit(solution)/shard_map/ppermute | solution.py:456
  103.0 12.2 %collective-permute-start.8 = (bf16[1024,256]{1,0:T(8,128)(2,1)S(1)}, bf16[1024,256]{1,0:T(8,128)(2,1)S(1)}, u32[]{:S(2)}, u32[]{:S(2)}) collective-permute-start(bf16[1024,256]{1,0:T(8,128)(2,1)S(1)} %get-tuple-element.108), channel_id=1, source_target_pairs={{0,1},{1,0},{2,3},{3,2},{4,5},{5,4},{6,7},{7,6},{8,9},{9,8},{10,11... | collective-permute-start | bytes 1572872 | tf_op jit(solution)/shard_map/ppermute | solution.py:456

commit v5 on v3

--- a/solution.py
+++ b/solution.py
@@ -15,7 +15,7 @@
 F32 = jnp.float32
 BF16 = jnp.bfloat16
 BIG = 1 << 30
-VMEM_LIMIT = 48 * 1024 * 1024
+VMEM_LIMIT = 28 * 1024 * 1024
 
 NT = (((1,), (1,)), ((), ()))
 TN = (((0,), (0,)), ((), ()))
@@ -683,14 +683,18 @@
     )
     forward_rows = jnp.arange(8, dtype=jnp.int32)[:, None] < 4
     gated, squares = [], []
+    mixed_now = mixed[0:2]
     for half, m in enumerate(made):
         gated_f, square_f, gated_r, square_r = finish(
-            mixed[2 * half], m[2], m[1], m[3], m[4], into_f[half],
-            mixed[2 * half + 1], m[7], m[6], m[8], m[9], into_r[half],
+            mixed_now[0], m[2], m[1], m[3], m[4], into_f[half],
+            mixed_now[1], m[7], m[6], m[8], m[9], into_r[half],
             gain8, e1, e2,
         )
         gated.append((gated_f, gated_r))
-        squares.append(jnp.where(forward_rows, square_f, square_r))
+        square = jnp.where(forward_rows, square_f, square_r)
+        if half == 0:
+            square, mixed_now = lax.optimization_barrier((square, mixed[2:4]))
+        squares.append(square)
     other = [[shift(sq, "mp", k, True) for k in range(1, mp)] for sq in squares]
     totals = [sum(got, sq) for got, sq in zip(other, squares)]
     first = output(totals[0], *gated[0], out_f, out_r)

time: 129 us -> 117 us (0.907)
  Pallas kernels: 73.7 us -> 64.4 us
  local copies, waits for them, and re-layouts: 7.31 us -> 5.77 us
    pallas_call x2, Pallas kernels: 30.8 us -> 27.4 us  [shards(): project(sms[half], *blocks[half], *blocks[half], *[h[half * 32:half * 32...]
    pallas_call x1, Pallas kernels: 27.6 us -> 24.5 us  [shards(): pl.pallas_call(functools.partial(exchange_kernel, count, nc, heads, piece...]
    pallas_call x2, Pallas kernels: 11.3 us -> 8.58 us  [shards(): finish(mixed_now[0], m[2], m[1], m[3], m[4], into_f[half], mixed_now[1],...]
    unnamed x40 -> x34, local copies, waits for them, and re-layouts: 4.89 us -> 3.35 us
  transfers between devices with their start and end apart: 9 -> 9, of which waited for: 4 -> 4; matrix products, arithmetic and copies ran while one was open for 7% -> 8% of each run, Pallas kernels for 15% -> 19%
where the time goes in v5:
time: 117 us; the launch traced here: 116 us
  Pallas kernels  64.4 us (55%)
  waiting for transfers between devices  23.4 us (20%)
  starting transfers between devices  12.9 us (11%)
  local copies, waits for them, and re-layouts  5.77 us (5%)
  matrix products  5.34 us (5%)
  other arithmetic  3.67 us (3%)
    pallas_call x2, Pallas kernels, shards(): project(sms[half], *blocks[half], *blocks[half], *[h[half * 32:half * 32...  27.4 us
    pallas_call x1, Pallas kernels, shards(): pl.pallas_call(functools.partial(exchange_kernel, count, nc, heads, piece...  24.5 us
    ppermute x9, waiting for transfers between devices, shift(): return lax.ppermute(value, axis, pairs)  23.4 us
    ppermute x9, starting transfers between devices, shift(): return lax.ppermute(value, axis, pairs)  12.9 us
    pallas_call x2, Pallas kernels, shards(): finish(mixed_now[0], m[2], m[1], m[3], m[4], into_f[half], mixed_now[1],...  8.58 us
    unnamed x34, local copies, waits for them, and re-layouts  3.35 us
  transfers between devices with their start and end apart: 9, of which 4 were waited for; matrix products, arithmetic and copies ran while one was open for 8% of the time, Pallas kernels for 19%

profile of v5, /device:TPU:0, one launch (start us, length us, event | category | flops | bytes accessed | tf_op | source)
XLA Modules:
  0.0 115.8 jit_solution(7367082352894658594)
XLA Ops:
  0.0 0.0 copy-start
  0.0 0.8 fusion.24
  0.8 2.3 %collective-permute-start.1 = (bf16[16,256]{1,0:T(8,128)(2,1)S(1)}, bf16[16,256]{1,0:T(8,128)(2,1)S(1)}, u32[]{:S(2)}, u32[]{:S(2)}) collective-permute-start(bf16[16,256]{1,0:T(8,128)(2,1)S(1)} %get-tuple-element.115), channel_id=1, source_target_pairs={{0,2},{2,4},{4,6},{6,8},{8,10},{10,12},{12,14},{14,16},{16,18},{18... | collective-permute-start | bytes 24584 | tf_op jit(solution)/shard_map/ppermute | solution.py:456
  3.2 0.0 copy-start.3
  3.2 1.4 %collective-permute-start.2 = (bf16[16,256]{1,0:T(8,128)(2,1)S(1)}, bf16[16,256]{1,0:T(8,128)(2,1)S(1)}, u32[]{:S(2)}, u32[]{:S(2)}) collective-permute-start(bf16[16,256]{1,0:T(8,128)(2,1)S(1)} %get-tuple-element.116), channel_id=1, source_target_pairs={{2,0},{4,2},{6,4},{8,6},{10,8},{12,10},{14,12},{16,14},{18,16},{20... | collective-permute-start | bytes 24584 | tf_op jit(solution)/shard_map/ppermute | solution.py:456
  4.6 1.3 %fusion.25 = (bf16[1024,256]{1,0:T(8,128)(2,1)S(1)}, bf16[1024,256]{1,0:T(8,128)(2,1)S(1)}) fusion(bf16[2048,256]{1,0:T(8,128)(2,1)} %param.13), kind=kLoop, calls=%fused_computation.72 | loop fusion | bytes 2097152 | tf_op jit(solution)/shard_map/slice | solution.py:491
  5.9 0.0 copy-start.5
  5.9 0.0 copy-start.4
  5.9 2.4 %collective-permute-start = (bf16[1024,256]{1,0:T(8,128)(2,1)S(1)}, bf16[1024,256]{1,0:T(8,128)(2,1)S(1)}, u32[]{:S(2)}, u32[]{:S(2)}) collective-permute-start(bf16[1024,256]{1,0:T(8,128)(2,1)S(1)} %get-tuple-element.118.refs_1_.refs_3_), channel_id=1, source_target_pairs={{0,1},{1,0},{2,3},{3,2},{4,5},{5,4},{6,7},{7,6},{8,9},{9,8},{10,11... | collective-permute-start | bytes 1572872 | tf_op jit(solution)/shard_map/ppermute | solution.py:456
  8.3 0.9 iota_compare_fusion.2
  9.3 0.9 iota_compare_fusion.3
  10.2 0.0 copy-done.3
  10.2 0.0 copy-done.5
  10.3 2.0 %convolution_convert_fusion.refs_8_ = bf16[512,1280]{1,0:T(8,128)(2,1)} fusion(bf16[512,1280]{1,0:T(8,128)(2,1)S(1)} %constant_dynamic-update-slice_fusion, s32[512]{0:T(512)S(1)} %get-tuple-element.134), kind=kOutput, calls=%fused_computation | convolution fusion | flops 672006144 | bytes 2623488 | tf_op jit(solution)/shard_map/dot_general | solution.py:504
  12.3 2.0 %convolution_convert_fusion.1.refs_7_ = bf16[512,1280]{1,0:T(8,128)(2,1)} fusion(bf16[512,1280]{1,0:T(8,128)(2,1)S(1)} %constant_dynamic-update-slice_fusion, s32[512]{0:T(512)S(1)} %get-tuple-element.133), kind=kOutput, calls=%fused_computation.1 | convolution fusion | flops 672006144 | bytes 2623488 | tf_op jit(solution)/shard_map/dot_general | solution.py:503
  14.3 0.4 fusion.4
  14.8 0.0 copy-done
  14.8 0.0 copy-start.13
  14.8 0.0 copy-start.8
  14.8 0.0 copy-start.9
  14.8 0.0 copy-start.14
  14.8 0.0 copy-start.15
  14.8 0.0 copy-start.11
  14.8 0.5 fusion.1.wf_ref
  15.3 0.5 fusion.2.wr_ref
  15.9 0.2 reduce-window.9
  16.0 0.1 pad_add_fusion.7
  16.1 0.0 copy-done.8
  16.2 0.1 pad_maximum_fusion.6
  16.2 0.0 copy-done.11
  16.2 0.1 broadcast_in_dim.48
  16.3 0.1 broadcast_in_dim.49
  16.4 0.0 collective-permute-done.1
  16.4 0.0 collective-permute-done.2
  16.4 0.1 collective-permute-start.3
  16.5 2.6 %collective-permute-done.refs_2_.refs_4_ = bf16[1024,256]{1,0:T(8,128)(2,1)S(1)} collective-permute-done((bf16[1024,256]{1,0:T(8,128)(2,1)S(1)}, bf16[1024,256]{1,0:T(8,128)(2,1)S(1)}, u32[]{:S(2)}, u32[]{:S(2)}) %collective-permute-start) | collective-permute-done | bytes 524320 | tf_op jit(solution)/shard_map/ppermute | solution.py:456
  19.1 2.5 %collective-permute-start.4 = (bf16[1024,256]{1,0:T(8,128)(2,1)S(1)}, bf16[1024,256]{1,0:T(8,128)(2,1)S(1)}, u32[]{:S(2)}, u32[]{:S(2)}) collective-permute-start(bf16[1024,256]{1,0:T(8,128)(2,1)S(1)} %get-tuple-element.70.refs_1_.refs_3_), channel_id=1, source_target_pairs={{0,1},{1,0},{2,3},{3,2},{4,5},{5,4},{6,7},{7,6},{8,9},{9,8},{10,11... | collective-permute-start | bytes 1572872 | tf_op jit(solution)/shard_map/ppermute | solution.py:456
  21.6 0.0 collective-permute-done.3
  21.6 0.1 broadcast_in_dim.51.refs_11_
  21.7 1.3 %copy-done.1 = bf16[512,1280]{1,0:T(8,128)(2,1)S(1)} copy-done((bf16[512,1280]{1,0:T(8,128)(2,1)S(1)}, bf16[512,1280]{1,0:T(8,128)(2,1)}, u32[]{:S(2)}) %copy-start.1) | copy-done | bytes 1310744
  23.0 1.3 %copy-done.2 = bf16[512,1280]{1,0:T(8,128)(2,1)S(1)} copy-done((bf16[512,1280]{1,0:T(8,128)(2,1)S(1)}, bf16[512,1280]{1,0:T(8,128)(2,1)}, u32[]{:S(2)}) %copy-start.2) | copy-done | bytes 1310744
  24.3 13.7 %project.2 = (bf16[1024,512]{1,0:T(8,128)(2,1)S(1)}, bf16[1024,256]{1,0:T(8,128)(2,1)S(1)}, bf16[1024,512]{1,0:T(8,128)(2,1)S(1)}, f32[4,64,128]{2,1,0:T(8,128)S...) custom-call(s32[5]{0:T(128)S(1)} %get-tuple-element.130.refs_0_, ...), custom_call_target="tpu_custom_call" | custom-call | flops 2684354560 | bytes 10485760 | tf_op jit(solution)/shard_map/project/pallas_call | solution.py:600
  38.0 0.0 collective-permute-done.4.refs_2_.refs_4_
  38.0 13.7 %project.3 = (bf16[1024,512]{1,0:T(8,128)(2,1)S(1)}, bf16[1024,256]{1,0:T(8,128)(2,1)S(1)}, bf16[1024,512]{1,0:T(8,128)(2,1)S(1)}, f32[4,64,128]{2,1,0:T(8,128)S...) custom-call(s32[5]{0:T(128)S(1)} %get-tuple-element.129.refs_0_, ...), custom_call_target="tpu_custom_call" | custom-call | flops 2684354560 | bytes 10485760 | tf_op jit(solution)/shard_map/project/pallas_call | solution.py:600
  51.8 24.5 %exchange.1 = (bf16[1024,512]{1,0:T(8,128)(2,1)S(1)}, bf16[1024,512]{1,0:T(8,128)(2,1)S(1)}, bf16[1024,512]{1,0:T(8,128)(2,1)S(1)}, bf16[1024,512]{1,0:T(8,128)(...) custom-call(s32[5]{0:T(128)S(1)} %get-tuple-element.130.refs_0_, ...), custom_call_target="tpu_custom_call" | custom-call | flops 5368709120 | bytes 16777216 | tf_op jit(solution)/shard_map/exchange/pallas_call | solution.py:613
  76.3 0.0 copy-start.10
  76.4 0.6 copy-done.10
  77.0 4.3 %finish.2 = (bf16[1024,512]{1,0:T(8,128)(2,1)S(1)}, f32[8,1024]{1,0:T(8,128)S(1)}, bf16[1024,512]{1,0:T(8,128)(2,1)S(1)}, f32[8,1024]{1,0:T(8,128)S(1)}) custom-call(bf16[1024,512]{1,0:T(8,128)(2,1)S(1)} %get-tuple-element.81.refs_0_, bf16[1024,512]{1,0:T(8,128)(2,1)S(1)} %get-tuple-element.82.refs_1_, ...), custom_call_target="tpu_custom_call" | custom-call | flops 268435456 | bytes 12582912 | tf_op jit(solution)/shard_map/finish/pallas_call | solution.py:688
  81.3 0.1 broadcast_select_fusion.1
  81.4 0.5 collective-permute-start.5
  81.9 4.3 %finish.3 = (bf16[1024,512]{1,0:T(8,128)(2,1)S(1)}, f32[8,1024]{1,0:T(8,128)S(1)}, bf16[1024,512]{1,0:T(8,128)(2,1)S(1)}, f32[8,1024]{1,0:T(8,128)S(1)}) custom-call(bf16[1024,512]{1,0:T(8,128)(2,1)S(1)} %get-tuple-element.98.refs_0_, bf16[1024,512]{1,0:T(8,128)(2,1)S(1)} %get-tuple-element.99.refs_1_, ...), custom_call_target="tpu_custom_call" | custom-call | flops 268435456 | bytes 12582912 | tf_op jit(solution)/shard_map/finish/pallas_call | solution.py:688
  86.2 0.1 broadcast_select_fusion
  86.2 1.5 %collective-permute-start.6 = (f32[8,1024]{1,0:T(8,128)S(1)}, f32[8,1024]{1,0:T(8,128)S(1)}, u32[]{:S(2)}, u32[]{:S(2)}) collective-permute-start(f32[8,1024]{1,0:T(8,128)S(1)} %broadcast_select_fusion), channel_id=1, source_target_pairs={{0,1},{1,0},{2,3},{3,2},{4,5},{5,4},{6,7},{7,6},{8,9},{9,8},{10,11... | collective-permute-start | bytes 98312 | tf_op jit(solution)/shard_map/ppermute | solution.py:456
  87.8 0.0 collective-permute-done.5
  87.8 2.0 %output.2 = (f32[1024,256]{1,0:T(8,128)S(1)}, bf16[1024,256]{1,0:T(8,128)(2,1)S(1)}) custom-call(f32[8,1024]{1,0:T(8,128)S(1)} %add.82.ss_ref, bf16[1024,512]{1,0:T(8,128)(2,1)S(1)} %get-tuple-element.94.gf_ref, bf16[1024,512]{1,0:T(8,128)(2,1)S(1)} %get-tuple-element.95.gr_ref, bf16[512,512]{1,0:T(8,128)(2,1)S(1)} %fusion.1.wf_ref, ...), custom_call_target="tpu_custom_call" | custom-call | flops 1073741824 | bytes 4194304 | tf_op jit(solution)/shard_map/output/pallas_call | solution.py:700
  89.7 0.4 collective-permute-done.6
  90.2 1.5 %collective-permute-start.7 = (bf16[1024,256]{1,0:T(8,128)(2,1)S(1)}, bf16[1024,256]{1,0:T(8,128)(2,1)S(1)}, u32[]{:S(2)}, u32[]{:S(2)}) collective-permute-start(bf16[1024,256]{1,0:T(8,128)(2,1)S(1)} %get-tuple-element.107), channel_id=1, source_target_pairs={{0,1},{1,0},{2,3},{3,2},{4,5},{5,4},{6,7},{7,6},{8,9},{9,8},{10,11... | collective-permute-start | bytes 1572872 | tf_op jit(solution)/shard_map/ppermute | solution.py:456
  91.7 1.9 %output.3 = (f32[1024,256]{1,0:T(8,128)S(1)}, bf16[1024,256]{1,0:T(8,128)(2,1)S(1)}) custom-call(f32[8,1024]{1,0:T(8,128)S(1)} %add.85.ss_ref, bf16[1024,512]{1,0:T(8,128)(2,1)S(1)} %get-tuple-element.109.gf_ref, bf16[1024,512]{1,0:T(8,128)(2,1)S(1)} %get-tuple-element.110.gr_ref, bf16[512,512]{1,0:T(8,128)(2,1)S(1)} %fusion.1.wf_ref, ...), custom_call_target="tpu_custom_call" | custom-call | flops 1073741824 | bytes 4194304 | tf_op jit(solution)/shard_map/output/pallas_call | solution.py:703
  93.6 0.6 collective-permute-start.8
  94.2 10.8 %collective-permute-done.7 = bf16[1024,256]{1,0:T(8,128)(2,1)S(1)} collective-permute-done((bf16[1024,256]{1,0:T(8,128)(2,1)S(1)}, bf16[1024,256]{1,0:T(8,128)(2,1)S(1)}, u32[]{:S(2)}, u32[]{:S(2)}) %collective-permute-start.7) | collective-permute-done | bytes 524320 | tf_op jit(solution)/shard_map/ppermute | solution.py:456
  105.0 0.1 add_convert_fusion.1
  105.2 9.5 %collective-permute-done.8 = bf16[1024,256]{1,0:T(8,128)(2,1)S(1)} collective-permute-done((bf16[1024,256]{1,0:T(8,128)(2,1)S(1)}, bf16[1024,256]{1,0:T(8,128)(2,1)S(1)}, u32[]{:S(2)}, u32[]{:S(2)}) %collective-permute-start.8) | collective-permute-done | bytes 524320 | tf_op jit(solution)/shard_map/ppermute | solution.py:456
  114.7 0.1 add_convert_fusion
  114.8 1.0 pad_maximum_fusion
  (36 shorter events, 0.3 us)
Async XLA Ops:
  0.0 14.8 %copy-start = (bf16[512,512]{1,0:T(8,128)(2,1)S(1)}, bf16[512,512]{1,0:T(8,128)(2,1)}, u32[]{:S(2)}) copy-start(bf16[512,512]{1,0:T(8,128)(2,1)} %param.24) | copy-start | bytes 1572868
  0.8 15.6 %collective-permute-start.1 = (bf16[16,256]{1,0:T(8,128)(2,1)S(1)}, bf16[16,256]{1,0:T(8,128)(2,1)S(1)}, u32[]{:S(2)}, u32[]{:S(2)}) collective-permute-start(bf16[16,256]{1,0:T(8,128)(2,1)S(1)} %get-tuple-element.115), channel_id=1, source_target_pairs={{0,2},{2,4},{4,6},{6,8},{8,10},{10,12},{12,14},{14,16},{16,18},{18... | collective-permute-start | bytes 24584 | tf_op jit(solution)/shard_map/ppermute | solution.py:456
  3.2 7.0 %copy-start.3 = (bf16[512,512]{1,0:T(8,128)(2,1)S(1)}, bf16[512,512]{1,0:T(8,128)(2,1)}, u32[]{:S(2)}) copy-start(bf16[512,512]{1,0:T(8,128)(2,1)} %param.14) | copy-start | bytes 1572868
  3.2 13.2 %collective-permute-start.2 = (bf16[16,256]{1,0:T(8,128)(2,1)S(1)}, bf16[16,256]{1,0:T(8,128)(2,1)S(1)}, u32[]{:S(2)}, u32[]{:S(2)}) collective-permute-start(bf16[16,256]{1,0:T(8,128)(2,1)S(1)} %get-tuple-element.116), channel_id=1, source_target_pairs={{2,0},{4,2},{6,4},{8,6},{10,8},{12,10},{14,12},{16,14},{18,16},{20... | collective-permute-start | bytes 24584 | tf_op jit(solution)/shard_map/ppermute | solution.py:456
  5.9 4.3 %copy-start.5 = (bf16[512,256]{1,0:T(8,128)(2,1)S(1)}, bf16[512,256]{1,0:T(8,128)(2,1)}, u32[]{:S(2)}) copy-start(bf16[512,256]{1,0:T(8,128)(2,1)} %param.16) | copy-start | bytes 786436
  5.9 4.4 %copy-start.4 = (bf16[512,512]{1,0:T(8,128)(2,1)S(1)}, bf16[512,512]{1,0:T(8,128)(2,1)}, u32[]{:S(2)}) copy-start(bf16[512,512]{1,0:T(8,128)(2,1)} %param.15) | copy-start | bytes 1572868
  5.9 13.2 %collective-permute-start = (bf16[1024,256]{1,0:T(8,128)(2,1)S(1)}, bf16[1024,256]{1,0:T(8,128)(2,1)S(1)}, u32[]{:S(2)}, u32[]{:S(2)}) collective-permute-start(bf16[1024,256]{1,0:T(8,128)(2,1)S(1)} %get-tuple-element.118.refs_1_.refs_3_), channel_id=1, source_target_pairs={{0,1},{1,0},{2,3},{3,2},{4,5},{5,4},{6,7},{7,6},{8,9},{9,8},{10,11... | collective-permute-start | bytes 1572872 | tf_op jit(solution)/shard_map/ppermute | solution.py:456
  12.3 2.0 %copy-start.6 = (pred[512,512]{1,0:T(32,128)(4,1)S(1)}, pred[512,512]{1,0:T(32,128)(4,1)}, u32[]{:S(2)}) copy-start(pred[512,512]{1,0:T(32,128)(4,1)} %iota_compare_fusion.2) | copy-start | bytes 786436
  12.3 2.0 %copy-start.7 = (pred[512,512]{1,0:T(32,128)(4,1)S(1)}, pred[512,512]{1,0:T(32,128)(4,1)}, u32[]{:S(2)}) copy-start(pred[512,512]{1,0:T(32,128)(4,1)} %iota_compare_fusion.3) | copy-start | bytes 786436
  12.3 2.0 %copy-start.12 = (bf16[512,8]{0,1:T(8,128)(2,1)S(1)}, bf16[512,8]{0,1:T(8,128)(2,1)}, u32[]{:S(2)}) copy-start(bf16[512,8]{0,1:T(8,128)(2,1)} %param.17) | copy-start | bytes 24580
  14.8 1.1 copy-start.13
  14.8 1.3 %copy-start.8 = (f32[4,512]{1,0:T(4,128)S(1)}, f32[4,512]{1,0:T(4,128)}, u32[]{:S(2)}) copy-start(f32[4,512]{1,0:T(4,128)} %param.18) | copy-start | bytes 24580
  14.8 1.3 %copy-start.9 = (f32[4,256]{1,0:T(4,128)S(1)}, f32[4,256]{1,0:T(4,128)}, u32[]{:S(2)}) copy-start(f32[4,256]{1,0:T(4,128)} %param.19) | copy-start | bytes 12292
  14.8 1.3 %copy-start.14 = (f32[8]{0:T(128)S(1)}, f32[8]{0:T(128)}, u32[]{:S(2)}) copy-start(f32[8]{0:T(128)} %param.21) | copy-start | bytes 100
  14.8 1.3 %copy-start.15 = (f32[8]{0:T(128)S(1)}, f32[8]{0:T(128)}, u32[]{:S(2)}) copy-start(f32[8]{0:T(128)} %param.20) | copy-start | bytes 100
  14.8 1.4 %copy-start.11 = (f32[8]{0:T(128)S(1)}, f32[8]{0:T(128)}, u32[]{:S(2)}) copy-start(f32[8]{0:T(128)} %param.22) | copy-start | bytes 100
  16.4 5.2 %collective-permute-start.3 = (bf16[64,256]{1,0:T(8,128)(2,1)S(1)}, bf16[64,256]{1,0:T(8,128)(2,1)S(1)}, u32[]{:S(2)}, u32[]{:S(2)}) collective-permute-start(bf16[64,256]{1,0:T(8,128)(2,1)S(1)} %pad_maximum_fusion.1), channel_id=1, source_target_pairs={{0,1},{1,0},{2,3},{3,2},{4,5},{5,4},{6,7},{7,6},{8,9},{9,8},{10,11... | collective-permute-start | bytes 98312 | tf_op jit(solution)/shard_map/ppermute | solution.py:456
  19.1 18.9 %collective-permute-start.4 = (bf16[1024,256]{1,0:T(8,128)(2,1)S(1)}, bf16[1024,256]{1,0:T(8,128)(2,1)S(1)}, u32[]{:S(2)}, u32[]{:S(2)}) collective-permute-start(bf16[1024,256]{1,0:T(8,128)(2,1)S(1)} %get-tuple-element.70.refs_1_.refs_3_), channel_id=1, source_target_pairs={{0,1},{1,0},{2,3},{3,2},{4,5},{5,4},{6,7},{7,6},{8,9},{9,8},{10,11... | collective-permute-start | bytes 1572872 | tf_op jit(solution)/shard_map/ppermute | solution.py:456
  21.7 1.3 %copy-start.1 = (bf16[512,1280]{1,0:T(8,128)(2,1)S(1)}, bf16[512,1280]{1,0:T(8,128)(2,1)}, u32[]{:S(2)}) copy-start(bf16[512,1280]{1,0:T(8,128)(2,1)} %convolution_convert_fusion.refs_8_) | copy-start | bytes 3932164
  23.0 1.3 %copy-start.2 = (bf16[512,1280]{1,0:T(8,128)(2,1)S(1)}, bf16[512,1280]{1,0:T(8,128)(2,1)}, u32[]{:S(2)}) copy-start(bf16[512,1280]{1,0:T(8,128)(2,1)} %convolution_convert_fusion.1.refs_7_) | copy-start | bytes 3932164
  76.3 0.7 copy-start.10
  81.4 6.4 %collective-permute-start.5 = (f32[8,1024]{1,0:T(8,128)S(1)}, f32[8,1024]{1,0:T(8,128)S(1)}, u32[]{:S(2)}, u32[]{:S(2)}) collective-permute-start(f32[8,1024]{1,0:T(8,128)S(1)} %broadcast_select_fusion.1), channel_id=1, source_target_pairs={{0,1},{1,0},{2,3},{3,2},{4,5},{5,4},{6,7},{7,6},{8,9},{9,8},{10,11... | collective-permute-start | bytes 98312 | tf_op jit(solution)/shard_map/ppermute | solution.py:456
  86.2 3.9 %collective-permute-start.6 = (f32[8,1024]{1,0:T(8,128)S(1)}, f32[8,1024]{1,0:T(8,128)S(1)}, u32[]{:S(2)}, u32[]{:S(2)}) collective-permute-start(f32[8,1024]{1,0:T(8,128)S(1)} %broadcast_select_fusion), channel_id=1, source_target_pairs={{0,1},{1,0},{2,3},{3,2},{4,5},{5,4},{6,7},{7,6},{8,9},{9,8},{10,11... | collective-permute-start | bytes 98312 | tf_op jit(solution)/shard_map/ppermute | solution.py:456
  90.2 14.9 %collective-permute-start.7 = (bf16[1024,256]{1,0:T(8,128)(2,1)S(1)}, bf16[1024,256]{1,0:T(8,128)(2,1)S(1)}, u32[]{:S(2)}, u32[]{:S(2)}) collective-permute-start(bf16[1024,256]{1,0:T(8,128)(2,1)S(1)} %get-tuple-element.107), channel_id=1, source_target_pairs={{0,1},{1,0},{2,3},{3,2},{4,5},{5,4},{6,7},{7,6},{8,9},{9,8},{10,11... | collective-permute-start | bytes 1572872 | tf_op jit(solution)/shard_map/ppermute | solution.py:456
  93.6 21.1 %collective-permute-start.8 = (bf16[1024,256]{1,0:T(8,128)(2,1)S(1)}, bf16[1024,256]{1,0:T(8,128)(2,1)S(1)}, u32[]{:S(2)}, u32[]{:S(2)}) collective-permute-start(bf16[1024,256]{1,0:T(8,128)(2,1)S(1)} %get-tuple-element.112), channel_id=1, source_target_pairs={{0,1},{1,0},{2,3},{3,2},{4,5},{5,4},{6,7},{7,6},{8,9},{9,8},{10,11... | collective-permute-start | bytes 1572872 | tf_op jit(solution)/shard_map/ppermute | solution.py:456
